TPU v7x, 32 devices: a whole 2x2x4 slice. The times are simulated.
32 devices in a mesh: dp: 8 (over z, y), mp: 4 (over x, core).
Axes of the slice: x: 2, y: 2, z: 4, core: 2. Of those that a mesh axis runs over, the one named last changes fastest.
Arguments:
- stream: float32 [16384, 512], P('dp', 'mp'), may hold values from -6 to 6
- cotangent: float32 [16384, 512], P('dp', 'mp'), may hold values from -6 to 6
- start_offsets: int32 [8], P('dp'), may hold values from 0 to 2047, as said below
- norm_gain: float32 [2, 512], P(None, 'mp'), may hold values from 0.5 to 1.5
- norm_shift: float32 [2, 512], P(None, 'mp'), may hold values from -3 to 3
- input_map: bfloat16 [2, 512, 512], replicated, may hold values from -0.25 to 0.25
- decay_log: float32 [2, 256], replicated, may hold values from -9 to -2.5
- phase_log: float32 [2, 256], replicated, may hold values from -3 to 0.5
- scale_log: float32 [2, 256], replicated, may hold values from -4.7 to -0.4
- output_map: bfloat16 [2, 512, 512], P(None, None, 'mp'), may hold values from -0.25 to 0.25
- skip_gain: float32 [2, 512], P(None, 'mp'), may hold values from -4 to 4
- value_weight: bfloat16 [2, 512, 512], P(None, None, 'mp'), may hold values from -0.25 to 0.25
- gate_weight: bfloat16 [2, 512, 512], P(None, None, 'mp'), may hold values from -0.25 to 0.25
- value_bias: float32 [2, 512], P(None, 'mp'), may hold values from -3 to 3
- gate_bias: float32 [2, 512], P(None, 'mp'), may hold values from -3 to 3
Outputs:
- result: float32 [16384, 512], P('dp', 'mp')
- stream_grad: float32 [16384, 512], P('dp', 'mp')
- gain_grad: float32 [2, 512], P(None, 'mp')
- shift_grad: float32 [2, 512], P(None, 'mp')
- input_map_grad: float32 [2, 512, 512], replicated
- decay_grad: float32 [2, 256], replicated
- phase_grad: float32 [2, 256], replicated
- scale_grad: float32 [2, 256], replicated
- output_map_grad: float32 [2, 512, 512], P(None, None, 'mp')
- skip_grad: float32 [2, 512], P(None, 'mp')
- value_weight_grad: float32 [2, 512, 512], P(None, None, 'mp')
- gate_weight_grad: float32 [2, 512, 512], P(None, None, 'mp')
- value_bias_grad: float32 [2, 512], P(None, 'mp')
- gate_bias_grad: float32 [2, 512], P(None, 'mp')
Inputs may be any that keep to these rules, and one draw needn't show every extreme that they name: `start_offsets`: only the first and the last token block have a nonzero entry, each of 1 to 2047, and one of the two is 2047; so one sequence runs from the first token block to the last.
All inputs are finite; a program needn't handle non-finite values.
Results may differ from a plain program's by a relative error of at most 0.019.
Values may be sent and summed in bfloat16 or wider, within the bound.
No kernel may reach another device: no remote copies, remote signals or barrier semaphores. Data moves between devices by JAX's collectives and lax.ppermute only.
A program may use at most 192 MiB of HBM per device.

v0:
```python
import jax
import jax.numpy as jnp
from jax import lax
from jax.sharding import PartitionSpec as P

epsilon = 1e-05


def carried_in(part, axis, combine, identity, reverse):
    count = lax.axis_size(axis)
    place = lax.axis_index(axis)
    ahead = count - 1 - place if reverse else place
    gathered = jax.tree.map(lambda a: lax.all_gather(a, axis), part)
    state = jax.tree.map(lambda a, e: jnp.zeros_like(a) + jnp.asarray(e, a.dtype), part, identity)

    def one(hop, state):
        source = count - 1 - hop if reverse else hop
        return combine(
            state, jax.tree.map(lambda a: lax.dynamic_index_in_dim(a, source, 0, False), gathered)
        )

    return lax.fori_loop(0, ahead, one, state)


def complex_product_fn(left_re, left_im, right_re, right_im):
    return (left_re * right_re - left_im * right_im, left_re * right_im + left_im * right_re)


def linear_combine_operator(earlier_element, later_element):
    (
        earlier_multiplier_real,
        earlier_multiplier_imaginary,
        earlier_value_real,
        earlier_value_imaginary,
    ) = earlier_element
    later_multiplier_real, later_multiplier_imaginary, later_value_real, later_value_imaginary = (
        later_element
    )
    combined_real, combined_imaginary = complex_product_fn(
        later_multiplier_real,
        later_multiplier_imaginary,
        earlier_multiplier_real,
        earlier_multiplier_imaginary,
    )
    propagated_real, propagated_imaginary = complex_product_fn(
        later_multiplier_real,
        later_multiplier_imaginary,
        earlier_value_real,
        earlier_value_imaginary,
    )
    return (
        combined_real,
        combined_imaginary,
        propagated_real + later_value_real,
        propagated_imaginary + later_value_imaginary,
    )


def chain(drive_re, drive_im, log_radius, angle_val, row_gates, reverse_time_scan, adjoint):
    rate_re = jnp.exp(log_radius) * jnp.cos(angle_val)
    rate_im = jnp.exp(log_radius) * jnp.sin(angle_val)
    mult_re = row_gates[:, None] * rate_re
    mult_im = row_gates[:, None] * rate_im
    prefix = lax.associative_scan(
        linear_combine_operator, (mult_re, mult_im, drive_re, drive_im), axis=0
    )
    linked = (prefix[0][-1], prefix[1][-1], prefix[2][-1], prefix[3][-1])
    neutral_element = (
        jnp.ones_like(log_radius),
        jnp.zeros_like(log_radius),
        jnp.zeros_like(log_radius),
        jnp.zeros_like(log_radius),
    )
    if adjoint:
        incoming = carried_in(
            linked, "dp", linear_combine_operator, neutral_element, reverse_time_scan
        )
    else:
        incoming = carried_in(
            linked, "dp", linear_combine_operator, neutral_element, reverse_time_scan
        )
    added_re, added_im = complex_product_fn(prefix[0], prefix[1], incoming[2], incoming[3])
    return (prefix[2] + added_re, prefix[3] + added_im, incoming[2], incoming[3])


def on_device(
    stream,
    cotangent,
    start_offsets,
    norm_gain,
    norm_shift,
    input_map,
    decay_log,
    phase_log,
    scale_log,
    output_map,
    skip_gain,
    value_weight,
    gate_weight,
    value_bias,
    gate_bias,
):
    rows_total, width_own = stream.shape
    layers_total = input_map.shape[0]
    states_total = input_map.shape[2] // 2
    count_all = rows_total * lax.axis_size("dp")
    offset_here = start_offsets[0]
    row_ids = jnp.arange(rows_total, dtype=jnp.int32)
    begin_rows = ((row_ids == offset_here) & (offset_here > 0)).astype(jnp.float32)
    finish_rows = jnp.concatenate([begin_rows[1:], jnp.zeros((1,), jnp.float32)])
    ahead_gates = 1.0 - begin_rows
    behind_gates = jnp.flip(1.0 - finish_rows, 0)
    contract_rows = (((0,), (0,)), ((), ()))
    contract_cols = (((1,), (1,)), ((), ()))
    saved = []
    hidden = stream
    for layer_index in range(layers_total):
        backward_time = layer_index % 2 == 1
        moments = lax.psum((jnp.sum(hidden, axis=0), jnp.sum(hidden * hidden, axis=0)), "dp")
        mean_val = moments[0] / count_all
        spread = moments[1] / count_all - mean_val * mean_val
        inverse = lax.rsqrt(spread + epsilon)
        normed = (hidden - mean_val) * inverse
        scaled = normed * norm_gain[layer_index] + norm_shift[layer_index]
        scaled_low = scaled.astype(jnp.bfloat16)
        normed_all = lax.all_gather(scaled_low, "mp", axis=1, tiled=True)
        driven = jnp.dot(normed_all, input_map[layer_index], preferred_element_type=jnp.float32)
        log_radius = -jnp.exp(decay_log[layer_index])
        angle_val = jnp.exp(phase_log[layer_index])
        factor = jnp.exp(scale_log[layer_index])
        drive_re = factor * driven[:, :states_total]
        drive_im = factor * driven[:, states_total:]
        if backward_time:
            drive_re = jnp.flip(drive_re, 0)
            drive_im = jnp.flip(drive_im, 0)
            forward_rows = behind_gates
        else:
            forward_rows = ahead_gates
        state_re, state_im, enter_re, enter_im = chain(
            drive_re, drive_im, log_radius, angle_val, forward_rows, backward_time, False
        )
        if backward_time:
            natural_re = jnp.flip(state_re, 0)
            natural_im = jnp.flip(state_im, 0)
        else:
            natural_re = state_re
            natural_im = state_im
        states_low = jnp.concatenate([natural_re, natural_im], axis=1).astype(jnp.bfloat16)
        mixed_val = (
            jnp.dot(states_low, output_map[layer_index], preferred_element_type=jnp.float32)
            + skip_gain[layer_index] * scaled
        )
        sent_low = jax.nn.gelu(mixed_val).astype(jnp.bfloat16)
        glu_all = lax.all_gather(sent_low, "mp", axis=1, tiled=True)
        value_part = (
            jnp.dot(glu_all, value_weight[layer_index], preferred_element_type=jnp.float32)
            + value_bias[layer_index]
        )
        gate_part = (
            jnp.dot(glu_all, gate_weight[layer_index], preferred_element_type=jnp.float32)
            + gate_bias[layer_index]
        )
        kept_pair = (None, None)
        saved.append(
            (
                normed,
                inverse,
                scaled,
                scaled_low,
                driven,
                state_re,
                state_im,
                enter_re,
                enter_im,
                states_low,
                mixed_val,
                sent_low,
                value_part,
                gate_part,
                kept_pair,
            )
        )
        hidden = hidden + value_part * jax.nn.sigmoid(gate_part)
    upstream = cotangent
    full_parts = []
    data_parts = []
    for layer_index in reversed(range(layers_total)):
        backward_time = layer_index % 2 == 1
        (
            normed,
            inverse,
            scaled,
            scaled_low,
            driven,
            state_re,
            state_im,
            enter_re,
            enter_im,
            states_low,
            mixed_val,
            sent_low,
            value_part,
            gate_part,
            kept_pair,
        ) = saved[layer_index]
        sig_gate = jax.nn.sigmoid(gate_part)
        grad_value = upstream * sig_gate
        grad_gate = upstream * value_part * sig_gate * (1.0 - sig_gate)
        value_b_grad = jnp.sum(grad_value, axis=0)
        gate_b_grad = jnp.sum(grad_gate, axis=0)
        stacked_low = jnp.concatenate([grad_value, grad_gate], axis=1).astype(jnp.bfloat16)
        glu_weights = lax.dot_general(
            lax.all_gather(sent_low, "mp", axis=1, tiled=True),
            stacked_low,
            contract_rows,
            preferred_element_type=jnp.float32,
        )
        value_w_grad = glu_weights[:, :width_own]
        gate_w_grad = glu_weights[:, width_own:]
        both_maps = jnp.concatenate([value_weight[layer_index], gate_weight[layer_index]], axis=1)
        activated_grad = (
            lax.psum_scatter(
                lax.dot_general(
                    both_maps, stacked_low, contract_cols, preferred_element_type=jnp.float32
                ).astype(jnp.bfloat16),
                "mp",
                scatter_dimension=0,
                tiled=True,
            )
            .astype(jnp.float32)
            .T
        )
        mixed_grad = jax.vjp(jax.nn.gelu, mixed_val)[1](activated_grad)[0]
        skip_w_grad = jnp.sum(mixed_grad * scaled, axis=0)
        mixed_low = mixed_grad.astype(jnp.bfloat16)
        output_w_grad = lax.dot_general(
            states_low, mixed_low, contract_rows, preferred_element_type=jnp.float32
        )
        state_grad = lax.dot_general(
            mixed_low, output_map[layer_index], contract_cols, preferred_element_type=jnp.float32
        )
        grad_re = state_grad[:, :states_total]
        grad_im = state_grad[:, states_total:]
        log_radius = -jnp.exp(decay_log[layer_index])
        angle_val = jnp.exp(phase_log[layer_index])
        factor = jnp.exp(scale_log[layer_index])
        if backward_time:
            other_re, other_im = (grad_re, grad_im)
            adjoint_rows = ahead_gates
            forward_rows = behind_gates
        else:
            other_re, other_im = (jnp.flip(grad_re, 0), jnp.flip(grad_im, 0))
            adjoint_rows = behind_gates
            forward_rows = ahead_gates
        adj_q_re, adj_q_im, _, _ = chain(
            other_re, other_im, log_radius, -angle_val, adjoint_rows, not backward_time, True
        )
        adj_p_re = jnp.flip(adj_q_re, 0)
        adj_p_im = jnp.flip(adj_q_im, 0)
        prev_re = forward_rows[:, None] * jnp.concatenate(
            [enter_re[None, :], state_re[:-1]], axis=0
        )
        prev_im = forward_rows[:, None] * jnp.concatenate(
            [enter_im[None, :], state_im[:-1]], axis=0
        )
        rate_grad_re = jnp.sum(adj_p_re * prev_re + adj_p_im * prev_im, axis=0)
        rate_grad_im = jnp.sum(adj_p_im * prev_re - adj_p_re * prev_im, axis=0)
        rate_re = jnp.exp(log_radius) * jnp.cos(angle_val)
        rate_im = jnp.exp(log_radius) * jnp.sin(angle_val)
        decay_w_grad = -jnp.exp(decay_log[layer_index]) * (
            rate_grad_re * rate_re + rate_grad_im * rate_im
        )
        phase_w_grad = angle_val * (rate_grad_im * rate_re - rate_grad_re * rate_im)
        if backward_time:
            adj_nat_re, adj_nat_im = (adj_q_re, adj_q_im)
        else:
            adj_nat_re, adj_nat_im = (adj_p_re, adj_p_im)
        scale_w_grad = factor * jnp.sum(
            adj_nat_re * driven[:, :states_total] + adj_nat_im * driven[:, states_total:], axis=0
        )
        driven_low = jnp.concatenate([factor * adj_nat_re, factor * adj_nat_im], axis=1).astype(
            jnp.bfloat16
        )
        input_w_grad = lax.dot_general(
            lax.all_gather(scaled_low, "mp", axis=1, tiled=True),
            driven_low,
            contract_rows,
            preferred_element_type=jnp.float32,
        )
        map_here = input_map[layer_index]
        scaled_grad = (
            lax.psum_scatter(
                lax.dot_general(
                    map_here, driven_low, contract_cols, preferred_element_type=jnp.float32
                ).astype(jnp.bfloat16),
                "mp",
                scatter_dimension=0,
                tiled=True,
            )
            .astype(jnp.float32)
            .T
            + mixed_grad * skip_gain[layer_index]
        )
        shift_w_grad = jnp.sum(scaled_grad, axis=0)
        gain_w_grad = jnp.sum(scaled_grad * normed, axis=0)
        normed_grad = scaled_grad * norm_gain[layer_index]
        back_sums = lax.psum(
            (jnp.sum(normed_grad, axis=0), jnp.sum(normed_grad * normed, axis=0)), "dp"
        )
        upstream = upstream + inverse * (
            normed_grad - back_sums[0] / count_all - normed * (back_sums[1] / count_all)
        )
        full_terms = (input_w_grad, decay_w_grad, phase_w_grad, scale_w_grad)
        data_terms = (
            output_w_grad,
            skip_w_grad,
            value_w_grad,
            gate_w_grad,
            value_b_grad,
            gate_b_grad,
            gain_w_grad,
            shift_w_grad,
        )
        full_parts.insert(0, full_terms)
        data_parts.insert(0, data_terms)
    full_stack = [
        jnp.stack([layer_terms[position] for layer_terms in full_parts]) for position in range(4)
    ]
    data_stack = [
        jnp.stack([layer_terms[position] for layer_terms in data_parts]) for position in range(8)
    ]
    full_stack = lax.psum(
        (full_stack[0], full_stack[1], full_stack[2], full_stack[3]), ("dp", "mp")
    )
    data_stack = lax.psum(
        (
            data_stack[0],
            data_stack[1],
            data_stack[2],
            data_stack[3],
            data_stack[4],
            data_stack[5],
            data_stack[6],
            data_stack[7],
        ),
        "dp",
    )
    return (
        hidden,
        upstream,
        data_stack[6],
        data_stack[7],
        full_stack[0],
        full_stack[1],
        full_stack[2],
        full_stack[3],
        data_stack[0],
        data_stack[1],
        data_stack[2],
        data_stack[3],
        data_stack[4],
        data_stack[5],
    )


def solution(mesh):
    placed = (
        P("dp", "mp"),
        P("dp", "mp"),
        P("dp"),
        P(None, "mp"),
        P(None, "mp"),
        P(),
        P(),
        P(),
        P(),
        P(None, None, "mp"),
        P(None, "mp"),
        P(None, None, "mp"),
        P(None, None, "mp"),
        P(None, "mp"),
        P(None, "mp"),
    )
    return jax.shard_map(
        on_device,
        mesh=mesh,
        in_specs=placed,
        out_specs=(
            P("dp", "mp"),
            P("dp", "mp"),
            P(None, "mp"),
            P(None, "mp"),
            P(),
            P(),
            P(),
            P(),
            P(None, None, "mp"),
            P(None, "mp"),
            P(None, None, "mp"),
            P(None, None, "mp"),
            P(None, "mp"),
            P(None, "mp"),
        ),
        check_vma=False,
    )
```

profile of v0, /device:TPU:0, one launch (start us, length us, event | category | flops | bytes accessed | tf_op | source)
XLA Modules:
  0.0 2307.6 jit_solution(11046097774312977944)
XLA Ops:
  8.8 23.1 %all-reduce.356 = (f32[128]{0:T(128)S(1)}, f32[128]{0:T(128)S(1)}) all-reduce(f32[128]{0:T(128)S(1)} %get-tuple-element.446, f32[128]{0:T(128)S(1)} %get-tuple-element.445), channel_id=1, replica_groups=mesh['dp'=8,'mp'=4] {'dp'}, use_global_device_ids=true, to_apply=%region_3.4 | all-reduce | flops 256 | bytes 2048 | tf_op jit(solution)/shard_map/psum | solution.py:119
  266.1 18.3 all-gather.1
  360.3 18.3 all-gather.3
  390.4 23.9 %all-gather.23.cloned.1.call-done = bf16[2048,512]{1,0:T(8,128)(2,1)} async-done(((bf16[2048,128]{1,0:T(8,128)(2,1)}), bf16[2048,512]{1,0:T(8,128)(2,1)}) %all-gather.23.cloned.1.call-update) | async-done | bytes 2097168 | tf_op jit(solution)/shard_map/all_gather | solution.py:154
  418.5 21.4 all-reduce.355
  806.8 18.3 all-gather.5
  896.8 16.3 all-gather.6
  928.9 18.3 all-gather.7
  971.5 16.4 rev.29
  992.9 17.9 all-gather.27.cloned.1.call-done
  1216.1 20.8 all-gather.8
  1339.1 18.3 all-gather.10
  1373.3 16.3 all-gather.11
  1407.9 34.7 %reduce-scatter.15.cloned.1.call-done = bf16[128,2048]{1,0:T(8,128)(2,1)} async-done(((bf16[512,2048]{1,0:T(8,128)(2,1)}), bf16[128,2048]{1,0:T(8,128)(2,1)}) %reduce-scatter.15.cloned.1.call-update) | async-done | bytes 524304
  1449.0 21.3 all-reduce.354
  1478.1 16.7 rev.33
  1863.4 18.3 all-gather.13
  1958.2 18.3 all-gather.15
  1990.2 16.8 rev.30
  2007.0 16.8 rev.31
  2048.7 37.2 %all-reduce.352 = (f32[2,256]{1,0:T(2,128)}, f32[2,256]{1,0:T(2,128)}, f32[2,256]{1,0:T(2,128)}) all-reduce(f32[2,256]{1,0:T(2,128)S(1)} %pad_maximum_fusion.187, f32[2,256]{1,0:T(2,128)S(1)} %pad_maximum_fusion.188, f32[2,256]{1,0:T(2,128)S(1)} %pad_maximum_fusion.189), channel_id=1, replica_groups=mesh['dp'=8,'mp'=4] {'dp','mp'}, use_global_device_ids=true, to_apply=%region_39.40 | all-reduce | flops 1536 | bytes 12288 | tf_op jit(solution)/shard_map/psum | solution.py:332
  2094.2 22.3 all-reduce.353
  2117.8 83.6 %all-reduce.361.cloned.1.call-done = f32[2,512,512]{2,1,0:T(8,128)} async-done(((f32[2,512,512]{2,1,0:T(8,128)}), f32[2,512,512]{2,1,0:T(8,128)}) %all-reduce.361.cloned.1.call-update) | async-done | bytes 2097168 | tf_op jit(solution)/shard_map/psum | solution.py:332
  2201.4 93.5 %all-reduce.363.cloned.1.call-done = (f32[2,512,128]{2,1,0:T(8,128)}, f32[2,512,128]{2,1,0:T(8,128)}, f32[2,512,128]{2,1,0:T(8,128)}) async-done(((f32[2,512,128]{2,1,0:T(8,128)}, f32[2,512,128]{2,1,0:T(8,128)}, f32[2,512,128]{2,1,0:T(8,128)}), (f32[2,512,128]{2,1,0:T(8,128)}, f32[2,512,128]{2,1,0:T(8,128)}, f32[2,512,128]{2,1,0:T(8,128)})) %all-reduce.363.cloned.1.call-update) | async-done | bytes 1572880 | tf_op jit(solution)/shard_map/psum | solution.py:335
  (2548 shorter events, 1667.7 us)
Async XLA Ops:
  7.2 64.9 %all-gather.21.cloned.1.call-start = ((), (), s32[]{:S(2)}) async-start(), calls=%async_computation.4 | async-start | bytes 2621440 | tf_op jit(solution)/shard_map/all_gather | solution.py:126
  36.0 378.3 %all-gather.23.cloned.1.call-start = ((), (), s32[]{:S(2)}) async-start(), calls=%async_computation.5 | async-start | bytes 2621440 | tf_op jit(solution)/shard_map/all_gather | solution.py:154
  47.3 176.3 %copy-start.29 = (f32[1023,256]{1,0:T(8,128)}, f32[1023,256]{1,0:T(8,128)S(1)}, u32[]{:S(2)}) copy-start(f32[1023,256]{1,0:T(8,128)S(1)} %slice.2966) | copy-start | bytes 3142660
  389.2 85.3 %all-gather.25.cloned.1.call-start = ((), (), s32[]{:S(2)}) async-start(), calls=%async_computation.6 | async-start | bytes 2621440 | tf_op jit(solution)/shard_map/all_gather | solution.py:126
  441.4 569.4 %all-gather.27.cloned.1.call-start = ((), (), s32[]{:S(2)}) async-start(), calls=%async_computation.7 | async-start | bytes 2621440 | tf_op jit(solution)/shard_map/all_gather | solution.py:154
  605.2 123.4 %copy-start.139 = (f32[127,256]{1,0:T(8,128)}, f32[127,256]{1,0:T(8,128)S(1)}, u32[]{:S(2)}) copy-start(f32[127,256]{1,0:T(8,128)S(1)} %slice.3068) | copy-start | bytes 390148
  614.0 102.5 %copy-start.105 = (f32[1023,256]{1,0:T(8,128)S(1)}, f32[1023,256]{1,0:T(8,128)}, u32[]{:S(2)}) copy-start(f32[1023,256]{1,0:T(8,128)} %slice.3201) | copy-start | bytes 3142660
  620.4 101.4 %copy-start.107 = (f32[1023,256]{1,0:T(8,128)S(1)}, f32[1023,256]{1,0:T(8,128)}, u32[]{:S(2)}) copy-start(f32[1023,256]{1,0:T(8,128)} %slice.3249) | copy-start | bytes 3142660
  806.0 49.1 %copy-start.59 = (f32[2048,256]{1,0:T(8,128)}, f32[2048,256]{1,0:T(8,128)S(1)}, u32[]{:S(2)}) copy-start(f32[2048,256]{1,0:T(8,128)S(1)} %pad.1245) | copy-start | bytes 6291460
  991.5 59.1 %reduce-scatter.13.cloned.1.call-start = ((), (), s32[]{:S(2)}) async-start(), calls=%async_computation.9 | async-start | bytes 2621440
  1018.8 423.8 %reduce-scatter.15.cloned.1.call-start = ((), (), s32[]{:S(2)}) async-start(), calls=%async_computation.10 | async-start | bytes 2621440
  1252.7 44.6 %copy-start.50 = (f32[2048,256]{1,0:T(8,128)}, f32[2048,256]{1,0:T(8,128)S(1)}, u32[]{:S(2)}) copy-start(f32[2048,256]{1,0:T(8,128)S(1)} %pad.1333) | copy-start | bytes 6291460
  1407.8 36.8 %copy-start.336 = (f32[128]{0:T(128)S(1)}, f32[128]{0:T(128)}, u32[]{:S(2)}) copy-start(f32[128]{0:T(128)} %get-tuple-element.1070) | copy-start | bytes 1540
  1407.8 36.9 %copy-start.458 = (f32[128]{0:T(128)S(1)}, f32[128]{0:T(128)}, u32[]{:S(2)}) copy-start(f32[128]{0:T(128)} %get-tuple-element.1066) | copy-start | bytes 1540
  1407.8 132.7 %reduce-scatter.17.cloned.1.call-start = ((), (), s32[]{:S(2)}) async-start(), calls=%async_computation.11 | async-start | bytes 2621440
  1477.8 611.3 %reduce-scatter.19.cloned.1.call-start = ((), (), s32[]{:S(2)}) async-start(), calls=%async_computation.12 | async-start | bytes 2621440
  1516.9 304.2 %copy-start.23 = (f32[1023,256]{1,0:T(8,128)}, f32[1023,256]{1,0:T(8,128)S(1)}, u32[]{:S(2)}) copy-start(f32[1023,256]{1,0:T(8,128)S(1)} %slice.3473) | copy-start | bytes 3142660
  1678.5 102.5 %copy-start.106 = (f32[1023,256]{1,0:T(8,128)S(1)}, f32[1023,256]{1,0:T(8,128)}, u32[]{:S(2)}) copy-start(f32[1023,256]{1,0:T(8,128)} %slice.3641) | copy-start | bytes 3142660
  1684.9 101.5 %copy-start.108 = (f32[1023,256]{1,0:T(8,128)S(1)}, f32[1023,256]{1,0:T(8,128)}, u32[]{:S(2)}) copy-start(f32[1023,256]{1,0:T(8,128)} %slice.3689) | copy-start | bytes 3142660
  2033.9 167.6 %all-reduce.361.cloned.1.call-start = ((), (), s32[]{:S(2)}) async-start(), calls=%async_computation.8 | async-start | bytes 4194304 | tf_op jit(solution)/shard_map/psum | solution.py:332
  2046.2 39.7 %copy-start.153 = (bf16[2048,256]{1,0:T(8,128)(2,1)S(1)}, bf16[2048,256]{1,0:T(8,128)(2,1)}, u32[]{:S(2)}) copy-start(bf16[2048,256]{1,0:T(8,128)(2,1)} %copy-done.152) | copy-start | bytes 3145732
  2047.9 38.0 %copy-start.138 = (bf16[128,2048]{0,1:T(8,128)(2,1)S(1)}, bf16[128,2048]{0,1:T(8,128)(2,1)}, u32[]{:S(2)}) copy-start(bf16[128,2048]{0,1:T(8,128)(2,1)} %copy-done.137) | copy-start | bytes 1572868
  2047.9 38.0 %copy-start.151 = (bf16[2048,256]{1,0:T(8,128)(2,1)S(1)}, bf16[2048,256]{1,0:T(8,128)(2,1)}, u32[]{:S(2)}) copy-start(bf16[2048,256]{1,0:T(8,128)(2,1)} %copy-done.150) | copy-start | bytes 3145732
  2047.9 247.0 %all-reduce.363.cloned.1.call-start = ((), (), s32[]{:S(2)}) async-start(), calls=%async_computation.13 | async-start | bytes 3145728 | tf_op jit(solution)/shard_map/psum | solution.py:335
  (460 other events, 3714.9 us)
Sparse Core Ops, SparseCore 0:
  36.1 20.0 all-gather.20
  389.3 24.9 all-gather.22
  441.6 19.1 all-gather.24
  991.6 19.1 all-gather.26
  1018.9 31.4 reduce-scatter.12
  1407.9 34.5 reduce-scatter.14
  1478.0 27.7 reduce-scatter.16
  2034.0 28.3 reduce-scatter.18
  2067.7 133.6 all-reduce.360
  2206.2 88.6 all-reduce.362
where the time goes:
time: 2350 us; the launch traced here: 2310 us
  local copies, waits for them, and re-layouts  1270 us (54%)
  blocking collectives  404 us (17%)
  other arithmetic  315 us (13%)
  waiting for transfers between devices  254 us (11%)
  matrix products  41.7 us (2%)
  between operations  23.7 us (1%)
    slice x630, local copies, waits for them, and re-layouts, chain(): lax.associative_scan(linear_combine_operator, (mult_re, mult_im, drive_re...  772 us
    pad x320, local copies, waits for them, and re-layouts, chain(): lax.associative_scan(linear_combine_operator, (mult_re, mult_im, drive_re...  320 us
    all_gather x16, blocking collectives, carried_in(): gathered = jax.tree.map(lambda a: lax.all_gather(a, axis), part)  279 us
    psum x1, waiting for transfers between devices, on_device(): lax.psum((data_stack[0], data_stack[1], data_stack[2], data_stack[3], dat...  93.5 us
    add x160, other arithmetic, chain(): lax.associative_scan(linear_combine_operator, (mult_re, mult_im, drive_re...  86.7 us
    psum x1, waiting for transfers between devices, on_device(): lax.psum((full_stack[0], full_stack[1], full_stack[2], full_stack[3]), ('...  83.6 us
    unnamed x974, local copies, waits for them, and re-layouts  70.2 us
    concatenate x160, other arithmetic, chain(): lax.associative_scan(linear_combine_operator, (mult_re, mult_im, drive_re...  57 us
  transfers between devices with their start and end apart: 10, of which 5 were waited for; matrix products, arithmetic and copies ran while one was open for 8% of the time, Pallas kernels for 0%

commit v1 on v0

v1 whole, which is shorter than its diff:
```python
import functools

import jax
import jax.numpy as jnp
from jax import lax
from jax.experimental import pallas as pl
from jax.experimental.pallas import tpu as pltpu
from jax.sharding import PartitionSpec as P

epsilon = 1e-05
LANES = 128
SUB = 8
ROOT = 0.7978845608028654
CUBE = 0.044715
AXES = ("dp", "mp")
F32 = jnp.float32
BF16 = jnp.bfloat16
NT = (((1,), (1,)), ((), ()))
TN = (((0,), (0,)), ((), ()))
GAIN, SHIFT, SKIP, VBIAS, GBIAS = range(5)
PARAMS = 5


def params():
    return pltpu.CompilerParams(vmem_limit_bytes=48 * 1024 * 1024)


def call(body, outs, scratch, *args, scalars=0):
    specs = [pl.BlockSpec(memory_space=pltpu.SMEM)] * scalars + [
        pl.BlockSpec(memory_space=pltpu.VMEM)
    ] * (len(args) - scalars)
    return pl.pallas_call(
        body,
        out_shape=outs,
        in_specs=specs,
        out_specs=[pl.BlockSpec(memory_space=pltpu.VMEM)] * len(outs),
        scratch_shapes=scratch,
        compiler_params=params(),
    )(*args)


def cat(ref, rows):
    return jnp.concatenate([ref[j, rows, :] for j in range(ref.shape[0])], axis=1)


def put(ref, rows, val):
    for j in range(ref.shape[0]):
        ref[j, rows, :] = val[:, j * LANES : (j + 1) * LANES].astype(ref.dtype)


def rowcat(ref, r):
    return jnp.concatenate([ref[j, r : r + 1, :] for j in range(ref.shape[0])], axis=1)


def lanes(rows):
    return jnp.concatenate([rows[j : j + 1, :] for j in range(rows.shape[0])], axis=1)


def dot(a, b):
    return jnp.dot(a, b, preferred_element_type=F32)


def dot_nt(a, b):
    return lax.dot_general(a, b, NT, preferred_element_type=F32)


def dot_tn(a, b):
    return lax.dot_general(a, b, TN, preferred_element_type=F32)


def chunks(rows, count):
    size = rows // count
    return [slice(i * size, (i + 1) * size) for i in range(count)]


def sweep(src, dst, table, init, reset, reverse, conj, extra=None):
    halves = src.shape[0] // 2
    span = src.shape[1] // SUB
    rate_re = [jnp.broadcast_to(table[h : h + 1, :], (SUB, LANES)) for h in range(halves)]
    rate_im = [
        jnp.broadcast_to(table[halves + h : halves + h + 1, :], (SUB, LANES))
        for h in range(halves)
    ]
    if conj:
        rate_im = [-r for r in rate_im]
    base = lax.broadcasted_iota(jnp.int32, (SUB, LANES), 0) * span - reset

    def body(step, carry):
        j = span - 1 - step if reverse else step
        state, sums = carry
        drop = base == -j
        at = pl.ds(j, SUB, stride=span)
        new_re, new_im = [], []
        for h in range(halves):
            a = jnp.where(drop, 0.0, rate_re[h])
            b = jnp.where(drop, 0.0, rate_im[h])
            re, im = state[h], state[halves + h]
            new_re.append((src[h, at, :] + a * re) - b * im)
            new_im.append((src[halves + h, at, :] + a * im) + b * re)
        state = tuple(new_re + new_im)
        if dst is not None:
            for k in range(2 * halves):
                dst[k, at, :] = state[k]
        if extra is not None:
            sums = extra(at, state, sums)
        return state, sums

    sums = ()
    if extra is not None:
        sums = tuple(jnp.zeros((SUB, LANES), F32) for _ in range(4 * halves))
    return lax.fori_loop(0, span, body, (init, sums), unroll=8)


def zeros_state(halves):
    return tuple(jnp.zeros((SUB, LANES), F32) for _ in range(2 * halves))


def chain_segments(ends, first, table, reset, span, reverse, conj):
    halves = len(ends) // 2
    power_re = [table[4 + h : 5 + h, :] for h in range(halves)]
    power_im = [table[6 + h : 7 + h, :] for h in range(halves)]
    if conj:
        power_im = [-r for r in power_im]
    state = list(first)
    incoming = [[None] * SUB for _ in ends]
    order = range(SUB - 1, -1, -1) if reverse else range(SUB)
    for k in order:
        inside = (reset >= k * span) & (reset < (k + 1) * span)
        keep = jnp.where(inside, 0.0, 1.0)
        new = [None] * len(ends)
        for h in range(halves):
            re, im = state[h], state[halves + h]
            incoming[h][k], incoming[halves + h][k] = re, im
            new[h] = keep * (power_re[h] * re - power_im[h] * im) + ends[h][k : k + 1, :]
            new[halves + h] = (
                keep * (power_re[h] * im + power_im[h] * re) + ends[halves + h][k : k + 1, :]
            )
        state = new
    return [jnp.concatenate(rows, axis=0) for rows in incoming], state


def zero_rows(halves):
    return [jnp.zeros((1, LANES), F32) for _ in range(2 * halves)]


def emit_ends(out, ends_out, ends, table, reset, span, reverse, conj):
    halves = len(ends) // 2
    _, last = chain_segments(ends, zero_rows(halves), table, reset, span, reverse, conj)
    tile = jnp.concatenate(last, axis=0)
    out[...] = jnp.broadcast_to(tile[None], out.shape)
    for k in range(2 * halves):
        ends_out[k, :, :] = ends[k]


def carried_in(gathered, moments, table, me, reverse, conj):
    count = gathered.shape[0]
    power_re = table[8:10, :]
    power_im = table[10:12, :]
    if conj:
        power_im = -power_im
    flag = 3 if reverse else 2

    def body(i, state):
        d = count - 1 - i if reverse else i
        re, im = state
        keep = moments[d, flag : flag + 1, :]
        tile = gathered[d]
        return (
            keep * (power_re * re - power_im * im) + tile[0:2, :],
            keep * (power_re * im + power_im * re) + tile[2:4, :],
        )

    zero = jnp.zeros((2, LANES), F32)
    re, im = lax.fori_loop(0, count - 1 - me if reverse else me, body, (zero, zero))
    return [re[0:1, :], re[1:2, :], im[0:1, :], im[1:2, :]]


def local_resets(offset, mp, rows):
    shift = jnp.where(offset > 0, offset - mp * rows, -(1 << 20))
    return shift, shift - 1


def first_kernel(rows, scal, stream, plist, decay, phase, scale, packed, moments, table):
    offset, mp = scal[0], scal[1]
    total = stream.shape[0]
    parts = packed.shape[0]
    size = 64

    def body(i, carry):
        one, two = carry
        x = stream[pl.ds(i * size, size), :]
        for g in range(0, size, SUB):
            piece = x[g : g + SUB, :]
            one = one + piece
            two = two + piece * piece
        packed[(i * size) // rows, pl.ds((i * size) % rows, size), :] = x
        return one, two

    zero = jnp.zeros((SUB, LANES), F32)
    one, two = lax.fori_loop(0, total // size, body, (zero, zero))
    for j in range(parts):
        packed[j, rows : rows + plist.shape[0], :] = plist[...]
    fwd, bwd = local_resets(offset, mp, rows)
    keep_f = jnp.where((fwd >= 0) & (fwd < rows), 0.0, 1.0)
    keep_b = jnp.where((bwd >= 0) & (bwd < rows), 0.0, 1.0)
    tile = jnp.concatenate(
        [
            jnp.sum(one, axis=0, keepdims=True),
            jnp.sum(two, axis=0, keepdims=True),
            jnp.full((1, LANES), keep_f, F32),
            jnp.full((1, LANES), keep_b, F32),
        ],
        axis=0,
    )
    moments[...] = jnp.broadcast_to(tile[None], moments.shape)
    span = rows // SUB
    for layer in range(decay.shape[0]):
        for h in range(2):
            cols = slice(h * LANES, (h + 1) * LANES)
            radius = jnp.exp(-jnp.exp(decay[layer : layer + 1, cols]))
            angle = jnp.exp(phase[layer : layer + 1, cols])
            re, im = radius * jnp.cos(angle), radius * jnp.sin(angle)
            table[layer, h : h + 1, :] = re
            table[layer, 2 + h : 3 + h, :] = im
            length = 1
            while length < rows:
                re, im = re * re - im * im, 2.0 * re * im
                length *= 2
                if length == span:
                    table[layer, 4 + h : 5 + h, :] = re
                    table[layer, 6 + h : 7 + h, :] = im
            table[layer, 8 + h : 9 + h, :] = re
            table[layer, 10 + h : 11 + h, :] = im
            table[layer, 12 + h : 13 + h, :] = jnp.exp(scale[layer : layer + 1, cols])
            table[layer, 14 + h : 15 + h, :] = jnp.zeros((1, LANES), F32)


def norm_rows(mean, second, gain, shift):
    inverse = lax.rsqrt(second - mean * mean + epsilon)
    factor = inverse * gain
    return inverse, factor, shift - mean * factor


def drive_body(layer, total_tokens, scal, h, mom, prm, prm_base, table, weight, drive, norms, out, ends_out):
    offset, mp = scal[0], scal[1]
    rows = drive.shape[1]
    reverse = layer % 2 == 1
    if layer == 0:
        groups = prm.shape[0]
        sums = [mom[j, 0:2, :] for j in range(groups)]
        for d in range(groups, mom.shape[0]):
            sums[d % groups] = sums[d % groups] + mom[d, 0:2, :]
        both = jnp.concatenate(sums, axis=1) * (1.0 / total_tokens)
        mean, second = both[0:1, :], both[1:2, :]
    else:
        tile = mom[0]
        for d in range(1, mom.shape[0]):
            tile = tile + mom[d]
        tile = tile * (1.0 / total_tokens)
        half = tile.shape[0] // 2
        mean, second = lanes(tile[:half]), lanes(tile[half:])
    base = prm_base + layer * PARAMS
    inverse, factor, bias = norm_rows(
        mean, second, rowcat(prm, base + GAIN), rowcat(prm, base + SHIFT)
    )
    norms[...] = jnp.concatenate(
        [factor, bias, inverse, mean] + [jnp.zeros_like(mean)] * 4, axis=0
    )
    gamma = lanes(table[layer, 12:14, :])
    gamma = jnp.concatenate([gamma, gamma], axis=1)
    for at in chunks(rows, 2):
        low = (cat(h, at) * factor + bias).astype(BF16)
        put(drive, at, dot(low, weight[layer]) * gamma)
    fwd, bwd = local_resets(offset, mp, rows)
    reset = bwd if reverse else fwd
    ends, _ = sweep(drive, None, table[layer], zeros_state(2), reset, reverse, False)
    emit_ends(out, ends_out, ends, table[layer], reset, rows // SUB, reverse, False)


def drive_first(layer, total_tokens, scal, h, mom, table, weight, drive, norms, out, ends, prm_out):
    rows = drive.shape[1]
    drive_body(layer, total_tokens, scal, h, mom, h, rows, table, weight, drive, norms, out, ends)
    for j in range(prm_out.shape[0]):
        prm_out[j, :, :] = h[j, rows : rows + prm_out.shape[1], :]


def drive_next(layer, total_tokens, scal, h, mom, prm, table, weight, drive, norms, out, ends):
    drive_body(layer, total_tokens, scal, h, mom, prm, 0, table, weight, drive, norms, out, ends)


def resume(scal, rows, gathered, mom, tab, ends, reverse, conj):
    offset, mp, me = scal[0], scal[1], scal[2]
    fwd, bwd = local_resets(offset, mp, rows)
    reset = bwd if reverse else fwd
    first = carried_in(gathered, mom, tab, me, reverse, conj)
    incoming, _ = chain_segments(
        [ends[k] for k in range(4)], first, tab, reset, rows // SUB, reverse, conj
    )
    return tuple(incoming), reset


def mix_chunk(layer, at, h, norms, states, c_map, v_map, g_map, prm):
    base = layer * PARAMS
    x = cat(h, at)
    scaled = x * norms[0:1, :] + norms[1:2, :]
    states_low = cat(states, at).astype(BF16)
    mixed = dot(states_low, c_map) + rowcat(prm, base + SKIP) * scaled
    square = mixed * mixed
    wave = jnp.tanh(ROOT * mixed * (1.0 + CUBE * square))
    half = 0.5 * (1.0 + wave)
    sent_low = (mixed * half).astype(BF16)
    slope = half + 0.5 * mixed * (1.0 - wave * wave) * (ROOT * (1.0 + 3.0 * CUBE * square))
    value = dot(sent_low, v_map) + rowcat(prm, base + VBIAS)
    gate = dot(sent_low, g_map) + rowcat(prm, base + GBIAS)
    sig = 0.5 + 0.5 * jnp.tanh(0.5 * gate)
    gated = value * sig
    return x, scaled, states_low, sent_low, slope, sig, gated


def back_chunk(layer, at, g, sig, gain_part, sent_low, states_low, scaled, slope, c_map, v_map, g_map, refs, sums):
    dv_ref, dg_ref, dm_ref, dmlow_ref, ds = refs
    dvalue = g * sig
    dgate = g * gain_part
    dv_low, dg_low = dvalue.astype(BF16), dgate.astype(BF16)
    dmixed = (dot_nt(dv_low, v_map) + dot_nt(dg_low, g_map)) * slope
    dm_low = dmixed.astype(BF16)
    put(ds, at, dot_nt(dm_low, c_map))
    dv_ref[at, :] = dv_low
    dg_ref[at, :] = dg_low
    dmlow_ref[at, :] = dm_low
    put(dm_ref, at, dmixed)
    add = lambda v: jnp.sum(v, axis=0, keepdims=True)
    return [
        s + n for s, n in zip(sums, [add(dvalue), add(dgate), add(dmixed * scaled)], strict=True)
    ]


def weight_grads(pack, sent, states, dv, dg, dm, sums):
    width = sent.shape[1]
    parts = pack.shape[0]
    for first, left, right in ((0, sent, dv), (1, sent, dg), (2, states, dm)):
        grad = dot_tn(left[...], right[...])
        put(pack, slice(first * width, (first + 1) * width), grad)
    top = 3 * width
    for j in range(parts):
        cols = slice(j * LANES, (j + 1) * LANES)
        rows = [s[:, cols] for s in sums] + [jnp.zeros((16 - len(sums), LANES), F32)]
        pack[j, top : top + 16, :] = jnp.concatenate(rows, axis=0).astype(pack.dtype)


def add_chunk(mom, one, two):
    tile = jnp.concatenate(
        [one[:, j * LANES : (j + 1) * LANES] for j in range(one.shape[1] // LANES)]
        + [two[:, j * LANES : (j + 1) * LANES] for j in range(two.shape[1] // LANES)],
        axis=0,
    )
    mom[...] = jnp.broadcast_to(tile[None], mom.shape)


def mix_first(layer, scal, gathered, mom, table, ends, h, norms, drive, prm, c4, v4, g4,
              states, sent, slope_out, sig_out, part_out, new_h, new_mom):
    rows = drive.shape[1]
    reverse = layer % 2 == 1
    tab = table[layer]
    init, reset = resume(scal, rows, gathered, mom, tab, ends, reverse, False)
    sweep(drive, states, tab, init, reset, reverse, False)
    c_map, v_map, g_map = cat(c4, slice(None)), cat(v4, slice(None)), cat(g4, slice(None))
    one = two = 0.0
    for at in chunks(rows, 2):
        x, scaled, states_low, sent_low, slope, sig, gated = mix_chunk(
            layer, at, h, norms, states, c_map, v_map, g_map, prm
        )
        sent[at, :] = sent_low
        put(slope_out, at, slope)
        put(sig_out, at, sig)
        put(part_out, at, gated * (1.0 - sig))
        new = x + gated
        put(new_h, at, new)
        one = one + jnp.sum(new, axis=0, keepdims=True)
        two = two + jnp.sum(new * new, axis=0, keepdims=True)
    add_chunk(new_mom, one, two)


def turn(layer, scal, gathered, mom, table, ends, h, norms, drive, prm, c4, v4, g4, cot,
         states, new_h, ds, dm, pack, out, ends_out, sent, slow, dv, dg, dml):
    rows = drive.shape[1]
    reverse = layer % 2 == 1
    tab = table[layer]
    init, reset = resume(scal, rows, gathered, mom, tab, ends, reverse, False)
    sweep(drive, states, tab, init, reset, reverse, False)
    c_map, v_map, g_map = cat(c4, slice(None)), cat(v4, slice(None)), cat(g4, slice(None))
    sums = [0.0, 0.0, 0.0]
    for at in chunks(rows, 2):
        x, scaled, states_low, sent_low, slope, sig, gated = mix_chunk(
            layer, at, h, norms, states, c_map, v_map, g_map, prm
        )
        sent[at, :] = sent_low
        slow[at, :] = states_low
        put(new_h, at, x + gated)
        sums = back_chunk(layer, at, cat(cot, at), sig, gated * (1.0 - sig), sent_low, states_low,
                          scaled, slope, c_map, v_map, g_map, (dv, dg, dm, dml, ds), sums)
    adjoint_start(layer, scal, tab, ds, out, ends_out)
    weight_grads(pack, sent, slow, dv, dg, dml, sums)


def adjoint_start(layer, scal, tab, ds, out, ends_out):
    rows = ds.shape[1]
    reverse = layer % 2 == 0
    fwd, bwd = local_resets(scal[0], scal[1], rows)
    reset = bwd if reverse else fwd
    ends, _ = sweep(ds, None, tab, zeros_state(2), reset, reverse, True)
    emit_ends(out, ends_out, ends, tab, reset, rows // SUB, reverse, True)


def corrected(total_tokens, layer, u, normed, norms, back, prm):
    tile = back[0]
    for d in range(1, back.shape[0]):
        tile = tile + back[d]
    half = tile.shape[0] // 2
    factor = norms[0:1, :] * (1.0 / total_tokens)
    return u - factor * lanes(tile[:half]) - normed * (factor * lanes(tile[half:]))


def back_first(layer, total_tokens, scal, back, u, h1, norms1, h, norms, sent, states, slope, sig, part,
               prm, table, c4, v4, g4, g_out, ds, dm, pack, out, ends_out, slow, dv, dg, dml):
    rows = ds.shape[1]
    tab = table[layer]
    tile = back[0]
    for d in range(1, back.shape[0]):
        tile = tile + back[d]
    half = tile.shape[0] // 2
    factor = norms1[0:1, :] * (1.0 / total_tokens)
    m_one, m_two = factor * lanes(tile[:half]), factor * lanes(tile[half:])
    inverse1, mean1 = norms1[2:3, :], norms1[3:4, :]
    c_map, v_map, g_map = cat(c4, slice(None)), cat(v4, slice(None)), cat(g4, slice(None))
    sums = [0.0, 0.0, 0.0]
    for at in chunks(rows, 2):
        normed1 = (cat(h1, at) - mean1) * inverse1
        g = cat(u, at) - m_one - normed1 * m_two
        put(g_out, at, g)
        scaled = cat(h, at) * norms[0:1, :] + norms[1:2, :]
        states_low = cat(states, at).astype(BF16)
        slow[at, :] = states_low
        sums = back_chunk(layer, at, g, cat(sig, at), cat(part, at), sent[at, :], states_low, scaled,
                          cat(slope, at), c_map, v_map, g_map, (dv, dg, dm, dml, ds), sums)
    adjoint_start(layer, scal, tab, ds, out, ends_out)
    weight_grads(pack, sent, slow, dv, dg, dml, sums)


def back_second(layer, scal, gathered, mom, table, ends, ds, drive, states, h, norms, dm, g, prm, weight,
                u_out, back, pack, adj, slow, dlow):
    rows = ds.shape[1]
    reverse = layer % 2 == 0
    tab = table[layer]
    init, reset = resume(scal, rows, gathered, mom, tab, ends, reverse, True)

    def extra(at, a, sums):
        new = []
        for h_ in range(2):
            re, im = a[h_], a[2 + h_]
            for ref in (states, drive):
                sre, sim = ref[h_, at, :], ref[2 + h_, at, :]
                new.append(re * sre + im * sim)
                new.append(im * sre - re * sim)
        return tuple(s + n for s, n in zip(sums, new, strict=True))

    _, sums = sweep(ds, adj, tab, init, reset, reverse, True, extra)
    flat = [jnp.sum(s, axis=0, keepdims=True) for s in sums]
    gamma = lanes(tab[12:14, :])
    gamma = jnp.concatenate([gamma, gamma], axis=1)
    base = layer * PARAMS
    gain, skip = rowcat(prm, base + GAIN), rowcat(prm, base + SKIP)
    factor, bias, inverse, mean = (norms[i : i + 1, :] for i in range(4))
    one = two = 0.0
    for at in chunks(rows, 2):
        x = cat(h, at)
        normed = (x - mean) * inverse
        slow[at, :] = (x * factor + bias).astype(BF16)
        low = (cat(adj, at) * gamma).astype(BF16)
        dlow[at, :] = low
        dscaled = dot_nt(low, weight[layer]) + cat(dm, at) * skip
        put(u_out, at, cat(g, at) + factor * dscaled)
        one = one + jnp.sum(dscaled, axis=0, keepdims=True)
        two = two + jnp.sum(dscaled * normed, axis=0, keepdims=True)
    add_chunk(back, one, two)
    put(pack, slice(0, slow.shape[1]), dot_tn(slow[...], dlow[...]))
    top = slow.shape[1]
    rows_out = []
    for h_ in range(2):
        x_re, x_im, y_re, y_im = flat[4 * h_ : 4 * h_ + 4]
        rows_out += [x_re - y_re, x_im - y_im, y_re]
    tile = jnp.concatenate(rows_out + [jnp.zeros((16 - 6, LANES), F32)], axis=0).astype(pack.dtype)
    for j in range(pack.shape[0]):
        pack[j, top : top + 16, :] = tile


def last_kernel(total_tokens, groups, scal, u, stream, norms, back, out, sums_out):
    mp = scal[1]
    tile = back[0]
    for d in range(1, back.shape[0]):
        tile = tile + back[d]
    half = tile.shape[0] // 2
    one = two = factor = inverse = mean = jnp.zeros((1, LANES), F32)
    for j in range(groups):
        mine = jnp.where(mp == j, 1.0, 0.0)
        cols = slice(j * LANES, (j + 1) * LANES)
        one = one + mine * tile[j : j + 1, :]
        two = two + mine * tile[half + j : half + j + 1, :]
        factor = factor + mine * norms[0:1, cols]
        inverse = inverse + mine * norms[2:3, cols]
        mean = mean + mine * norms[3:4, cols]
    scaled = factor * (1.0 / total_tokens)
    m_one, m_two = scaled * one, scaled * two
    size = 128

    def body(i, carry):
        at = pl.ds(i * size, size)
        normed = (stream[at, :] - mean) * inverse
        out[at, :] = u[at, :] - m_one - normed * m_two
        return carry

    lax.fori_loop(0, out.shape[0] // size, body, 0)
    sums_out[...] = jnp.concatenate([one, two] + [jnp.zeros((6, LANES), F32)], axis=0)


def shape(dims, dtype=F32):
    return jax.ShapeDtypeStruct(tuple(dims), dtype)


def every(x):
    return lax.all_to_all(x, AXES, 0, 0)


def across(x):
    return lax.all_to_all(x, "mp", 0, 0)


def reduced(pack, count_dp):
    parts, rows, width = pack.shape
    own = jnp.sum(across(pack).astype(F32), axis=0)
    unit = 16 * count_dp
    padded = -(-rows // unit) * unit
    own = jnp.pad(own, ((0, padded - rows), (0, 0))).astype(BF16)
    pieces = lax.all_to_all(own.reshape(count_dp, padded // count_dp, width), "dp", 0, 0)
    mine = jnp.sum(pieces.astype(F32), axis=0).astype(BF16)
    full = lax.all_to_all(jnp.broadcast_to(mine[None], (count_dp,) + mine.shape), "dp", 0, 0)
    return full.reshape(padded, width)[:rows]


def on_device(
    stream,
    cotangent,
    start_offsets,
    norm_gain,
    norm_shift,
    input_map,
    decay_log,
    phase_log,
    scale_log,
    output_map,
    skip_gain,
    value_weight,
    gate_weight,
    value_bias,
    gate_bias,
):
    block, width = stream.shape
    layers = input_map.shape[0]
    count_dp, parts = lax.axis_size("dp"), lax.axis_size("mp")
    devices = count_dp * parts
    tokens = block * count_dp
    rows = block // parts
    features = width * parts
    assert width == LANES and features == 4 * LANES and layers == 2
    mp = lax.axis_index("mp")
    me = lax.axis_index("dp") * parts + mp
    scal = jnp.stack([start_offsets[0], mp, me]).astype(jnp.int32)

    plist = jnp.concatenate(
        [
            a[layer : layer + 1]
            for layer in range(layers)
            for a in (norm_gain, norm_shift, skip_gain, value_bias, gate_bias)
        ]
        + [jnp.zeros((16 - PARAMS * layers, width), F32)],
        axis=0,
    )
    blocks = (parts, rows, width)
    tall = (parts, rows + 16, width)
    ends_shape = shape((4, SUB, LANES))
    every_shape = shape((devices, 4, LANES))
    sums_shape = shape((devices, 2 * parts, LANES))
    norm_shape = shape((8, features))

    packed, mom_out, table = call(
        functools.partial(first_kernel, rows),
        [shape(tall), every_shape, shape((layers, 16, LANES))],
        [],
        scal, stream, plist, decay_log, phase_log, scale_log,
        scalars=1,
    )
    h0 = across(packed)
    mom0 = every(mom_out)
    cot = across(cotangent.reshape(blocks))
    maps = []
    for layer in range(layers):
        own = jnp.stack([output_map[layer], value_weight[layer], gate_weight[layer]])
        got = across(jnp.broadcast_to(own[None], (parts,) + own.shape))
        maps.append([got[:, k] for k in range(3)])

    drive0, norms0, ends_all, ends0, prm = call(
        functools.partial(drive_first, 0, tokens),
        [shape(blocks), norm_shape, every_shape, ends_shape, shape((parts, 16, width))],
        [],
        scal, h0, mom0, table, input_map,
        scalars=1,
    )
    got = every(ends_all)
    states0, sent0, slope0, sig0, part0, h1, mom_out = call(
        functools.partial(mix_first, 0),
        [shape(blocks), shape((rows, features), BF16), shape(blocks), shape(blocks), shape(blocks),
         shape(blocks), sums_shape],
        [],
        scal, got, mom0, table, ends0, h0, norms0, drive0, prm, *maps[0],
        scalars=1,
    )
    mom1 = every(mom_out)
    drive1, norms1, ends_all, ends1 = call(
        functools.partial(drive_next, 1, tokens),
        [shape(blocks), norm_shape, every_shape, ends_shape],
        [],
        scal, h1, mom1, prm, table, input_map,
        scalars=1,
    )
    got = every(ends_all)
    low = pltpu.VMEM((rows, features), BF16)
    pack_shape = shape((parts, 3 * features + 16, width), BF16)
    states1, h2, ds1, dm1, pack1, ends_all, back_ends1 = call(
        functools.partial(turn, 1),
        [shape(blocks), shape(blocks), shape(blocks), shape(blocks), pack_shape, every_shape, ends_shape],
        [low] * 5,
        scal, got, mom0, table, ends1, h1, norms1, drive1, prm, *maps[1], cot,
        scalars=1,
    )
    result = across(h2).reshape(block, width)
    got = every(ends_all)
    in_pack_shape = shape((parts, features + 16, width), BF16)
    u1, back_out, in_pack1 = call(
        functools.partial(back_second, 1),
        [shape(blocks), sums_shape, in_pack_shape],
        [pltpu.VMEM(blocks, F32), low, low],
        scal, got, mom0, table, back_ends1, ds1, drive1, states1, h1, norms1, dm1, cot, prm, input_map,
        scalars=1,
    )
    back1 = every(back_out)
    g0, ds0, dm0, pack0, ends_all, back_ends0 = call(
        functools.partial(back_first, 0, tokens),
        [shape(blocks), shape(blocks), shape(blocks), pack_shape, every_shape, ends_shape],
        [low] * 4,
        scal, back1, u1, h1, norms1, h0, norms0, sent0, states0, slope0, sig0, part0, prm, table, *maps[0],
        scalars=1,
    )
    got = every(ends_all)
    u0, back_out, in_pack0 = call(
        functools.partial(back_second, 0),
        [shape(blocks), sums_shape, in_pack_shape],
        [pltpu.VMEM(blocks, F32), low, low],
        scal, got, mom0, table, back_ends0, ds0, drive0, states0, h0, norms0, dm0, g0, prm, input_map,
        scalars=1,
    )
    u0 = across(u0).reshape(block, width)
    back0 = every(back_out)
    stream_grad, own_sums0 = call(
        functools.partial(last_kernel, tokens, parts),
        [shape((block, width)), shape((8, width))],
        [],
        scal, u0, stream, norms0, back0,
        scalars=1,
    )

    own_sums1 = lax.dynamic_slice_in_dim(
        jnp.sum(back1, axis=0).reshape(2, parts, width), mp, 1, axis=1
    ).reshape(2, width)
    gain_grad = jnp.stack([own_sums0[1], own_sums1[1]])
    shift_grad = jnp.stack([own_sums0[0], own_sums1[0]])

    vgo, inputs = [], []
    for pack, in_pack in ((pack0, in_pack0), (pack1, in_pack1)):
        full = reduced(jnp.concatenate([pack, in_pack], axis=1), count_dp)
        split = 3 * features + 16
        vgo.append(full[:split].astype(F32))
        inputs.append(full[split:])
    mats = jnp.stack([g[: 3 * features] for g in vgo]).reshape(layers, 3, features, width)
    vecs = jnp.stack([g[3 * features : 3 * features + 3] for g in vgo])
    in_own = jnp.stack([g[:features] for g in inputs])
    in_all = across(jnp.broadcast_to(in_own[None], (parts,) + in_own.shape))
    input_grad = in_all.transpose(1, 2, 0, 3).reshape(layers, features, features).astype(F32)
    state_vecs = jnp.stack([g[features : features + 6] for g in inputs]).astype(F32)
    state_vecs = state_vecs.reshape(layers, 2, 3, LANES).transpose(2, 0, 1, 3).reshape(3, layers, -1)
    decay_grad = -jnp.exp(decay_log) * state_vecs[0]
    phase_grad = jnp.exp(phase_log) * state_vecs[1]
    scale_grad = state_vecs[2]
    return (
        result,
        stream_grad,
        gain_grad,
        shift_grad,
        input_grad,
        decay_grad,
        phase_grad,
        scale_grad,
        mats[:, 2],
        vecs[:, 2],
        mats[:, 0],
        mats[:, 1],
        vecs[:, 0],
        vecs[:, 1],
    )


def solution(mesh):
    split = P("dp", "mp")
    cols = P(None, "mp")
    wide = P(None, None, "mp")
    placed = (
        split, split, P("dp"), cols, cols, P(), P(), P(), P(), wide, cols, wide, wide, cols, cols,
    )
    return jax.shard_map(
        on_device,
        mesh=mesh,
        in_specs=placed,
        out_specs=(
            split, split, cols, cols, P(), P(), P(), P(), wide, cols, wide, wide, cols, cols,
        ),
        check_vma=False,
    )
```

time: 2350 us -> 416 us (0.18); the launches traced: 2310 us -> 414 us
  local copies, waits for them, and re-layouts: 1270 us -> 34.5 us
  blocking collectives: 404 us -> 93.4 us
  other arithmetic: 315 us -> 19.6 us
  waiting for transfers between devices: 254 us -> 169 us
  starting transfers between devices: 1.03 us -> 50 us
  Pallas kernels: 0 us -> 46.2 us
  matrix products: 41.7 us -> 0 us
    slice x633 -> x14, local copies, waits for them, and re-layouts: 775 us -> 4.5 us  [the longest x3 2.28 us: on_device(): a[layer:layer + 1]]
    pad x320 -> x2, local copies, waits for them, and re-layouts: 320 us -> 2.82 us  [reduced(): own = jnp.pad(own, ((0, padded - rows), (0, 0))).astype(BF16)]
    all_gather x16 -> x0, blocking collectives: 279 us -> none  [carried_in(): gathered = jax.tree.map(lambda a: lax.all_gather(a, axis), part)]
    psum x2 -> x0, waiting for transfers between devices: 177 us -> none  [the longest x1 93.5 us: on_device(): lax.psum((data_stack[0], data_stack[1], data_stack[2], data_stack[3], dat...]
    add x291 -> x0, other arithmetic: 174 us -> none  [the longest x160 86.7 us: chain(): lax.associative_scan(linear_combine_operator, (mult_re, mult_im, drive_re...]
    all_to_all x0 -> x14, waiting for transfers between devices: none -> 169 us  [the longest x7 101 us: across(): return lax.all_to_all(x, 'mp', 0, 0)]
    psum x5 -> x0, blocking collectives: 125 us -> none  [the longest x2 44.5 us: on_device(): lax.psum((jnp.sum(hidden, axis=0), jnp.sum(hidden * hidden, axis=0)), 'dp')]
    all_to_all x0 -> x7, blocking collectives: none -> 93.4 us  [the longest x5 52.5 us: every(): return lax.all_to_all(x, AXES, 0, 0)]
  transfers between devices with their start and end apart: 10 -> 14, of which waited for: 5 -> 14; matrix products, arithmetic and copies ran while one was open for 8% -> 7% of each run, Pallas kernels for 0% -> 3%
where the time goes in v1:
time: 416 us; the launch traced here: 414 us
  waiting for transfers between devices  169 us (41%)
  blocking collectives  93.4 us (22%)
  starting transfers between devices  50 us (12%)
  Pallas kernels  46.2 us (11%)
  local copies, waits for them, and re-layouts  34.5 us (8%)
  other arithmetic  19.6 us (5%)
    all_to_all x7, waiting for transfers between devices, across(): return lax.all_to_all(x, 'mp', 0, 0)  101 us
    all_to_all x5, blocking collectives, every(): return lax.all_to_all(x, AXES, 0, 0)  52.5 us
    pallas_call x9, Pallas kernels, call(): pl.pallas_call(body, out_shape=outs, in_specs=specs, out_specs=[pl.BlockS...  46.2 us
    all_to_all x2, blocking collectives, across(): return lax.all_to_all(x, 'mp', 0, 0)  40.9 us
    all_to_all x7, starting transfers between devices, across(): return lax.all_to_all(x, 'mp', 0, 0)  27.4 us
    all_to_all x2, waiting for transfers between devices, reduced(): lax.all_to_all(own.reshape(count_dp, padded // count_dp, width), 'dp', 0, 0)  24.6 us
    all_to_all x2, waiting for transfers between devices, reduced(): lax.all_to_all(jnp.broadcast_to(mine[None], (count_dp,) + mine.shape), 'd...  24.4 us
    all_to_all x3, waiting for transfers between devices, every(): return lax.all_to_all(x, AXES, 0, 0)  19 us
  transfers between devices with their start and end apart: 14, of which 14 were waited for; matrix products, arithmetic and copies ran while one was open for 7% of the time, Pallas kernels for 3%

profile of v1, /device:TPU:0, one launch (start us, length us, event | category | flops | bytes accessed | tf_op | source)
XLA Modules:
  0.0 414.4 jit_solution(11644907490063805808)
XLA Ops:
  8.9 14.5 %all_to_all.105.mom = f32[32,4,128]{2,1,0:T(4,128)S(1)} all-to-all(f32[32,4,128]{2,1,0:T(4,128)S(1)} %get-tuple-element.55), channel_id=1, replica_groups=mesh['dp'=8,'mp'=4] {'dp','mp'}, dimensions={0} | all-to-all | bytes 131072 | tf_op jit(solution)/shard_map/all_to_all | solution.py:531
  27.7 14.0 %all-to-all-done.h = f32[4,528,128]{2,1,0:T(8,128)S(1)} async-done(((f32[4,528,128]{2,1,0:T(8,128)}), f32[4,528,128]{2,1,0:T(8,128)S(1)}, u32[]{:S(2)}, u32[]{:S(2)}) %all-to-all-start) | async-done | bytes 1081376 | tf_op jit(solution)/shard_map/all_to_all | solution.py:535
  48.3 6.7 %all-to-all-done.2.gathered = f32[32,4,128]{2,1,0:T(4,128)S(1)} async-done(((f32[32,4,128]{2,1,0:T(4,128)}), f32[32,4,128]{2,1,0:T(4,128)S(1)}, u32[]{:S(2)}, u32[]{:S(2)}) %all-to-all-start.2) | async-done | bytes 65568 | tf_op jit(solution)/shard_map/all_to_all | solution.py:531
  55.3 23.3 %all_to_all.106 = bf16[4,3,512,128]{3,2,1,0:T(8,128)(2,1)} all-to-all(bf16[4,3,512,128]{3,2,1,0:T(8,128)(2,1)S(1)} %broadcast_in_dim.13), channel_id=1, replica_groups=mesh['dp'=8,'mp'=4] {'mp'}, dimensions={0} | all-to-all | bytes 3145728 | tf_op jit(solution)/shard_map/all_to_all | solution.py:535
  83.6 6.3 %shard_map.256 = (f32[4,512,128]{2,1,0:T(8,128)S(1)}, bf16[512,512]{1,0:T(8,128)(2,1)S(1)}, f32[4,512,128]{2,1,0:T(8,128)S(1)}, f32[4,512,128]{2,1,0:T(8,128)S(1...) custom-call(s32[3]{0:T(128)S(1)} %pad_add_fusion.scal, ...), custom_call_target="tpu_custom_call" | custom-call | tf_op jit(solution)/shard_map/pallas_call | solution.py:32
  100.9 6.4 %all-to-all-done.4.mom = f32[32,8,128]{2,1,0:T(8,128)S(1)} async-done(((f32[32,8,128]{2,1,0:T(8,128)}), f32[32,8,128]{2,1,0:T(8,128)S(1)}, u32[]{:S(2)}, u32[]{:S(2)}) %all-to-all-start.4) | async-done | bytes 131104 | tf_op jit(solution)/shard_map/all_to_all | solution.py:531
  118.1 16.2 %all-to-all-done.6 = bf16[4,3,512,128]{3,2,1,0:T(8,128)(2,1)} async-done(((bf16[4,3,512,128]{3,2,1,0:T(8,128)(2,1)}), bf16[4,3,512,128]{3,2,1,0:T(8,128)(2,1)}, u32[]{:S(2)}, u32[]{:S(2)}) %all-to-all-start.6) | async-done | bytes 1572896 | tf_op jit(solution)/shard_map/all_to_all | solution.py:535
  138.3 5.9 %all-to-all-done.5.gathered = f32[32,4,128]{2,1,0:T(4,128)S(1)} async-done(((f32[32,4,128]{2,1,0:T(4,128)}), f32[32,4,128]{2,1,0:T(4,128)S(1)}, u32[]{:S(2)}, u32[]{:S(2)}) %all-to-all-start.5) | async-done | bytes 65568 | tf_op jit(solution)/shard_map/all_to_all | solution.py:531
  144.3 9.7 %shard_map.258 = (f32[4,512,128]{2,1,0:T(8,128)S(1)}, f32[4,512,128]{2,1,0:T(8,128)S(1)}, f32[4,512,128]{2,1,0:T(8,128)S(1)}, f32[4,512,128]{2,1,0:T(8,128)S(1)}...) custom-call(s32[3]{0:T(128)S(1)} %copy-done.22, ...), custom_call_target="tpu_custom_call" | custom-call | tf_op jit(solution)/shard_map/pallas_call | solution.py:32
  155.0 9.1 %all_to_all.107.gathered = f32[32,4,128]{2,1,0:T(4,128)S(1)} all-to-all(f32[32,4,128]{2,1,0:T(4,128)S(1)} %get-tuple-element.69), channel_id=1, replica_groups=mesh['dp'=8,'mp'=4] {'dp','mp'}, dimensions={0} | all-to-all | bytes 131072 | tf_op jit(solution)/shard_map/all_to_all | solution.py:531
  170.7 9.9 %all_to_all.108.back = f32[32,8,128]{2,1,0:T(8,128)S(1)} all-to-all(f32[32,8,128]{2,1,0:T(8,128)S(1)} %get-tuple-element.74), channel_id=1, replica_groups=mesh['dp'=8,'mp'=4] {'dp','mp'}, dimensions={0} | all-to-all | bytes 262144 | tf_op jit(solution)/shard_map/all_to_all | solution.py:531
  180.6 8.0 %shard_map.260 = (f32[4,512,128]{2,1,0:T(8,128)S(1)}, f32[4,512,128]{2,1,0:T(8,128)S(1)}, f32[4,512,128]{2,1,0:T(8,128)S(1)}, bf16[4,1552,128]{2,1,0:T(8,128)(2,...) custom-call(s32[3]{0:T(128)S(1)} %copy-done.23, f32[32,8,128]{2,1,0:T(8,128)S(1)} %all_to_all.108.back, ...), custom_call_target="tpu_custom_call" | custom-call | tf_op jit(solution)/shard_map/pallas_call | solution.py:32
  189.6 9.1 %all_to_all.109.gathered = f32[32,4,128]{2,1,0:T(4,128)S(1)} all-to-all(f32[32,4,128]{2,1,0:T(4,128)S(1)} %get-tuple-element.81), channel_id=1, replica_groups=mesh['dp'=8,'mp'=4] {'dp','mp'}, dimensions={0} | all-to-all | bytes 131072 | tf_op jit(solution)/shard_map/all_to_all | solution.py:531
  198.7 7.8 %shard_map.261 = (f32[4,512,128]{2,1,0:T(8,128)}, f32[32,8,128]{2,1,0:T(8,128)S(1)}, bf16[4,528,128]{2,1,0:T(8,128)(2,1)S(1)}) custom-call(s32[3]{0:T(128)S(1)} %copy-done.23, f32[32,4,128]{2,1,0:T(4,128)S(1)} %all_to_all.109.gathered, f32[32,4,128]{2,1,0:T(4,128)S(1)} %all_to_all.105.mom, f32[2,16,128]{2,1,0:T(8,128)S(1)} %get-tuple-element.56.table, ...), custom_call_target="tpu_custom_call" | custom-call | tf_op jit(solution)/shard_map/pallas_call | solution.py:32
  206.5 9.9 %all_to_all.110.back = f32[32,8,128]{2,1,0:T(8,128)S(1)} all-to-all(f32[32,8,128]{2,1,0:T(8,128)S(1)} %get-tuple-element.87), channel_id=1, replica_groups=mesh['dp'=8,'mp'=4] {'dp','mp'}, dimensions={0} | all-to-all | bytes 262144 | tf_op jit(solution)/shard_map/all_to_all | solution.py:531
  216.4 17.6 %all_to_all.111 = f32[4,512,128]{2,1,0:T(8,128)} all-to-all(f32[4,512,128]{2,1,0:T(8,128)S(1)} %get-tuple-element.68), channel_id=1, replica_groups=mesh['dp'=8,'mp'=4] {'mp'}, dimensions={0} | all-to-all | bytes 2097152 | tf_op jit(solution)/shard_map/all_to_all | solution.py:535
  240.5 11.5 %all-to-all-done.12 = f32[4,512,128]{2,1,0:T(8,128)S(1)} async-done(((f32[4,512,128]{2,1,0:T(8,128)}), f32[4,512,128]{2,1,0:T(8,128)S(1)}, u32[]{:S(2)}, u32[]{:S(2)}) %all-to-all-start.12) | async-done | bytes 1048608 | tf_op jit(solution)/shard_map/all_to_all | solution.py:535
  259.4 23.2 %all-to-all-done.17 = bf16[4,2080,128]{2,1,0:T(8,128)(2,1)} async-done(((bf16[4,2080,128]{2,1,0:T(8,128)(2,1)}), bf16[4,2080,128]{2,1,0:T(8,128)(2,1)}, u32[]{:S(2)}, u32[]{:S(2)}) %all-to-all-start.17) | async-done | bytes 2129952 | tf_op jit(solution)/shard_map/all_to_all | solution.py:535
  290.1 23.1 %all-to-all-done.14 = bf16[4,2080,128]{2,1,0:T(8,128)(2,1)} async-done(((bf16[4,2080,128]{2,1,0:T(8,128)(2,1)}), bf16[4,2080,128]{2,1,0:T(8,128)(2,1)}, u32[]{:S(2)}, u32[]{:S(2)}) %all-to-all-start.14) | async-done | bytes 2129952 | tf_op jit(solution)/shard_map/all_to_all | solution.py:535
  321.5 10.4 %all-to-all-done.18 = bf16[8,272,128]{2,1,0:T(8,128)(2,1)S(1)} async-done(((bf16[8,272,128]{2,1,0:T(8,128)(2,1)}), bf16[8,272,128]{2,1,0:T(8,128)(2,1)S(1)}, u32[]{:S(2)}, u32[]{:S(2)}) %all-to-all-start.18) | async-done | bytes 557088 | tf_op jit(solution)/shard_map/all_to_all | solution.py:544
  337.4 14.2 %all-to-all-done.15 = bf16[8,272,128]{2,1,0:T(8,128)(2,1)S(1)} async-done(((bf16[8,272,128]{2,1,0:T(8,128)(2,1)}), bf16[8,272,128]{2,1,0:T(8,128)(2,1)S(1)}, u32[]{:S(2)}, u32[]{:S(2)}) %all-to-all-start.15) | async-done | bytes 557088 | tf_op jit(solution)/shard_map/all_to_all | solution.py:544
  358.7 13.0 %all-to-all-done.19 = bf16[8,272,128]{2,1,0:T(8,128)(2,1)} async-done(((bf16[8,272,128]{2,1,0:T(8,128)(2,1)}), bf16[8,272,128]{2,1,0:T(8,128)(2,1)}, u32[]{:S(2)}, u32[]{:S(2)}) %all-to-all-start.19) | async-done | bytes 557088 | tf_op jit(solution)/shard_map/all_to_all | solution.py:546
  380.0 11.4 %all-to-all-done.16 = bf16[8,272,128]{2,1,0:T(8,128)(2,1)S(1)} async-done(((bf16[8,272,128]{2,1,0:T(8,128)(2,1)}), bf16[8,272,128]{2,1,0:T(8,128)(2,1)S(1)}, u32[]{:S(2)}, u32[]{:S(2)}) %all-to-all-start.16) | async-done | bytes 557088 | tf_op jit(solution)/shard_map/all_to_all | solution.py:546
  399.9 10.8 %all-to-all-done.20 = bf16[4,2,512,128]{3,2,1,0:T(8,128)(2,1)S(1)} async-done(((bf16[4,2,512,128]{3,2,1,0:T(8,128)(2,1)}), bf16[4,2,512,128]{3,2,1,0:T(8,128)(2,1)S(1)}, u32[]{:S(2)}, u32[]{:S(2)}) %all-to-all-start.20) | async-done | bytes 1048608 | tf_op jit(solution)/shard_map/all_to_all | solution.py:535
  (149 shorter events, 120.7 us)
Async XLA Ops:
  3.7 79.9 %copy-start.21 = (s32[3]{0:T(128)}, s32[3]{0:T(128)S(1)}, u32[]{:S(2)}) copy-start(s32[3]{0:T(128)S(1)} %pad_add_fusion.scal) | copy-start | bytes 40
  7.0 19.9 %copy-start.34 = (bf16[2,512,128]{2,1,0:T(8,128)(2,1)S(1)}, bf16[2,512,128]{2,1,0:T(8,128)(2,1)}, u32[]{:S(2)}) copy-start(bf16[2,512,128]{2,1,0:T(8,128)(2,1)} %param.24) | copy-start | bytes 786436
  7.0 19.9 %copy-start.35 = (bf16[2,512,128]{2,1,0:T(8,128)(2,1)S(1)}, bf16[2,512,128]{2,1,0:T(8,128)(2,1)}, u32[]{:S(2)}) copy-start(bf16[2,512,128]{2,1,0:T(8,128)(2,1)} %param.26) | copy-start | bytes 786436
  7.0 34.7 %copy-start.3 = (bf16[2,512,512]{2,1,0:T(8,128)(2,1)S(1)}, bf16[2,512,512]{2,1,0:T(8,128)(2,1)}, u32[]{:S(2)}) copy-start(bf16[2,512,512]{2,1,0:T(8,128)(2,1)} %weight.7) | copy-start | bytes 3145732
  23.4 18.3 %all-to-all-start = ((f32[4,528,128]{2,1,0:T(8,128)}), f32[4,528,128]{2,1,0:T(8,128)S(1)}, u32[]{:S(2)}, u32[]{:S(2)}) async-start(f32[4,528,128]{2,1,0:T(8,128)} %get-tuple-element.54), calls=%async_computation | async-start | bytes 2162688 | tf_op jit(solution)/shard_map/all_to_all | solution.py:535
  26.9 20.7 %copy-start.33 = (bf16[2,512,128]{2,1,0:T(8,128)(2,1)S(1)}, bf16[2,512,128]{2,1,0:T(8,128)(2,1)}, u32[]{:S(2)}) copy-start(bf16[2,512,128]{2,1,0:T(8,128)(2,1)} %param.27) | copy-start | bytes 786436
  45.0 10.0 %all-to-all-start.2 = ((f32[32,4,128]{2,1,0:T(4,128)}), f32[32,4,128]{2,1,0:T(4,128)S(1)}, u32[]{:S(2)}, u32[]{:S(2)}) async-start(f32[32,4,128]{2,1,0:T(4,128)} %get-tuple-element.57), calls=%async_computation.2 | async-start | bytes 131072 | tf_op jit(solution)/shard_map/all_to_all | solution.py:531
  78.6 18.0 %all-to-all-start.7 = ((f32[4,512,128]{2,1,0:T(8,128)}), f32[4,512,128]{2,1,0:T(8,128)S(1)}, u32[]{:S(2)}, u32[]{:S(2)}) async-start(f32[4,512,128]{2,1,0:T(8,128)} %bitcast.86), calls=%async_computation.7 | async-start | bytes 2097152 | tf_op jit(solution)/shard_map/all_to_all | solution.py:535
  96.5 10.8 %all-to-all-start.4 = ((f32[32,8,128]{2,1,0:T(8,128)}), f32[32,8,128]{2,1,0:T(8,128)S(1)}, u32[]{:S(2)}, u32[]{:S(2)}) async-start(f32[32,8,128]{2,1,0:T(8,128)} %get-tuple-element.63), calls=%async_computation.4 | async-start | bytes 262144 | tf_op jit(solution)/shard_map/all_to_all | solution.py:531
  109.8 24.5 %all-to-all-start.6 = ((bf16[4,3,512,128]{3,2,1,0:T(8,128)(2,1)}), bf16[4,3,512,128]{3,2,1,0:T(8,128)(2,1)}, u32[]{:S(2)}, u32[]{:S(2)}) async-start(bf16[4,3,512,128]{3,2,1,0:T(8,128)(2,1)} %broadcast_in_dim.14), calls=%async_computation.6 | async-start | bytes 3145728 | tf_op jit(solution)/shard_map/all_to_all | solution.py:535
  134.3 10.0 %all-to-all-start.5 = ((f32[32,4,128]{2,1,0:T(4,128)}), f32[32,4,128]{2,1,0:T(4,128)S(1)}, u32[]{:S(2)}, u32[]{:S(2)}) async-start(f32[32,4,128]{2,1,0:T(4,128)} %get-tuple-element.64), calls=%async_computation.5 | async-start | bytes 131072 | tf_op jit(solution)/shard_map/all_to_all | solution.py:531
  144.3 19.8 %copy-start.2 = (f32[4,512,128]{2,1,0:T(8,128)S(1)}, f32[4,512,128]{2,1,0:T(8,128)}, u32[]{:S(2)}) copy-start(f32[4,512,128]{2,1,0:T(8,128)} %get-tuple-element.62.h.h1) | copy-start | bytes 3145732
  144.3 19.8 %copy-start.13 = (f32[4,512,128]{2,1,0:T(8,128)S(1)}, f32[4,512,128]{2,1,0:T(8,128)}, u32[]{:S(2)}) copy-start(f32[4,512,128]{2,1,0:T(8,128)} %copy-done.12) | copy-start | bytes 3145732
  180.6 18.0 %copy-start.9 = (f32[4,512,128]{2,1,0:T(8,128)S(1)}, f32[4,512,128]{2,1,0:T(8,128)}, u32[]{:S(2)}) copy-start(f32[4,512,128]{2,1,0:T(8,128)} %copy-done.8) | copy-start | bytes 3145732
  180.6 18.0 %copy-start.11 = (f32[4,512,128]{2,1,0:T(8,128)S(1)}, f32[4,512,128]{2,1,0:T(8,128)}, u32[]{:S(2)}) copy-start(f32[4,512,128]{2,1,0:T(8,128)} %copy-done.10) | copy-start | bytes 3145732
  234.0 18.0 %all-to-all-start.12 = ((f32[4,512,128]{2,1,0:T(8,128)}), f32[4,512,128]{2,1,0:T(8,128)S(1)}, u32[]{:S(2)}, u32[]{:S(2)}) async-start(f32[4,512,128]{2,1,0:T(8,128)} %get-tuple-element.86), calls=%async_computation.12 | async-start | bytes 2097152 | tf_op jit(solution)/shard_map/all_to_all | solution.py:535
  252.0 30.6 %all-to-all-start.17 = ((bf16[4,2080,128]{2,1,0:T(8,128)(2,1)}), bf16[4,2080,128]{2,1,0:T(8,128)(2,1)}, u32[]{:S(2)}, u32[]{:S(2)}) async-start(bf16[4,2080,128]{2,1,0:T(8,128)(2,1)} %pad_maximum_fusion.1), calls=%async_computation.17 | async-start | bytes 4259840 | tf_op jit(solution)/shard_map/all_to_all | solution.py:535
  282.6 30.6 %all-to-all-start.14 = ((bf16[4,2080,128]{2,1,0:T(8,128)(2,1)}), bf16[4,2080,128]{2,1,0:T(8,128)(2,1)}, u32[]{:S(2)}, u32[]{:S(2)}) async-start(bf16[4,2080,128]{2,1,0:T(8,128)(2,1)} %pad_maximum_fusion), calls=%async_computation.14 | async-start | bytes 4259840 | tf_op jit(solution)/shard_map/all_to_all | solution.py:535
  313.1 18.7 %all-to-all-start.18 = ((bf16[8,272,128]{2,1,0:T(8,128)(2,1)}), bf16[8,272,128]{2,1,0:T(8,128)(2,1)S(1)}, u32[]{:S(2)}, u32[]{:S(2)}) async-start(bf16[8,272,128]{2,1,0:T(8,128)(2,1)} %bitcast.17), calls=%async_computation.18 | async-start | bytes 1114112 | tf_op jit(solution)/shard_map/all_to_all | solution.py:544
  319.5 37.3 %copy-start.7 = (f32[2048,128]{1,0:T(8,128)S(1)}, f32[2048,128]{1,0:T(8,128)}, u32[]{:S(2)}) copy-start(f32[2048,128]{1,0:T(8,128)} %stream.3) | copy-start | bytes 3145732
  332.7 19.0 %all-to-all-start.15 = ((bf16[8,272,128]{2,1,0:T(8,128)(2,1)}), bf16[8,272,128]{2,1,0:T(8,128)(2,1)S(1)}, u32[]{:S(2)}, u32[]{:S(2)}) async-start(bf16[8,272,128]{2,1,0:T(8,128)(2,1)} %bitcast.82), calls=%async_computation.15 | async-start | bytes 1114112 | tf_op jit(solution)/shard_map/all_to_all | solution.py:544
  352.6 19.2 %all-to-all-start.19 = ((bf16[8,272,128]{2,1,0:T(8,128)(2,1)}), bf16[8,272,128]{2,1,0:T(8,128)(2,1)}, u32[]{:S(2)}, u32[]{:S(2)}) async-start(bf16[8,272,128]{2,1,0:T(8,128)(2,1)} %broadcast_in_dim.16), calls=%async_computation.19 | async-start | bytes 1114112 | tf_op jit(solution)/shard_map/all_to_all | solution.py:546
  372.6 18.9 %all-to-all-start.16 = ((bf16[8,272,128]{2,1,0:T(8,128)(2,1)}), bf16[8,272,128]{2,1,0:T(8,128)(2,1)S(1)}, u32[]{:S(2)}, u32[]{:S(2)}) async-start(bf16[8,272,128]{2,1,0:T(8,128)(2,1)} %broadcast_in_dim.15), calls=%async_computation.16 | async-start | bytes 1114112 | tf_op jit(solution)/shard_map/all_to_all | solution.py:546
  392.8 18.0 %all-to-all-start.20 = ((bf16[4,2,512,128]{3,2,1,0:T(8,128)(2,1)}), bf16[4,2,512,128]{3,2,1,0:T(8,128)(2,1)S(1)}, u32[]{:S(2)}, u32[]{:S(2)}) async-start(bf16[4,2,512,128]{3,2,1,0:T(8,128)(2,1)} %broadcast_in_dim.17), calls=%async_computation.20 | async-start | bytes 2097152 | tf_op jit(solution)/shard_map/all_to_all | solution.py:535
  (27 other events, 132.4 us)

commit v2 on v1

v2 whole, which is shorter than its diff:
```python
import functools

import jax
import jax.numpy as jnp
from jax import lax
from jax.experimental import pallas as pl
from jax.experimental.pallas import tpu as pltpu
from jax.sharding import PartitionSpec as P

epsilon = 1e-05
LANES = 128
SUB = 8
ROOT = 0.7978845608028654
CUBE = 0.044715
AXES = ("dp", "mp")
F32 = jnp.float32
BF16 = jnp.bfloat16
NT = (((1,), (1,)), ((), ()))
TN = (((0,), (0,)), ((), ()))
GAIN, SHIFT, SKIP, VBIAS, GBIAS = range(5)
PARAMS = 5


class Copies:
    def __init__(self, sems):
        self.sems, self.used, self.open = sems, 0, []

    def start(self, src, dst):
        copy = pltpu.make_async_copy(src, dst, self.sems.at[self.used])
        self.used += 1
        copy.start()
        return copy

    def flush(self, src, dst):
        self.open.append(self.start(src, dst))

    def finish(self):
        for copy in self.open:
            copy.wait()
        self.open = []


def along(ref, part, parts):
    if parts == 1:
        return ref
    axis = len(ref.shape) - 2
    size = ref.shape[axis] // parts
    at = pl.ds(part * size, size)
    return ref.at[at] if axis == 0 else ref.at[:, at]


class Arrival:
    def __init__(self, copies, src, dst, parts):
        self.copies, self.src, self.dst, self.parts = copies, src, dst, parts
        self.waits = [None] * parts

    def begin(self, part):
        src, dst = (along(r, part, self.parts) for r in (self.src, self.dst))
        self.waits[part] = self.copies.start(src, dst)

    def part(self, part):
        if self.waits[part] is not None:
            self.waits[part].wait()
            self.waits[part] = None
        return self.dst

    def __call__(self):
        for part in range(self.parts):
            self.part(part)
        return self.dst


class Result:
    def __init__(self, copies, ref, dst):
        self.copies, self.ref, self.dst, self.sent = copies, ref, dst, False

    def flush(self, part=0, parts=1):
        self.sent = True
        self.copies.flush(along(self.ref, part, parts), along(self.dst, part, parts))


class Raw:
    def __init__(self, array):
        self.array = array


class Halves:
    def __init__(self, array):
        self.array = array


class Near:
    def __init__(self, array):
        self.array = array


class Here:
    def __init__(self, ref):
        self.ref = self.dst = ref

    def part(self, part):
        return self.ref

    def __call__(self):
        return self.ref

    def flush(self, part=0, parts=1):
        pass


def call(body, outs, scratch, *args, scalars=0):
    wraps = (Raw, Halves, Near)
    plain = [a.array if isinstance(a, wraps) else a for a in args]
    out_shapes = [o.array if isinstance(o, wraps) else o for o in outs]
    autos = [i for i, a in enumerate(args) if i >= scalars and not isinstance(a, (Raw, Near))]
    made = [i for i, o in enumerate(outs) if not isinstance(o, (Raw, Near))]
    rooms = [pltpu.VMEM(plain[i].shape, plain[i].dtype) for i in autos]
    rooms += [pltpu.VMEM(out_shapes[i].shape, out_shapes[i].dtype) for i in made]

    def kernel(*refs):
        ins, refs = refs[: len(args)], refs[len(args) :]
        dsts, refs = refs[: len(outs)], refs[len(outs) :]
        sems, refs = refs[0], refs[1:]
        vin, refs = refs[: len(autos)], refs[len(autos) :]
        vout, rest = refs[: len(made)], refs[len(made) :]
        copies = Copies(sems)
        operands = [Here(r) if isinstance(a, Near) else r for a, r in zip(args, ins, strict=True)]
        for i, room in zip(autos, vin, strict=True):
            parts = 2 if isinstance(args[i], Halves) else 1
            operands[i] = Arrival(copies, ins[i], room, parts)
        results = [Here(r) if isinstance(o, Near) else r for o, r in zip(outs, dsts, strict=True)]
        for i, room in zip(made, vout, strict=True):
            results[i] = Result(copies, room, dsts[i])

        def begin():
            for part in range(2):
                for i in autos:
                    if part < operands[i].parts:
                        operands[i].begin(part)

        body(copies, begin, *operands, *results, *rest)
        for r in results:
            if isinstance(r, Result) and not r.sent:
                r.flush()
        copies.finish()
        used.append(copies.used)

    near = pl.BlockSpec(memory_space=pltpu.VMEM)
    far = pl.BlockSpec(memory_space=pltpu.HBM)
    plain[scalars:] = [
        a if isinstance(w, Near) else pltpu.with_memory_space_constraint(a, pltpu.HBM)
        for w, a in zip(args[scalars:], plain[scalars:], strict=True)
    ]
    used = []

    def made_call(count):
        return pl.pallas_call(
            kernel,
            out_shape=[
                s if isinstance(o, Near) else pltpu.HBM(s.shape, s.dtype)
                for o, s in zip(outs, out_shapes, strict=True)
            ],
            in_specs=[pl.BlockSpec(memory_space=pltpu.SMEM)] * scalars
            + [near if isinstance(a, Near) else far for a in args[scalars:]],
            out_specs=[near if isinstance(o, Near) else far for o in outs],
            scratch_shapes=[pltpu.SemaphoreType.DMA((count,))] + rooms + list(scratch),
            compiler_params=pltpu.CompilerParams(vmem_limit_bytes=32 * 1024 * 1024),
        )

    jax.eval_shape(made_call(128), *plain)
    return made_call(max(used[0], 1))(*plain)


def cat(ref, rows):
    return jnp.concatenate([ref[j, rows, :] for j in range(ref.shape[0])], axis=1)


def put(ref, rows, val):
    for j in range(ref.shape[0]):
        ref[j, rows, :] = val[:, j * LANES : (j + 1) * LANES].astype(ref.dtype)


def rowcat(ref, r):
    return jnp.concatenate([ref[j, r : r + 1, :] for j in range(ref.shape[0])], axis=1)


def lanes(rows):
    return jnp.concatenate([rows[j : j + 1, :] for j in range(rows.shape[0])], axis=1)


def dot(a, b):
    return jnp.dot(a, b, preferred_element_type=F32)


def dot_nt(a, b):
    return lax.dot_general(a, b, NT, preferred_element_type=F32)


def dot_tn(a, b):
    return lax.dot_general(a, b, TN, preferred_element_type=F32)


def chunks(rows, count):
    size = rows // count
    return [slice(i * size, (i + 1) * size) for i in range(count)]


def sweep(src, dst, table, init, reset, reverse, conj, extra=None):
    halves = src.shape[0] // 2
    span = src.shape[1] // SUB
    rate_re = [jnp.broadcast_to(table[h : h + 1, :], (SUB, LANES)) for h in range(halves)]
    rate_im = [
        jnp.broadcast_to(table[halves + h : halves + h + 1, :], (SUB, LANES))
        for h in range(halves)
    ]
    if conj:
        rate_im = [-r for r in rate_im]
    base = lax.broadcasted_iota(jnp.int32, (SUB, LANES), 0) * span - reset

    def body(step, carry):
        j = span - 1 - step if reverse else step
        state, sums = carry
        drop = base == -j
        at = pl.ds(j, SUB, stride=span)
        new_re, new_im = [], []
        for h in range(halves):
            a = jnp.where(drop, 0.0, rate_re[h])
            b = jnp.where(drop, 0.0, rate_im[h])
            re, im = state[h], state[halves + h]
            new_re.append((src[h, at, :] + a * re) - b * im)
            new_im.append((src[halves + h, at, :] + a * im) + b * re)
        state = tuple(new_re + new_im)
        if dst is not None:
            for k in range(2 * halves):
                dst[k, at, :] = state[k]
        if extra is not None:
            sums = extra(at, state, sums)
        return state, sums

    sums = ()
    if extra is not None:
        sums = tuple(jnp.zeros((SUB, LANES), F32) for _ in range(2 * halves))
    return lax.fori_loop(0, span, body, (init, sums), unroll=8)


def zeros_state(halves):
    return tuple(jnp.zeros((SUB, LANES), F32) for _ in range(2 * halves))


def chain_segments(ends, first, table, reset, span, reverse, conj):
    halves = len(ends) // 2
    power_re = [table[4 + h : 5 + h, :] for h in range(halves)]
    power_im = [table[6 + h : 7 + h, :] for h in range(halves)]
    if conj:
        power_im = [-r for r in power_im]
    state = list(first)
    incoming = [[None] * SUB for _ in ends]
    order = range(SUB - 1, -1, -1) if reverse else range(SUB)
    for k in order:
        inside = (reset >= k * span) & (reset < (k + 1) * span)
        keep = jnp.where(inside, 0.0, 1.0)
        new = [None] * len(ends)
        for h in range(halves):
            re, im = state[h], state[halves + h]
            incoming[h][k], incoming[halves + h][k] = re, im
            new[h] = keep * (power_re[h] * re - power_im[h] * im) + ends[h][k : k + 1, :]
            new[halves + h] = (
                keep * (power_re[h] * im + power_im[h] * re) + ends[halves + h][k : k + 1, :]
            )
        state = new
    return [jnp.concatenate(rows, axis=0) for rows in incoming], state


def zero_rows(halves):
    return [jnp.zeros((1, LANES), F32) for _ in range(2 * halves)]


def emit_ends(out, ends_out, ends, table, reset, span, reverse, conj):
    halves = len(ends) // 2
    _, last = chain_segments(ends, zero_rows(halves), table, reset, span, reverse, conj)
    tile = jnp.concatenate(last, axis=0)
    out.ref[...] = jnp.broadcast_to(tile[None], out.ref.shape)
    out.flush()
    for k in range(2 * halves):
        ends_out.ref[k, :, :] = ends[k]
    ends_out.flush()


def carried_in(gathered, moments, table, me, reverse, conj):
    count = gathered.shape[0]
    power_re = table[8:10, :]
    power_im = table[10:12, :]
    if conj:
        power_im = -power_im
    flag = 3 if reverse else 2

    def body(i, state):
        d = count - 1 - i if reverse else i
        re, im = state
        keep = moments[d, flag : flag + 1, :]
        tile = gathered[d]
        return (
            keep * (power_re * re - power_im * im) + tile[0:2, :],
            keep * (power_re * im + power_im * re) + tile[2:4, :],
        )

    zero = jnp.zeros((2, LANES), F32)
    re, im = lax.fori_loop(0, count - 1 - me if reverse else me, body, (zero, zero))
    return [re[0:1, :], re[1:2, :], im[0:1, :], im[1:2, :]]


def place():
    mp = lax.axis_index("mp")
    return mp, lax.axis_index("dp") * lax.axis_size("mp") + mp


def local_resets(start, rows):
    offset = start[0]
    shift = jnp.where(offset > 0, offset - lax.axis_index("mp") * rows, -(1 << 20))
    return shift, shift - 1


def first_kernel(rows, copies, begin, start, stream, gain, shift, skip, vbias, gbias, decay, phase, scale,
                 moments, table_out, send1, send2, send3, held):
    mp, _ = place()
    total, width = held.shape
    parts = total // rows
    arrive = [copies.start(along(stream, i, parts), along(held, i, parts)) for i in range(parts)]
    begin()
    size = 128
    one = two = jnp.zeros((SUB, LANES), F32)

    def body(i, carry):
        one, two = carry
        x = held[pl.ds(i * size, size), :]
        for g in range(0, size, SUB):
            piece = x[g : g + SUB, :]
            one = one + piece
            two = two + piece * piece
        return one, two

    for i in range(parts):
        arrive[i].wait()
        one, two = lax.fori_loop(i * rows // size, (i + 1) * rows // size, body, (one, two))
    fwd, bwd = local_resets(start, rows)
    keep_f = jnp.where((fwd >= 0) & (fwd < rows), 0.0, 1.0)
    keep_b = jnp.where((bwd >= 0) & (bwd < rows), 0.0, 1.0)
    tile = jnp.concatenate(
        [
            jnp.sum(one, axis=0, keepdims=True),
            jnp.sum(two, axis=0, keepdims=True),
            jnp.full((1, LANES), keep_f, F32),
            jnp.full((1, LANES), keep_b, F32),
        ],
        axis=0,
    )
    moments.ref[...] = jnp.broadcast_to(tile[None], moments.ref.shape)
    moments.flush()
    gain, shift, skip, vbias, gbias = (a() for a in (gain, shift, skip, vbias, gbias))
    decay, phase, scale = decay(), phase(), scale()
    layers = decay.shape[0]
    plist = jnp.concatenate(
        [a[l : l + 1, :] for l in range(layers) for a in (gain, shift, skip, vbias, gbias)]
        + [jnp.zeros((16 - PARAMS * layers, width), F32)],
        axis=0,
    )
    high = plist.astype(BF16)
    rest = (plist - high.astype(F32)).astype(BF16)
    for k, send in ((1, send1), (2, send2), (3, send3)):
        base = (mp ^ k) * rows
        send.ref[0:rows, :] = held[pl.ds(pl.multiple_of(base, SUB), rows), :].astype(BF16)
        send.ref[rows : rows + 16, :] = high
        send.ref[rows + 16 : rows + 32, :] = rest
        send.flush()
    span = rows // SUB
    table = table_out.ref
    for layer in range(layers):
        for h in range(2):
            cols = slice(h * LANES, (h + 1) * LANES)
            radius = jnp.exp(-jnp.exp(decay[layer : layer + 1, cols]))
            angle = jnp.exp(phase[layer : layer + 1, cols])
            re, im = radius * jnp.cos(angle), radius * jnp.sin(angle)
            table[layer, h : h + 1, :] = re
            table[layer, 2 + h : 3 + h, :] = im
            length = 1
            while length < rows:
                re, im = re * re - im * im, 2.0 * re * im
                length *= 2
                if length == span:
                    table[layer, 4 + h : 5 + h, :] = re
                    table[layer, 6 + h : 7 + h, :] = im
            table[layer, 8 + h : 9 + h, :] = re
            table[layer, 10 + h : 11 + h, :] = im
            table[layer, 12 + h : 13 + h, :] = jnp.exp(scale[layer : layer + 1, cols])
            table[layer, 14 + h : 15 + h, :] = jnp.zeros((1, LANES), F32)


def pack_maps(layers, copies, begin, c_own, v_own, g_own, *packs):
    begin()
    for layer in range(layers):
        for i, own in enumerate((c_own, v_own, g_own)):
            deep = own().shape[1]
            packs[layer].ref[i * deep : (i + 1) * deep, :] = own()[layer]
        packs[layer].flush()


def pack_block(copies, begin, x, *sends):
    mp, _ = place()
    rows = sends[0].ref.shape[0]
    begin()
    whole = x()
    for k, send in enumerate(sends):
        base = pl.multiple_of((mp ^ (k + 1)) * rows, SUB)
        send.ref[...] = whole[pl.ds(base, rows), :].astype(BF16)
        send.flush()


def gather_block(copies, begin, got1, got2, got3, gain, shift, skip, vbias, gbias, stream, h, prm, held):
    mp, _ = place()
    rows = h.ref.shape[1]
    own = Later(copies, [(own_rows(stream, rows), held)], held)
    begin()
    plist = [a() for a in (gain, shift, skip, vbias, gbias)]
    layers = plist[0].shape[0]
    for k, got in ((1, got1), (2, got2), (3, got3)):
        got = got()
        h.ref[mp ^ k, :, :] = got[0:rows, :].astype(F32)
        pair = got[rows : rows + 16, :].astype(F32) + got[rows + 16 : rows + 32, :].astype(F32)
        prm.ref[mp ^ k, :, :] = pair
    mine = [a[l : l + 1, :] for l in range(layers) for a in plist]
    prm.ref[mp, 0 : PARAMS * layers, :] = jnp.concatenate(mine, axis=0)
    prm.ref[mp, PARAMS * layers :, :] = jnp.zeros((16 - PARAMS * layers, LANES), F32)
    h.ref[mp, :, :] = own()[...]


def norm_rows(mean, second, gain, shift):
    inverse = lax.rsqrt(second - mean * mean + epsilon)
    factor = inverse * gain
    return inverse, factor, shift - mean * factor


def drive_body(layer, mean, second, start, h, prm, table, weight, drive, norms, out, ends_out, slow):
    rows = drive.ref.shape[1]
    reverse = layer % 2 == 1
    base = layer * PARAMS
    inverse, factor, bias = norm_rows(
        mean, second, rowcat(prm, base + GAIN), rowcat(prm, base + SHIFT)
    )
    norms.ref[...] = jnp.concatenate(
        [factor, bias, inverse, mean] + [jnp.zeros_like(mean)] * 4, axis=0
    )
    norms.flush()
    gamma = lanes(table[layer, 12:14, :])
    gamma = jnp.concatenate([gamma, gamma], axis=1)
    for i, at in enumerate(chunks(rows, 2)):
        low = (cat(h, at) * factor + bias).astype(BF16)
        slow.ref[at, :] = low
        slow.flush(i, 2)
        put(drive.ref, at, dot(low, weight()[...]) * gamma)
        drive.flush(i, 2)
    fwd, bwd = local_resets(start, rows)
    reset = bwd if reverse else fwd
    ends, _ = sweep(drive.ref, None, table[layer], zeros_state(2), reset, reverse, False)
    emit_ends(out, ends_out, ends, table[layer], reset, rows // SUB, reverse, False)


class Later:
    def __init__(self, copies, pairs, dst):
        self.waits, self.dst = [copies.start(src, to) for src, to in pairs], dst

    def __call__(self):
        for copy in self.waits:
            copy.wait()
        self.waits = []
        return self.dst


def own_rows(ref, rows, k=0):
    mp, _ = place()
    return ref.at[pl.ds(pl.multiple_of((mp ^ k) * rows, SUB), rows)]


def total_of(gathered):
    tile = gathered[0]
    for d in range(1, gathered.shape[0]):
        tile = tile + gathered[d]
    return tile


def drive_first(total_tokens, copies, begin, start, mom, table, h, prm, weight, drive, norms, out, ends, slow, maps):
    weight = Later(copies, [(weight.at[0], maps)], maps)
    mom = mom()
    groups = h.ref.shape[0]
    sums = [mom[j, 0:2, :] for j in range(groups)]
    for d in range(groups, mom.shape[0]):
        sums[d % groups] = sums[d % groups] + mom[d, 0:2, :]
    both = jnp.concatenate(sums, axis=1) * (1.0 / total_tokens)
    drive_body(0, both[0:1, :], both[1:2, :], start, h(), prm(), table(), weight, drive, norms, out, ends, slow)


def drive_next(layer, total_tokens, copies, begin, start, mom, prm, table, h, weight, drive, norms, out, ends, slow, maps):
    weight = Later(copies, [(weight.at[layer], maps)], maps)
    tile = total_of(mom()) * (1.0 / total_tokens)
    half = tile.shape[0] // 2
    mean, second = lanes(tile[:half]), lanes(tile[half:])
    drive_body(layer, mean, second, start, h(), prm(), table(), weight, drive, norms, out, ends, slow)


def resume(start, rows, gathered, mom, tab, ends, reverse, conj):
    fwd, bwd = local_resets(start, rows)
    reset = bwd if reverse else fwd
    first = carried_in(gathered, mom, tab, place()[1], reverse, conj)
    incoming, _ = chain_segments(
        [ends[k] for k in range(4)], first, tab, reset, rows // SUB, reverse, conj
    )
    return tuple(incoming), reset


def assemble(copies, begin, p0, p1, p2, p3, maps):
    begin()
    mp, _ = place()
    count, deep = maps.ref.shape[0], maps.ref.shape[1]
    for k, piece in enumerate((p0, p1, p2, p3)):
        cols = pl.ds(pl.multiple_of((mp ^ k) * LANES, LANES), LANES)
        for i in range(count):
            maps.ref[i, :, cols] = piece()[i * deep : (i + 1) * deep, :]


def fetch_maps(copies, far, near, order=(0, 1, 2)):
    return {i: Later(copies, [(far.at[i], near.at[i])], near.at[i]) for i in order}


def mix_chunk(layer, at, h, norms, states, maps, prm):
    base = layer * PARAMS
    x = cat(h, at)
    scaled = x * norms[0:1, :] + norms[1:2, :]
    states_low = cat(states, at).astype(BF16)
    mixed = dot(states_low, maps[0]()[...]) + rowcat(prm, base + SKIP) * scaled
    square = mixed * mixed
    wave = jnp.tanh(ROOT * mixed * (1.0 + CUBE * square))
    half = 0.5 * (1.0 + wave)
    sent_low = (mixed * half).astype(BF16)
    slope = half + 0.5 * mixed * (1.0 - wave * wave) * (ROOT * (1.0 + 3.0 * CUBE * square))
    value = dot(sent_low, maps[1]()[...]) + rowcat(prm, base + VBIAS)
    gate = dot(sent_low, maps[2]()[...]) + rowcat(prm, base + GBIAS)
    sig = 0.5 + 0.5 * jnp.tanh(0.5 * gate)
    gated = value * sig
    return x, scaled, states_low, sent_low, slope, sig, gated


def back_chunk(i, at, g, sig, gain_part, scaled, slope, maps, outs, sums):
    dv, dg, dml, ds = outs
    dvalue = g * sig
    dgate = g * gain_part
    dv_low, dg_low = dvalue.astype(BF16), dgate.astype(BF16)
    dmixed = (dot_nt(dv_low, maps[1]()[...]) + dot_nt(dg_low, maps[2]()[...])) * slope()
    dm_low = dmixed.astype(BF16)
    put(ds.ref, at, dot_nt(dm_low, maps[0]()[...]))
    dv.ref[at, :] = dv_low
    dg.ref[at, :] = dg_low
    dml.ref[at, :] = dm_low
    for o in outs:
        o.flush(i, 2)
    add = lambda v: jnp.sum(v, axis=0, keepdims=True)
    return [
        s + n for s, n in zip(sums, [add(dvalue), add(dgate), add(dmixed * scaled())], strict=True)
    ]


def sums_rows(sums_out, sums):
    rows = sums + [jnp.zeros_like(sums[0])] * (8 - len(sums))
    sums_out.ref[...] = jnp.concatenate(rows, axis=0)
    sums_out.flush()


def share_out(keep, send, pack, copies):
    mp, _ = place()
    for ref, i, k in ((send, 0, 1), (send, 1, 3), (keep, 0, 0), (keep, 1, 2)):
        ref.ref[i, :, :] = pack[mp ^ k, :, :]


def weight_grads(copies, begin, sent, dv, dg, states, dml, sums, keep, send, pack):
    begin()
    width = sent.dst.shape[1]
    parts = pack.shape[0]
    both = jnp.concatenate([dv()[...], dg()[...]], axis=1)
    both = dot_tn(sent()[...], both)
    put(pack, slice(0, width), both[:, :width])
    put(pack, slice(width, 2 * width), both[:, width:])
    put(pack, slice(2 * width, 3 * width), dot_tn(states()[...], dml()[...]))
    sums = sums()
    for j in range(parts):
        cols = slice(j * LANES, (j + 1) * LANES)
        rows = jnp.concatenate([sums[:, cols], jnp.zeros((8, LANES), F32)], axis=0)
        pack[j, 3 * width : 3 * width + 16, :] = rows.astype(pack.dtype)
    share_out(keep, send, pack, copies)


def input_grads(layer, copies, begin, slow, dlow, prods, weight, keep, send, pack, held, maps):
    begin()
    weight = Later(copies, [(weight.at[layer], maps)], maps)
    width = slow.dst.shape[1]
    held[...] = dot_tn(slow()[...], dlow()[...])
    half = width // 2
    y_re = y_im = jnp.zeros((1, half), F32)
    size = 64
    for top in range(0, width, size):
        rows = slice(top, top + size)
        grad = held[rows, :]
        put(pack, rows, grad)
        grad_re, grad_im = grad[:, :half], grad[:, half:]
        w = weight()[rows, :].astype(F32)
        w_re, w_im = w[:, :half], w[:, half:]
        y_re = y_re + jnp.sum(grad_re * w_re + grad_im * w_im, axis=0, keepdims=True)
        y_im = y_im + jnp.sum(grad_im * w_re - grad_re * w_im, axis=0, keepdims=True)
    prods = prods()
    rows = []
    for h in range(2):
        cols = slice(h * LANES, (h + 1) * LANES)
        rows += [prods[2 * h : 2 * h + 1, :] - y_re[:, cols], prods[2 * h + 1 : 2 * h + 2, :] - y_im[:, cols]]
        rows += [y_re[:, cols]]
    tile = jnp.concatenate(rows + [jnp.zeros((10, LANES), F32)], axis=0).astype(pack.dtype)
    for j in range(pack.shape[0]):
        pack[j, width : width + 16, :] = tile
    share_out(keep, send, pack, copies)


def add_chunk(mom, one, two):
    tile = jnp.concatenate(
        [one[:, j * LANES : (j + 1) * LANES] for j in range(one.shape[1] // LANES)]
        + [two[:, j * LANES : (j + 1) * LANES] for j in range(two.shape[1] // LANES)],
        axis=0,
    )
    mom.ref[...] = jnp.broadcast_to(tile[None], mom.ref.shape)
    mom.flush()


def mix_first(layer, copies, begin, start, gathered, mom, table, ends, norms, prm, drive, h, far_maps,
              new_h, new_mom, h_far, states_low_out, sent, slope_out, sig_out, part_out, states, maps):
    rows = states.shape[1]
    ready = fetch_maps(copies, far_maps, maps)
    copies.flush(h.ref, h_far)
    reverse = layer % 2 == 1
    tab = table()[layer]
    init, reset = resume(start, rows, gathered(), mom(), tab, ends(), reverse, False)
    sweep(drive(), states, tab, init, reset, reverse, False)
    norms, prm = norms(), prm()
    one = two = 0.0
    for i, at in enumerate(chunks(rows, 2)):
        x, scaled, states_low, sent_low, slope, sig, gated = mix_chunk(
            layer, at, h(), norms, states, ready, prm
        )
        states_low_out.ref[at, :] = states_low
        sent.ref[at, :] = sent_low
        put(slope_out.ref, at, slope)
        put(sig_out.ref, at, sig)
        put(part_out.ref, at, gated * (1.0 - sig))
        new = x + gated
        put(new_h.ref, at, new)
        one = one + jnp.sum(new, axis=0, keepdims=True)
        two = two + jnp.sum(new * new, axis=0, keepdims=True)
        for o in (states_low_out, sent, slope_out, sig_out, part_out):
            o.flush(i, 2)
    add_chunk(new_mom, one, two)


def turn(layer, copies, begin, start, gathered, mom, table, ends, norms, prm, drive, h, far_maps,
         got1, got2, got3, cot,
         ds, out, ends_out, h_far, states_low_out, full_cot, sent, dv, dg, dml, sums_out, r0, r1, r2, r3,
         maps, states, new_h, cot_blocks):
    mp, _ = place()
    rows = states.shape[1]
    ready = fetch_maps(copies, far_maps, maps)
    own_cot = Later(copies, [(own_rows(cot, rows), cot_blocks.at[mp])], cot_blocks)
    copies.flush(h.ref, h_far)
    reverse = layer % 2 == 1
    tab = table()[layer]
    init, reset = resume(start, rows, gathered(), mom(), tab, ends(), reverse, False)
    sweep(drive(), states, tab, init, reset, reverse, False)
    for k, got in ((1, got1), (2, got2), (3, got3)):
        cot_blocks[mp ^ k, :, :] = got()[...].astype(F32)
    own_cot()
    norms, prm = norms(), prm()
    sums = [0.0, 0.0, 0.0]
    for i, at in enumerate(chunks(rows, 2)):
        x, scaled, states_low, sent_low, slope, sig, gated = mix_chunk(
            layer, at, h(), norms, states, ready, prm
        )
        states_low_out.ref[at, :] = states_low
        sent.ref[at, :] = sent_low
        put(new_h, at, x + gated)
        g = cat(cot_blocks, at)
        full_cot.ref[at, :] = g.astype(BF16)
        for o in (states_low_out, sent, full_cot):
            o.flush(i, 2)
        sums = back_chunk(i, at, g, sig, gated * (1.0 - sig), lambda: scaled, lambda: slope,
                          ready, (dv, dg, dml, ds), sums)
    sums_rows(sums_out, sums)
    for k, r in enumerate((r0, r1, r2, r3)):
        r.ref[...] = new_h[mp ^ k, :, :].astype(r.ref.dtype)
        r.flush()
    adjoint_start(layer, start, tab, ds.ref, out, ends_out)


def adjoint_start(layer, start, tab, ds, out, ends_out):
    rows = ds.shape[1]
    reverse = layer % 2 == 0
    fwd, bwd = local_resets(start, rows)
    reset = bwd if reverse else fwd
    ends, _ = sweep(ds, None, tab, zeros_state(2), reset, reverse, True)
    emit_ends(out, ends_out, ends, tab, reset, rows // SUB, reverse, True)


def back_first(layer, total_tokens, copies, begin, start, back, norms1, table, prm, u, norms,
               slow1, sig, part, slope, slow, far_maps, g_out, ds, out, ends_out, tile_out, dv, dg, dml, sums_out,
               maps):
    begin()
    maps = fetch_maps(copies, far_maps, maps, (1, 2, 0))
    rows = ds.ref.shape[1]
    tile = total_of(back())
    tile_out.ref[...] = tile
    norms1, norms, prm = norms1(), norms(), prm()
    half = tile.shape[0] // 2
    base = (layer + 1) * PARAMS
    over = 1.0 / rowcat(prm, base + GAIN)
    shift = rowcat(prm, base + SHIFT)
    factor = norms1[0:1, :] * (1.0 / total_tokens)
    m_one, m_two = factor * lanes(tile[:half]), factor * over * lanes(tile[half:])
    m_one = m_one - shift * m_two
    sums = [0.0, 0.0, 0.0]
    for i, at in enumerate(chunks(rows, 2)):
        g = cat(u(), at) - m_one - slow1.part(i)[at, :].astype(F32) * m_two
        put(g_out.ref, at, g)
        sums = back_chunk(i, at, g, cat(sig.part(i), at), cat(part.part(i), at),
                          lambda: slow.part(i)[at, :].astype(F32),
                          lambda: cat(slope.part(i), at), maps, (dv, dg, dml, ds), sums)
    sums_rows(sums_out, sums)
    adjoint_start(layer, start, table()[layer], ds.ref, out, ends_out)


def back_second(layer, copies, begin, start, gathered, mom, table, ends, norms, prm, ds, states_low, g, dml, h,
                weight, *refs):
    if layer == 0:
        back, prods, dlow, u0, u1, u2, u3, adj, states, maps, u_ref = refs
    else:
        back, u_out, prods, dlow, adj, states, maps = refs
        u_ref = u_out.ref
    begin()
    weight = Later(copies, [(weight.at[layer], maps)], maps)
    rows = adj.shape[1]
    reverse = layer % 2 == 0
    tab = table()[layer]
    init, reset = resume(start, rows, gathered(), mom(), tab, ends(), reverse, True)
    for at in chunks(rows, 8):
        put(states, at, states_low()[at, :].astype(F32))

    def extra(at, a, sums):
        new = []
        for h_ in range(2):
            re, im = a[h_], a[2 + h_]
            sre, sim = states[h_, at, :], states[2 + h_, at, :]
            new.append(re * sre + im * sim)
            new.append(im * sre - re * sim)
        return tuple(s + n for s, n in zip(sums, new, strict=True))

    _, sums = sweep(ds(), adj, tab, init, reset, reverse, True, extra)
    flat = [jnp.sum(s, axis=0, keepdims=True) for s in sums]
    prods.ref[...] = jnp.concatenate(flat + [jnp.zeros((8 - len(flat), LANES), F32)], axis=0)
    prods.flush()
    gamma = lanes(tab[12:14, :])
    gamma = jnp.concatenate([gamma, gamma], axis=1)
    base = layer * PARAMS
    prm, norms = prm(), norms()
    skip = rowcat(prm, base + SKIP)
    factor, bias, inverse, mean = (norms[i : i + 1, :] for i in range(4))
    one = two = 0.0
    for i, at in enumerate(chunks(rows, 2)):
        low = (cat(adj, at) * gamma).astype(BF16)
        dlow.ref[at, :] = low
        dlow.flush(i, 2)
        dscaled = dot_nt(low, weight()[...]) + dml.part(i)[at, :].astype(F32) * skip
        normed = (cat(h.part(i), at) - mean) * inverse
        own = g()[at, :].astype(F32) if layer == 1 else cat(g(), at)
        put(u_ref, at, own + factor * dscaled)
        one = one + jnp.sum(dscaled, axis=0, keepdims=True)
        two = two + jnp.sum(dscaled * normed, axis=0, keepdims=True)
    add_chunk(back, one, two)
    if layer == 0:
        mp, _ = place()
        for k, piece in enumerate((u0, u1, u2, u3)):
            piece.ref[...] = u_ref[mp ^ k, :, :].astype(piece.ref.dtype)
            piece.flush()


def result_kernel(copies, begin, r0, r1, r2, r3, result):
    begin()
    mp, _ = place()
    rows = r0.dst.shape[0]
    for k, r in ((1, r1), (2, r2), (3, r3), (0, r0)):
        at = pl.ds(pl.multiple_of((mp ^ k) * rows, SUB), rows)
        result.ref[at, :] = r()[...].astype(F32)
        copies.flush(result.ref.at[at], result.dst.at[at])
    result.sent = True


def last_kernel(total_tokens, copies, begin, norms, back, tile1, u0, u1, u2, u3, stream,
                out, gain_out, shift_out, held):
    begin()
    mp, _ = place()
    rows = u0.dst.shape[0]
    streams = [Later(copies, [(own_rows(stream, rows, k), held.at[k])], held.at[k]) for k in range(4)]
    tile, tile1, norms = total_of(back()), tile1(), norms()
    half = tile.shape[0] // 2
    zero = jnp.zeros((1, LANES), F32)
    one, two, factor, inverse, mean, later_one, later_two = [zero] * 7
    for j in range(half):
        mine = jnp.where(mp == j, 1.0, 0.0)
        cols = slice(j * LANES, (j + 1) * LANES)
        one = one + mine * tile[j : j + 1, :]
        two = two + mine * tile[half + j : half + j + 1, :]
        later_one = later_one + mine * tile1[j : j + 1, :]
        later_two = later_two + mine * tile1[half + j : half + j + 1, :]
        factor = factor + mine * norms[0:1, cols]
        inverse = inverse + mine * norms[2:3, cols]
        mean = mean + mine * norms[3:4, cols]
    scaled = factor * (1.0 / total_tokens)
    m_one, m_two = scaled * one, scaled * two
    for k, u in enumerate((u0, u1, u2, u3)):
        at = pl.ds(pl.multiple_of((mp ^ k) * rows, SUB), rows)
        normed = (streams[k]()[...] - mean) * inverse
        out.ref[at, :] = u()[...].astype(F32) - m_one - normed * m_two
        copies.flush(out.ref.at[at], out.dst.at[at])
    out.sent = True
    gain_out.ref[...] = jnp.concatenate([two, later_two], axis=0)
    shift_out.ref[...] = jnp.concatenate([one, later_one], axis=0)


def pair_sum(copies, begin, keep, got, mine, other):
    keep, got = keep(), got()
    size = keep.shape[1]
    for at in chunks(size, size // 16):
        other.ref[at, :] = (keep[1, at, :].astype(F32) + got[1, at, :].astype(F32)).astype(other.ref.dtype)
        mine.ref[at, :] = (keep[0, at, :].astype(F32) + got[0, at, :].astype(F32)).astype(mine.ref.dtype)


def four_sum(copies, begin, *refs):
    *ins, out = refs
    out = out.ref
    top = 0
    for mine, got in zip(ins[::2], ins[1::2], strict=True):
        mine, got = mine(), got()
        rows = mine.shape[0]
        for at in chunks(rows, rows // 16):
            total = mine[at, :].astype(F32) + got[at, :].astype(F32)
            out[top + at.start : top + at.stop, :] = total.astype(out.dtype)
        top += rows
    if top < out.shape[0]:
        out[top:, :] = jnp.zeros((out.shape[0] - top, out.shape[1]), out.dtype)


def piece_sum(copies, begin, pieces, out):
    pieces = pieces()
    count, rows = pieces.shape[0], pieces.shape[1]
    for at in chunks(rows, rows // 16):
        total = pieces[0, at, :].astype(F32)
        for d in range(1, count):
            total = total + pieces[d, at, :].astype(F32)
        low = total.astype(out.ref.dtype)
        for d in range(count):
            out.ref[d, at, :] = low


def hand_out(features, copies, begin, decay, phase, full0,
             in_own, o_grad, skip_grad, v_grad, g_grad, vb, gb, d_grad, p_grad, s_grad):
    begin()
    in_rows = features + 16
    full0 = full0()
    for layer in range(2):
        top = layer * in_rows
        in_own.ref[layer, :, :] = full0[top : top + features, :]
    decay, phase = decay(), phase()
    for layer, full, top in ((0, full0, 2 * in_rows), (1, full0, 2 * in_rows + 3 * features + 16)):
        for i, out in enumerate((v_grad, g_grad, o_grad)):
            out.ref[layer, :, :] = full[top + i * features : top + (i + 1) * features, :].astype(F32)
            copies.flush(out.ref.at[layer], out.dst.at[layer])
            out.sent = True
        top += 3 * features
        row = slice(layer, layer + 1)
        vecs = full[top : top + 16, :].astype(F32)
        vb.ref[row, :] = vecs[0:1, :]
        gb.ref[row, :] = vecs[1:2, :]
        skip_grad.ref[row, :] = vecs[2:3, :]
        top = layer * in_rows + features
        tile = full0[top : top + 16, :].astype(F32)
        for h in range(2):
            cols = slice(h * LANES, (h + 1) * LANES)
            d_grad.ref[row, cols] = -jnp.exp(decay[row, cols]) * tile[3 * h : 3 * h + 1, :]
            p_grad.ref[row, cols] = jnp.exp(phase[row, cols]) * tile[3 * h + 1 : 3 * h + 2, :]
            s_grad.ref[row, cols] = tile[3 * h + 2 : 3 * h + 3, :]


def input_kernel(copies, begin, p0, p1, p2, p3, out):
    begin()
    mp, _ = place()
    for k, piece in enumerate((p0, p1, p2, p3)):
        cols = pl.ds(pl.multiple_of((mp ^ k) * LANES, LANES), LANES)
        piece = piece()
        for layer in range(out.ref.shape[0]):
            out.ref[layer, :, cols] = piece[layer].astype(F32)


def shape(dims, dtype=F32):
    return jax.ShapeDtypeStruct(tuple(dims), dtype)


def every(x):
    return lax.all_to_all(x, AXES, 0, 0)


def hop(x, k):
    count = lax.axis_size("mp")
    return lax.ppermute(x, "mp", [(i, i ^ k) for i in range(count)])


def spread(x, then=None):
    far = hop(x, 2)
    held = far if then is None else after(far, then)
    return hop(x, 1), far, hop(held, 1)


def swap(sends):
    return [hop(x, k + 1) for k, x in enumerate(sends)]


def after(x, *ys):
    return lax.optimization_barrier((x, *ys))[0]


def on_device(
    stream,
    cotangent,
    start_offsets,
    norm_gain,
    norm_shift,
    input_map,
    decay_log,
    phase_log,
    scale_log,
    output_map,
    skip_gain,
    value_weight,
    gate_weight,
    value_bias,
    gate_bias,
):
    block, width = stream.shape
    layers = input_map.shape[0]
    count_dp, parts = lax.axis_size("dp"), lax.axis_size("mp")
    devices = count_dp * parts
    tokens = block * count_dp
    rows = block // parts
    features = width * parts
    assert width == LANES and features == 4 * LANES and layers == 2 and parts == 4

    plist = (norm_gain, norm_shift, skip_gain, value_bias, gate_bias)
    blocks = shape((parts, rows, width))
    v_blocks = pltpu.VMEM(blocks.shape, F32)
    one_block = (rows, width)
    low_block = shape(one_block, BF16)
    wide_low = shape((rows, features), BF16)
    near_blocks = Near(blocks)
    near_ends = Near(shape((4, SUB, LANES)))
    near_every = Near(shape((devices, 4, LANES)))
    near_sums = Near(shape((devices, 2 * parts, LANES)))
    near_norms = Near(shape((8, features)))
    near_low = Near(low_block)
    packed_w = shape((3 * features, width), BF16)
    one_map = pltpu.VMEM((features, features), BF16)
    maps = pltpu.VMEM((3, features, features), BF16)
    all_maps = shape((3, features, features), BF16)

    mom_out, table, *sends = call(
        functools.partial(first_kernel, rows),
        [near_every, Near(shape((layers, 16, LANES)))] + [Near(shape((rows + 32, width), BF16))] * 3,
        [pltpu.VMEM((block, width), F32)],
        start_offsets, Raw(stream), *plist, decay_log, phase_log, scale_log,
        scalars=1,
    )
    table = Near(table)
    got_h = [Near(x) for x in swap(sends)]
    mom0 = Near(every(after(mom_out, got_h[1].array)))
    h0, prm = call(
        gather_block,
        [near_blocks, Near(shape((parts, 16, width)))],
        [pltpu.VMEM(one_block, F32)],
        *got_h, *plist, Raw(stream),
    )
    h0, prm = Near(h0), Near(prm)
    packs = call(
        functools.partial(pack_maps, layers), [packed_w] * layers, [], output_map, value_weight, gate_weight
    )
    w0 = after(packs[0], got_h[1].array, got_h[2].array)
    (full0,) = call(assemble, [all_maps], [], w0, *[Near(w) for w in spread(w0, mom0.array)])

    drive0, norms0, ends_all, ends0, slow0 = call(
        functools.partial(drive_first, tokens),
        [near_blocks, near_norms, near_every, near_ends, wide_low],
        [one_map],
        start_offsets, mom0, table, h0, prm, Raw(input_map),
        scalars=1,
    )
    got = Near(after(every(ends_all), full0))
    norms0 = Near(norms0)
    h1, mom_out, h0, states0, sent0, slope0, sig0, part0 = call(
        functools.partial(mix_first, 0),
        [near_blocks, near_sums, Raw(blocks), wide_low, wide_low,
         blocks, blocks, blocks],
        [v_blocks, maps],
        start_offsets, got, mom0, table, Near(ends0), norms0, prm, Near(drive0), h0, Raw(full0),
        scalars=1,
    )
    h1 = Near(h1)
    sends = call(pack_block, [low_block] * 3, [], after(cotangent, got.array))
    mom1 = Near(after(every(mom_out), *sends))
    got_cot = [Near(x) for x in swap(sends)]
    w1 = after(packs[1], got.array)
    (full1,) = call(assemble, [all_maps], [], w1, *[Near(w) for w in spread(w1, mom1.array)])
    drive1, norms1, ends_all, ends1, slow1 = call(
        functools.partial(drive_next, 1, tokens),
        [near_blocks, near_norms, near_every, near_ends, wide_low],
        [one_map],
        start_offsets, mom1, prm, table, h1, Raw(input_map),
        scalars=1,
    )
    got = Near(after(every(ends_all), full1))
    norms1 = Near(norms1)
    vgo_rows, in_rows = 3 * features + 16, features + 16

    def pair_share(keep, send):
        size = Near(shape(keep.shape[1:], BF16))
        return call(pair_sum, [size, size], [], Near(keep), Near(hop(send, 1)))

    vgo_half = Near(shape((2, vgo_rows, width), BF16))
    in_half = Near(shape((2, in_rows, width), BF16))
    vgo_pack = pltpu.VMEM((parts, vgo_rows, width), BF16)
    in_pack = pltpu.VMEM((parts, in_rows, width), BF16)
    in_room = [in_pack, pltpu.VMEM((features, features), F32), one_map]
    ds1, ends_all, back_ends1, h1, states1, cot, sent1, dv, dg, dml1, sums, *res = call(
        functools.partial(turn, 1),
        [near_blocks, near_every, near_ends, Raw(blocks)] + [wide_low] * 6 + [near_norms.array, shape(one_block)]
        + [low_block] * 3,
        [maps, v_blocks, v_blocks, v_blocks],
        start_offsets, got, mom0, table, Near(ends1), norms1, prm, Near(drive1), h1, Raw(full1), *got_cot, Raw(cotangent),
        scalars=1,
    )
    got = Near(every(ends_all))
    keep1, send1 = call(
        weight_grads, [vgo_half, vgo_half], [vgo_pack], sent1, dv, dg, states1, dml1, sums
    )
    got = Near(after(got.array, keep1))
    send1 = after(send1, got.array)
    got = Near(after(got.array, keep1))
    back_out, u1, prods, dlow = call(
        functools.partial(back_second, 1),
        [near_sums, near_blocks, Near(shape((8, LANES))), Near(wide_low)],
        [v_blocks, v_blocks, one_map],
        start_offsets, got, mom0, table, Near(back_ends1), norms1, prm, Near(ds1), states1, cot, Halves(dml1),
        Halves(h1), Raw(input_map),
        scalars=1,
    )
    back1 = Near(every(back_out))
    in_keep1, in_send1 = call(
        functools.partial(input_grads, 1), [in_half, in_half], in_room, slow1, Near(dlow), Near(prods), Raw(input_map)
    )
    mine1, other1 = pair_share(keep1, send1)
    in_send1 = after(in_send1, back1.array)
    back1 = Near(after(back1.array, in_keep1, mine1))
    far1 = hop(other1, 2)
    g0, ds0, ends_all, back_ends0, tile1, dv, dg, dml0, sums = call(
        functools.partial(back_first, 0, tokens),
        [near_blocks, near_blocks, near_every, near_ends, Near(shape((2 * parts, LANES)))] + [wide_low] * 3
        + [near_norms.array],
        [maps],
        start_offsets, back1, norms1, table, prm, Near(u1), norms0,
        Halves(slow1), Halves(sig0), Halves(part0), Halves(slope0), Halves(slow0), Raw(full0),
        scalars=1,
    )
    got = Near(every(after(ends_all, far1)))
    keep0, send0 = call(
        weight_grads, [vgo_half, vgo_half], [vgo_pack], sent0, dv, dg, states0, dml0, sums
    )
    in_mine1, in_other1 = pair_share(in_keep1, in_send1)
    in_far1 = hop(in_other1, 2)
    send0 = after(send0, got.array)
    got = Near(after(got.array, keep0, in_mine1))
    back_out, prods, dlow, *us = call(
        functools.partial(back_second, 0),
        [near_sums, Near(shape((8, LANES))), Near(wide_low), Near(shape(one_block))] + [near_low] * 3,
        [v_blocks, v_blocks, one_map, v_blocks],
        start_offsets, got, mom0, table, Near(back_ends0), norms0, prm, Near(ds0), states0, Near(g0), Halves(dml0),
        Halves(h0), Raw(input_map),
        scalars=1,
    )
    in_keep0, in_send0 = call(
        functools.partial(input_grads, 0), [in_half, in_half], in_room, slow0, Near(dlow), Near(prods), Raw(input_map)
    )
    mine0, other0 = pair_share(keep0, send0)
    far0 = hop(other0, 2)
    us = (us[0], *swap([after(u, in_send0) for u in us[1:]]))
    back0 = Near(every(after(back_out, in_send0, mine0)))
    in_mine0, in_other0 = pair_share(in_keep0, in_send0)
    in_far0 = hop(in_other0, 2)
    back0 = Near(after(back0.array, in_mine0))
    stream_grad, gain_grad, shift_grad = call(
        functools.partial(last_kernel, tokens),
        [shape((block, width)), shape((layers, width)), shape((layers, width))],
        [pltpu.VMEM((4,) + one_block, F32)],
        norms0, back0, Near(tile1), *[Near(u) for u in us], Raw(stream),
    )

    full_rows = 2 * (vgo_rows + in_rows)
    unit = 16 * count_dp
    padded = -(-full_rows // unit) * unit
    (own0,) = call(
        four_sum, [Near(shape((padded, width), BF16))], [],
        Near(in_mine0), Near(in_far0), Near(in_mine1), Near(in_far1), Near(mine0), Near(far0), Near(mine1), Near(far1),
    )
    split = (count_dp, padded // count_dp, width)
    pieces = lax.all_to_all(after(own0, back0.array).reshape(split), "dp", 0, 0)
    (copied,) = call(piece_sum, [Near(shape(split, BF16))], [], Near(pieces))
    copied = after(copied, stream_grad)
    result = [res[0], *swap([after(r, copied) for r in res[1:]])]
    (result,) = call(result_kernel, [shape((block, width))], [], res[0], *[Near(r) for r in result[1:]])
    full0 = lax.all_to_all(copied, "dp", 0, 0).reshape(padded, width)
    full0 = after(full0, result)
    mat, vec, state = shape((layers, features, width)), shape((layers, width)), shape(decay_log.shape)
    in_own, o_grad, skip_grad, v_grad, g_grad, vb, gb, d_grad, p_grad, s_grad = call(
        functools.partial(hand_out, features),
        [Near(shape((layers, features, width), BF16)), mat, vec, mat, mat, vec, vec, state, state, state],
        [],
        decay_log, phase_log, Near(full0),
    )
    (input_grad,) = call(
        input_kernel, [shape((layers, features, features))], [], Near(in_own), *[Near(x) for x in spread(in_own)]
    )
    return (
        result, stream_grad, gain_grad, shift_grad, input_grad, d_grad, p_grad, s_grad,
        o_grad, skip_grad, v_grad, g_grad, vb, gb,
    )


def solution(mesh):
    split = P("dp", "mp")
    cols = P(None, "mp")
    wide = P(None, None, "mp")
    placed = (
        split, split, P("dp"), cols, cols, P(), P(), P(), P(), wide, cols, wide, wide, cols, cols,
    )
    return jax.shard_map(
        on_device,
        mesh=mesh,
        in_specs=placed,
        out_specs=(
            split, split, cols, cols, P(), P(), P(), P(), wide, cols, wide, wide, cols, cols,
        ),
        check_vma=False,
    )
```

time: 416 us -> 244 us (0.59)
  blocking collectives: 93.4 us -> 0 us
  waiting for transfers between devices: 169 us -> 112 us
  local copies, waits for them, and re-layouts: 34.5 us -> 4.57 us
  Pallas kernels: 46.2 us -> 75.1 us
  other arithmetic: 19.6 us -> 0 us
    all_to_all x11 -> x2, waiting for transfers between devices: 150 us -> 32.5 us  [the longest x1 16.5 us: on_device(): full0 = lax.all_to_all(copied, 'dp', 0, 0).reshape(padded, width)]
    all_to_all x7 -> x0, blocking collectives: 93.4 us -> none  [the longest x5 52.5 us: every(): return lax.all_to_all(x, AXES, 0, 0)]
    ppermute x0 -> x29, waiting for transfers between devices: none -> 36.2 us  [hop(): return lax.ppermute(x, 'mp', [(i, i ^ k) for i in range(count)])]
    all_to_all x11 -> x2, starting transfers between devices: 42.3 us -> 7.42 us  [the longest x1 3.72 us: on_device(): full0 = lax.all_to_all(copied, 'dp', 0, 0).reshape(padded, width)]
    pallas_call x9 -> x27, Pallas kernels: 46.2 us -> 75.1 us  [call(): return made_call(max(used[0], 1))(*plain)]
    all_to_all x3 -> x8, waiting for transfers between devices: 19 us -> 43.2 us  [every(): return lax.all_to_all(x, AXES, 0, 0)]
    all_to_all x3 -> x8, starting transfers between devices: 7.71 us -> 25.3 us  [every(): return lax.all_to_all(x, AXES, 0, 0)]
    ppermute x0 -> x29, starting transfers between devices: none -> 16.1 us  [hop(): return lax.ppermute(x, 'mp', [(i, i ^ k) for i in range(count)])]
  transfers between devices with their start and end apart: 14 -> 39, of which waited for: 14 -> 23; matrix products, arithmetic and copies ran while one was open for 7% -> 0% of each run, Pallas kernels for 3% -> 24%
where the time goes in v2:
time: 244 us; the launch traced here: 242 us
  waiting for transfers between devices  112 us (46%)
  Pallas kernels  75.1 us (31%)
  starting transfers between devices  48.8 us (20%)
  local copies, waits for them, and re-layouts  4.57 us (2%)
    pallas_call x27, Pallas kernels, call(): return made_call(max(used[0], 1))(*plain)  75.1 us
    all_to_all x8, waiting for transfers between devices, every(): return lax.all_to_all(x, AXES, 0, 0)  43.2 us
    ppermute x29, waiting for transfers between devices, hop(): return lax.ppermute(x, 'mp', [(i, i ^ k) for i in range(count)])  36.2 us
    all_to_all x8, starting transfers between devices, every(): return lax.all_to_all(x, AXES, 0, 0)  25.3 us
    all_to_all x1, waiting for transfers between devices, on_device(): full0 = lax.all_to_all(copied, 'dp', 0, 0).reshape(padded, width)  16.5 us
    ppermute x29, starting transfers between devices, hop(): return lax.ppermute(x, 'mp', [(i, i ^ k) for i in range(count)])  16.1 us
    all_to_all x1, waiting for transfers between devices, on_device(): pieces = lax.all_to_all(after(own0, back0.array).reshape(split), 'dp', 0, 0)  16 us
  transfers between devices with their start and end apart: 39, of which 23 were waited for; matrix products, arithmetic and copies ran while one was open for 0% of the time, Pallas kernels for 24%

profile of v2, /device:TPU:0, one launch (start us, length us, event | category | flops | bytes accessed | tf_op | source)
XLA Modules:
  0.0 242.2 jit_solution(1305444606725926502)
XLA Ops:
  13.6 5.2 %all-to-all-start = ((f32[32,4,128]{2,1,0:T(4,128)}), f32[32,4,128]{2,1,0:T(4,128)S(1)}, u32[]{:S(2)}, u32[]{:S(2)}) async-start(f32[32,4,128]{2,1,0:T(4,128)} %get-tuple-element.138), calls=%async_computation | async-start | bytes 131072 | tf_op jit(solution)/shard_map/all_to_all | solution.py:917
  19.2 7.1 %all-to-all-done.refs_1_.refs_2_ = f32[32,4,128]{2,1,0:T(4,128)S(1)} async-done(((f32[32,4,128]{2,1,0:T(4,128)}), f32[32,4,128]{2,1,0:T(4,128)S(1)}, u32[]{:S(2)}, u32[]{:S(2)}) %all-to-all-start) | async-done | bytes 65568 | tf_op jit(solution)/shard_map/all_to_all | solution.py:917
  32.2 4.6 %all-to-all-start.1 = ((f32[32,4,128]{2,1,0:T(4,128)}), f32[32,4,128]{2,1,0:T(4,128)S(1)}, u32[]{:S(2)}, u32[]{:S(2)}) async-start(f32[32,4,128]{2,1,0:T(4,128)} %get-tuple-element.144), calls=%async_computation.1 | async-start | bytes 131072 | tf_op jit(solution)/shard_map/all_to_all | solution.py:917
  36.8 3.5 %shard_map.258.refs_9_.refs_12_ = bf16[3,512,512]{2,1,0:T(8,128)(2,1)} custom-call(bf16[1536,128]{1,0:T(8,128)(2,1)} %get-tuple-element.146.refs_0_, bf16[1536,128]{1,0:T(8,128)(2,1)S(1)} %collective-permute-done.3.refs_1_, bf16[1536,128]{1,0:T(8,128)(2,1)S(1)} %collective-permute-done.4.refs_2_, bf16[1536,128]{1,0:T(8,128)(2,1)} %collective-permute-done.5.refs_3_), custom_call_target="tpu_custom_call" | custom-call | tf_op jit(solution)/shard_map/pallas_call | solution.py:171
  40.3 3.9 %all-to-all-done.1.refs_1_ = f32[32,4,128]{2,1,0:T(4,128)S(1)} async-done(((f32[32,4,128]{2,1,0:T(4,128)}), f32[32,4,128]{2,1,0:T(4,128)S(1)}, u32[]{:S(2)}, u32[]{:S(2)}) %all-to-all-start.1) | async-done | bytes 65568 | tf_op jit(solution)/shard_map/all_to_all | solution.py:917
  44.6 5.8 %shard_map.259 = (f32[4,512,128]{2,1,0:T(8,128)S(1)}, f32[32,8,128]{2,1,0:T(8,128)}, f32[4,512,128]{2,1,0:T(8,128)}, bf16[512,512]{1,0:T(8,128)(2,1)}, bf16[512,...) custom-call(s32[1]{0:T(128)S(6)} %copy.29.refs_0_, ...), custom_call_target="tpu_custom_call" | custom-call | tf_op jit(solution)/shard_map/pallas_call | solution.py:171
  55.3 5.9 %all-to-all-done.2.refs_1_ = f32[32,8,128]{2,1,0:T(8,128)S(1)} async-done(((f32[32,8,128]{2,1,0:T(8,128)}), f32[32,8,128]{2,1,0:T(8,128)S(1)}, u32[]{:S(2)}, u32[]{:S(2)}) %all-to-all-start.2) | async-done | bytes 131104 | tf_op jit(solution)/shard_map/all_to_all | solution.py:917
  69.4 3.5 %shard_map.262.refs_9_ = bf16[3,512,512]{2,1,0:T(8,128)(2,1)} custom-call(bf16[1536,128]{1,0:T(8,128)(2,1)} %get-tuple-element.161.refs_0_, bf16[1536,128]{1,0:T(8,128)(2,1)S(1)} %collective-permute-done.6.refs_1_, bf16[1536,128]{1,0:T(8,128)(2,1)} %collective-permute-done.7.refs_2_, bf16[1536,128]{1,0:T(8,128)(2,1)S(1)} %collective-permute-done.8.refs_3_), custom_call_target="tpu_custom_call" | custom-call | tf_op jit(solution)/shard_map/pallas_call | solution.py:171
  72.9 3.9 %all-to-all-done.3.refs_1_ = f32[32,4,128]{2,1,0:T(4,128)S(1)} async-done(((f32[32,4,128]{2,1,0:T(4,128)}), f32[32,4,128]{2,1,0:T(4,128)S(1)}, u32[]{:S(2)}, u32[]{:S(2)}) %all-to-all-start.3) | async-done | bytes 65568 | tf_op jit(solution)/shard_map/all_to_all | solution.py:917
  78.3 8.1 %shard_map.263 = (f32[4,512,128]{2,1,0:T(8,128)S(1)}, f32[32,4,128]{2,1,0:T(4,128)}, f32[4,8,128]{2,1,0:T(8,128)S(1)}, f32[4,512,128]{2,1,0:T(8,128)}, bf16[512,...) custom-call(s32[1]{0:T(128)S(6)} %copy.29.refs_0_, ...), custom_call_target="tpu_custom_call" | custom-call | tf_op jit(solution)/shard_map/pallas_call | solution.py:171
  91.8 4.6 %all-to-all-done.4.refs_1_ = f32[32,4,128]{2,1,0:T(4,128)S(1)} async-done(((f32[32,4,128]{2,1,0:T(4,128)}), f32[32,4,128]{2,1,0:T(4,128)S(1)}, u32[]{:S(2)}, u32[]{:S(2)}) %all-to-all-start.4) | async-done | bytes 65568 | tf_op jit(solution)/shard_map/all_to_all | solution.py:917
  100.9 4.9 %shard_map.265 = (f32[32,8,128]{2,1,0:T(8,128)}, f32[4,512,128]{2,1,0:T(8,128)S(1)}, f32[8,128]{1,0:T(8,128)S(1)}, bf16[512,512]{1,0:T(8,128)(2,1)S(1)}) custom-call(s32[1]{0:T(128)S(6)} %copy.29.refs_0_, f32[32,4,128]{2,1,0:T(4,128)S(1)} %all-to-all-done.4.refs_1_, f32[32,4,128]{2,1,0:T(4,128)S(1)} %all-to-all-done.refs_1_.refs_2_, ...), custom_call_target="tpu_custom_call" | custom-call | tf_op jit(solution)/shard_map/pallas_call | solution.py:171
  110.9 5.7 %all-to-all-done.5.refs_1_ = f32[32,8,128]{2,1,0:T(8,128)S(1)} async-done(((f32[32,8,128]{2,1,0:T(8,128)}), f32[32,8,128]{2,1,0:T(8,128)S(1)}, u32[]{:S(2)}, u32[]{:S(2)}) %all-to-all-start.5) | async-done | bytes 131104 | tf_op jit(solution)/shard_map/all_to_all | solution.py:917
  116.6 6.5 %shard_map.268 = (f32[4,512,128]{2,1,0:T(8,128)S(1)}, f32[4,512,128]{2,1,0:T(8,128)S(1)}, f32[32,4,128]{2,1,0:T(4,128)}, f32[4,8,128]{2,1,0:T(8,128)S(1)}, f32[8...) custom-call(s32[1]{0:T(128)S(6)} %copy.29.refs_0_, ...), custom_call_target="tpu_custom_call" | custom-call | tf_op jit(solution)/shard_map/pallas_call | solution.py:171
  130.0 3.7 %all-to-all-done.6.refs_1_ = f32[32,4,128]{2,1,0:T(4,128)S(1)} async-done(((f32[32,4,128]{2,1,0:T(4,128)}), f32[32,4,128]{2,1,0:T(4,128)S(1)}, u32[]{:S(2)}, u32[]{:S(2)}) %all-to-all-start.6) | async-done | bytes 65568 | tf_op jit(solution)/shard_map/all_to_all | solution.py:917
  137.3 5.7 %shard_map.271 = (f32[32,8,128]{2,1,0:T(8,128)}, f32[8,128]{1,0:T(8,128)S(1)}, bf16[512,512]{1,0:T(8,128)(2,1)S(1)}, f32[512,128]{1,0:T(8,128)S(1)}, bf16[512,12...) custom-call(s32[1]{0:T(128)S(6)} %copy.29.refs_0_, ...), custom_call_target="tpu_custom_call" | custom-call | tf_op jit(solution)/shard_map/pallas_call | solution.py:171
  152.2 8.4 %all-to-all-done.7.refs_1_ = f32[32,8,128]{2,1,0:T(8,128)S(1)} async-done(((f32[32,8,128]{2,1,0:T(8,128)}), f32[32,8,128]{2,1,0:T(8,128)S(1)}, u32[]{:S(2)}, u32[]{:S(2)}) %all-to-all-start.7) | async-done | bytes 131104 | tf_op jit(solution)/shard_map/all_to_all | solution.py:917
  168.1 3.7 %all-to-all-start.8 = ((bf16[8,528,128]{2,1,0:T(8,128)(2,1)}), bf16[8,528,128]{2,1,0:T(8,128)(2,1)S(1)}, u32[]{:S(2)}, u32[]{:S(2)}) async-start(bf16[8,528,128]{2,1,0:T(8,128)(2,1)} %bitcast), calls=%async_computation.8 | async-start | bytes 2162688 | tf_op jit(solution)/shard_map/all_to_all | solution.py:1129
  173.8 4.5 %collective-permute-done.21.refs_5_ = bf16[512,128]{1,0:T(8,128)(2,1)S(1)} collective-permute-done((bf16[512,128]{1,0:T(8,128)(2,1)S(1)}, bf16[512,128]{1,0:T(8,128)(2,1)S(1)}, u32[]{:S(2)}, u32[]{:S(2)}) %collective-permute-start.21) | collective-permute-done | bytes 131104 | tf_op jit(solution)/shard_map/ppermute | solution.py:922
  182.2 16.0 %all-to-all-done.8.refs_0_ = bf16[8,528,128]{2,1,0:T(8,128)(2,1)S(1)} async-done(((bf16[8,528,128]{2,1,0:T(8,128)(2,1)}), bf16[8,528,128]{2,1,0:T(8,128)(2,1)S(1)}, u32[]{:S(2)}, u32[]{:S(2)}) %all-to-all-start.8) | async-done | bytes 1081376 | tf_op jit(solution)/shard_map/all_to_all | solution.py:1129
  199.4 3.7 %all-to-all-start.9 = ((bf16[8,528,128]{2,1,0:T(8,128)(2,1)}), bf16[8,528,128]{2,1,0:T(8,128)(2,1)S(1)}, u32[]{:S(2)}, u32[]{:S(2)}) async-start(bf16[8,528,128]{2,1,0:T(8,128)(2,1)} %shard_map.276), calls=%async_computation.9 | async-start | bytes 2162688 | tf_op jit(solution)/shard_map/all_to_all | solution.py:1134
  205.0 4.5 %collective-permute-done.24.refs_2_ = bf16[512,128]{1,0:T(8,128)(2,1)S(1)} collective-permute-done((bf16[512,128]{1,0:T(8,128)(2,1)S(1)}, bf16[512,128]{1,0:T(8,128)(2,1)S(1)}, u32[]{:S(2)}, u32[]{:S(2)}) %collective-permute-start.24) | collective-permute-done | bytes 131104 | tf_op jit(solution)/shard_map/ppermute | solution.py:922
  213.2 16.5 %all-to-all-done.9 = bf16[8,528,128]{2,1,0:T(8,128)(2,1)S(1)} async-done(((bf16[8,528,128]{2,1,0:T(8,128)(2,1)}), bf16[8,528,128]{2,1,0:T(8,128)(2,1)S(1)}, u32[]{:S(2)}, u32[]{:S(2)}) %all-to-all-start.9) | async-done | bytes 1081376 | tf_op jit(solution)/shard_map/all_to_all | solution.py:1134
  232.2 6.7 %collective-permute-done.27.refs_2_ = bf16[2,512,128]{2,1,0:T(8,128)(2,1)S(1)} collective-permute-done((bf16[2,512,128]{2,1,0:T(8,128)(2,1)S(1)}, bf16[2,512,128]{2,1,0:T(8,128)(2,1)S(1)}, u32[]{:S(2)}, u32[]{:S(2)}) %collective-permute-start.27) | collective-permute-done | bytes 262176 | tf_op jit(solution)/shard_map/ppermute | solution.py:922
  (119 shorter events, 93.8 us)
Async XLA Ops:
  12.4 13.9 %collective-permute-start.4 = (bf16[1536,128]{1,0:T(8,128)(2,1)}, bf16[1536,128]{1,0:T(8,128)(2,1)S(1)}, u32[]{:S(2)}, u32[]{:S(2)}) collective-permute-start(bf16[1536,128]{1,0:T(8,128)(2,1)} %get-tuple-element.146.refs_0_), channel_id=1, source_target_pairs={{0,2},{1,3},{2,0},{3,1},{4,6},{5,7},{6,4},{7,5},{8,10},{9,11},{10,... | collective-permute-start | bytes 1179656 | tf_op jit(solution)/shard_map/ppermute | solution.py:922
  13.6 12.6 %all-to-all-start = ((f32[32,4,128]{2,1,0:T(4,128)}), f32[32,4,128]{2,1,0:T(4,128)S(1)}, u32[]{:S(2)}, u32[]{:S(2)}) async-start(f32[32,4,128]{2,1,0:T(4,128)} %get-tuple-element.138), calls=%async_computation | async-start | bytes 131072 | tf_op jit(solution)/shard_map/all_to_all | solution.py:917
  18.9 17.9 %collective-permute-start.3 = (bf16[1536,128]{1,0:T(8,128)(2,1)}, bf16[1536,128]{1,0:T(8,128)(2,1)S(1)}, u32[]{:S(2)}, u32[]{:S(2)}) collective-permute-start(bf16[1536,128]{1,0:T(8,128)(2,1)} %get-tuple-element.146.refs_0_), channel_id=1, source_target_pairs={{0,1},{1,0},{2,3},{3,2},{4,5},{5,4},{6,7},{7,6},{8,9},{9,8},{10,11... | collective-permute-start | bytes 1179656 | tf_op jit(solution)/shard_map/ppermute | solution.py:922
  26.3 10.5 %collective-permute-start.5 = (bf16[1536,128]{1,0:T(8,128)(2,1)S(1)}, bf16[1536,128]{1,0:T(8,128)(2,1)}, u32[]{:S(2)}, u32[]{:S(2)}) collective-permute-start(bf16[1536,128]{1,0:T(8,128)(2,1)S(1)} %collective-permute-done.4.refs_2_), channel_id=1, source_target_pairs={{0,1},{1,0},{2,3},{3,2},{4,5},{5,4},{6,7},{7,6},{8,9},{9,8},{10,11... | collective-permute-start | bytes 1179656 | tf_op jit(solution)/shard_map/ppermute | solution.py:922
  32.2 12.0 %all-to-all-start.1 = ((f32[32,4,128]{2,1,0:T(4,128)}), f32[32,4,128]{2,1,0:T(4,128)S(1)}, u32[]{:S(2)}, u32[]{:S(2)}) async-start(f32[32,4,128]{2,1,0:T(4,128)} %get-tuple-element.144), calls=%async_computation.1 | async-start | bytes 131072 | tf_op jit(solution)/shard_map/all_to_all | solution.py:917
  44.2 17.1 %collective-permute-start.7 = (bf16[1536,128]{1,0:T(8,128)(2,1)}, bf16[1536,128]{1,0:T(8,128)(2,1)}, u32[]{:S(2)}, u32[]{:S(2)}) collective-permute-start(bf16[1536,128]{1,0:T(8,128)(2,1)} %get-tuple-element.161.refs_0_), channel_id=1, source_target_pairs={{0,2},{1,3},{2,0},{3,1},{4,6},{5,7},{6,4},{7,5},{8,10},{9,11},{10,... | collective-permute-start | bytes 1179656 | tf_op jit(solution)/shard_map/ppermute | solution.py:922
  50.4 10.8 %all-to-all-start.2 = ((f32[32,8,128]{2,1,0:T(8,128)}), f32[32,8,128]{2,1,0:T(8,128)S(1)}, u32[]{:S(2)}, u32[]{:S(2)}) async-start(f32[32,8,128]{2,1,0:T(8,128)} %get-tuple-element.152), calls=%async_computation.2 | async-start | bytes 262144 | tf_op jit(solution)/shard_map/all_to_all | solution.py:917
  53.0 16.3 %collective-permute-start.6 = (bf16[1536,128]{1,0:T(8,128)(2,1)}, bf16[1536,128]{1,0:T(8,128)(2,1)S(1)}, u32[]{:S(2)}, u32[]{:S(2)}) collective-permute-start(bf16[1536,128]{1,0:T(8,128)(2,1)} %get-tuple-element.161.refs_0_), channel_id=1, source_target_pairs={{0,1},{1,0},{2,3},{3,2},{4,5},{5,4},{6,7},{7,6},{8,9},{9,8},{10,11... | collective-permute-start | bytes 1179656 | tf_op jit(solution)/shard_map/ppermute | solution.py:922
  61.2 8.1 %collective-permute-start.8 = (bf16[1536,128]{1,0:T(8,128)(2,1)}, bf16[1536,128]{1,0:T(8,128)(2,1)S(1)}, u32[]{:S(2)}, u32[]{:S(2)}) collective-permute-start(bf16[1536,128]{1,0:T(8,128)(2,1)} %collective-permute-done.7.refs_2_), channel_id=1, source_target_pairs={{0,1},{1,0},{2,3},{3,2},{4,5},{5,4},{6,7},{7,6},{8,9},{9,8},{10,11... | collective-permute-start | bytes 1179656 | tf_op jit(solution)/shard_map/ppermute | solution.py:922
  61.5 15.3 %collective-permute-start.9 = (bf16[512,128]{1,0:T(8,128)(2,1)}, bf16[512,128]{1,0:T(8,128)(2,1)S(1)}, u32[]{:S(2)}, u32[]{:S(2)}) collective-permute-start(bf16[512,128]{1,0:T(8,128)(2,1)} %get-tuple-element.154), channel_id=1, source_target_pairs={{0,1},{1,0},{2,3},{3,2},{4,5},{5,4},{6,7},{7,6},{8,9},{9,8},{10,11... | collective-permute-start | bytes 393224 | tf_op jit(solution)/shard_map/ppermute | solution.py:922
  61.8 15.7 %collective-permute-start.10 = (bf16[512,128]{1,0:T(8,128)(2,1)}, bf16[512,128]{1,0:T(8,128)(2,1)}, u32[]{:S(2)}, u32[]{:S(2)}) collective-permute-start(bf16[512,128]{1,0:T(8,128)(2,1)} %get-tuple-element.155), channel_id=1, source_target_pairs={{0,2},{1,3},{2,0},{3,1},{4,6},{5,7},{6,4},{7,5},{8,10},{9,11},{10,... | collective-permute-start | bytes 393224 | tf_op jit(solution)/shard_map/ppermute | solution.py:922
  62.2 15.2 %collective-permute-start.11 = (bf16[512,128]{1,0:T(8,128)(2,1)}, bf16[512,128]{1,0:T(8,128)(2,1)}, u32[]{:S(2)}, u32[]{:S(2)}) collective-permute-start(bf16[512,128]{1,0:T(8,128)(2,1)} %get-tuple-element.156), channel_id=1, source_target_pairs={{0,3},{1,2},{2,1},{3,0},{4,7},{5,6},{6,5},{7,4},{8,11},{9,10},{10,... | collective-permute-start | bytes 393224 | tf_op jit(solution)/shard_map/ppermute | solution.py:922
  66.8 10.0 %all-to-all-start.3 = ((f32[32,4,128]{2,1,0:T(4,128)}), f32[32,4,128]{2,1,0:T(4,128)S(1)}, u32[]{:S(2)}, u32[]{:S(2)}) async-start(f32[32,4,128]{2,1,0:T(4,128)} %get-tuple-element.159), calls=%async_computation.3 | async-start | bytes 131072 | tf_op jit(solution)/shard_map/all_to_all | solution.py:917
  86.4 10.0 %all-to-all-start.4 = ((f32[32,4,128]{2,1,0:T(4,128)}), f32[32,4,128]{2,1,0:T(4,128)S(1)}, u32[]{:S(2)}, u32[]{:S(2)}) async-start(f32[32,4,128]{2,1,0:T(4,128)} %get-tuple-element.170), calls=%async_computation.4 | async-start | bytes 131072 | tf_op jit(solution)/shard_map/all_to_all | solution.py:917
  100.4 23.3 %collective-permute-start.13 = (bf16[1552,128]{1,0:T(8,128)(2,1)}, bf16[1552,128]{1,0:T(8,128)(2,1)}, u32[]{:S(2)}, u32[]{:S(2)}) collective-permute-start(bf16[1552,128]{1,0:T(8,128)(2,1)} %get-tuple-element.198), channel_id=1, source_target_pairs={{0,2},{1,3},{2,0},{3,1},{4,6},{5,7},{6,4},{7,5},{8,10},{9,11},{10,... | collective-permute-start | bytes 1191944 | tf_op jit(solution)/shard_map/ppermute | solution.py:922
  105.8 10.8 %all-to-all-start.5 = ((f32[32,8,128]{2,1,0:T(8,128)}), f32[32,8,128]{2,1,0:T(8,128)S(1)}, u32[]{:S(2)}, u32[]{:S(2)}) async-start(f32[32,8,128]{2,1,0:T(8,128)} %get-tuple-element.184), calls=%async_computation.5 | async-start | bytes 262144 | tf_op jit(solution)/shard_map/all_to_all | solution.py:917
  123.7 10.0 %all-to-all-start.6 = ((f32[32,4,128]{2,1,0:T(4,128)}), f32[32,4,128]{2,1,0:T(4,128)S(1)}, u32[]{:S(2)}, u32[]{:S(2)}) async-start(f32[32,4,128]{2,1,0:T(4,128)} %get-tuple-element.199), calls=%async_computation.6 | async-start | bytes 131072 | tf_op jit(solution)/shard_map/all_to_all | solution.py:917
  133.7 12.3 %collective-permute-start.18 = (bf16[2,1552,128]{2,1,0:T(8,128)(2,1)}, bf16[2,1552,128]{2,1,0:T(8,128)(2,1)S(1)}, u32[]{:S(2)}, u32[]{:S(2)}) collective-permute-start(bf16[2,1552,128]{2,1,0:T(8,128)(2,1)} %copy-done.8), channel_id=1, source_target_pairs={{0,1},{1,0},{2,3},{3,2},{4,5},{5,4},{6,7},{7,6},{8,9},{9,8},{10,11... | collective-permute-start | bytes 2383880 | tf_op jit(solution)/shard_map/ppermute | solution.py:922
  146.9 19.0 %collective-permute-start.19 = (bf16[1552,128]{1,0:T(8,128)(2,1)}, bf16[1552,128]{1,0:T(8,128)(2,1)S(1)}, u32[]{:S(2)}, u32[]{:S(2)}) collective-permute-start(bf16[1552,128]{1,0:T(8,128)(2,1)} %get-tuple-element.225), channel_id=1, source_target_pairs={{0,2},{1,3},{2,0},{3,1},{4,6},{5,7},{6,4},{7,5},{8,10},{9,11},{10,... | collective-permute-start | bytes 1191944 | tf_op jit(solution)/shard_map/ppermute | solution.py:922
  147.4 13.2 %all-to-all-start.7 = ((f32[32,8,128]{2,1,0:T(8,128)}), f32[32,8,128]{2,1,0:T(8,128)S(1)}, u32[]{:S(2)}, u32[]{:S(2)}) async-start(f32[32,8,128]{2,1,0:T(8,128)} %get-tuple-element.227), calls=%async_computation.7 | async-start | bytes 262144 | tf_op jit(solution)/shard_map/all_to_all | solution.py:917
  150.0 13.5 %collective-permute-start.17 = (bf16[528,128]{1,0:T(8,128)(2,1)}, bf16[528,128]{1,0:T(8,128)(2,1)S(1)}, u32[]{:S(2)}, u32[]{:S(2)}) collective-permute-start(bf16[528,128]{1,0:T(8,128)(2,1)} %get-tuple-element.221), channel_id=1, source_target_pairs={{0,2},{1,3},{2,0},{3,1},{4,6},{5,7},{6,4},{7,5},{8,10},{9,11},{10,... | collective-permute-start | bytes 405512 | tf_op jit(solution)/shard_map/ppermute | solution.py:922
  151.8 14.0 %collective-permute-start.16 = (bf16[528,128]{1,0:T(8,128)(2,1)S(1)}, bf16[528,128]{1,0:T(8,128)(2,1)S(1)}, u32[]{:S(2)}, u32[]{:S(2)}) collective-permute-start(bf16[528,128]{1,0:T(8,128)(2,1)S(1)} %get-tuple-element.220), channel_id=1, source_target_pairs={{0,2},{1,3},{2,0},{3,1},{4,6},{5,7},{6,4},{7,5},{8,10},{9,11},{10,... | collective-permute-start | bytes 405512 | tf_op jit(solution)/shard_map/ppermute | solution.py:922
  168.1 30.1 %all-to-all-start.8 = ((bf16[8,528,128]{2,1,0:T(8,128)(2,1)}), bf16[8,528,128]{2,1,0:T(8,128)(2,1)S(1)}, u32[]{:S(2)}, u32[]{:S(2)}) async-start(bf16[8,528,128]{2,1,0:T(8,128)(2,1)} %bitcast), calls=%async_computation.8 | async-start | bytes 2162688 | tf_op jit(solution)/shard_map/all_to_all | solution.py:1129
  199.4 30.4 %all-to-all-start.9 = ((bf16[8,528,128]{2,1,0:T(8,128)(2,1)}), bf16[8,528,128]{2,1,0:T(8,128)(2,1)S(1)}, u32[]{:S(2)}, u32[]{:S(2)}) async-start(bf16[8,528,128]{2,1,0:T(8,128)(2,1)} %shard_map.276), calls=%async_computation.9 | async-start | bytes 2162688 | tf_op jit(solution)/shard_map/all_to_all | solution.py:1134
  (34 other events, 160.5 us)

commit v3 on v2

--- a/solution.py
+++ b/solution.py
@@ -132,11 +132,11 @@
         for i, room in zip(made, vout, strict=True):
             results[i] = Result(copies, room, dsts[i])
 
-        def begin():
-            for part in range(2):
-                for i in autos:
-                    if part < operands[i].parts:
-                        operands[i].begin(part)
+        def begin(*some):
+            for one in some or [operands[i] for i in autos]:
+                operand, parts = one if isinstance(one, tuple) else (one, None)
+                for part in range(operand.parts) if parts is None else (parts,):
+                    operand.begin(part)
 
         body(copies, begin, *operands, *results, *rest)
         for r in results:
@@ -205,7 +205,7 @@
     return [slice(i * size, (i + 1) * size) for i in range(count)]
 
 
-def sweep(src, dst, table, init, reset, reverse, conj, extra=None):
+def sweep(src, dst, table, init, reset, reverse, conj):
     halves = src.shape[0] // 2
     span = src.shape[1] // SUB
     rate_re = [jnp.broadcast_to(table[h : h + 1, :], (SUB, LANES)) for h in range(halves)]
@@ -217,9 +217,8 @@
         rate_im = [-r for r in rate_im]
     base = lax.broadcasted_iota(jnp.int32, (SUB, LANES), 0) * span - reset
 
-    def body(step, carry):
+    def body(step, state):
         j = span - 1 - step if reverse else step
-        state, sums = carry
         drop = base == -j
         at = pl.ds(j, SUB, stride=span)
         new_re, new_im = [], []
@@ -233,14 +232,9 @@
         if dst is not None:
             for k in range(2 * halves):
                 dst[k, at, :] = state[k]
-        if extra is not None:
-            sums = extra(at, state, sums)
-        return state, sums
-
-    sums = ()
-    if extra is not None:
-        sums = tuple(jnp.zeros((SUB, LANES), F32) for _ in range(2 * halves))
-    return lax.fori_loop(0, span, body, (init, sums), unroll=8)
+        return state
+
+    return lax.fori_loop(0, span, body, init, unroll=8)
 
 
 def zeros_state(halves):
@@ -460,7 +454,7 @@
         drive.flush(i, 2)
     fwd, bwd = local_resets(start, rows)
     reset = bwd if reverse else fwd
-    ends, _ = sweep(drive.ref, None, table[layer], zeros_state(2), reset, reverse, False)
+    ends = sweep(drive.ref, None, table[layer], zeros_state(2), reset, reverse, False)
     emit_ends(out, ends_out, ends, table[layer], reset, rows // SUB, reverse, False)
 
 
@@ -524,6 +518,15 @@
         cols = pl.ds(pl.multiple_of((mp ^ k) * LANES, LANES), LANES)
         for i in range(count):
             maps.ref[i, :, cols] = piece()[i * deep : (i + 1) * deep, :]
+
+
+def gather_cotangent(copies, begin, got1, got2, got3, cot, full):
+    begin()
+    mp, _ = place()
+    rows = full.ref.shape[0]
+    own = cot()[pl.ds(pl.multiple_of(mp * rows, SUB), rows), :].astype(BF16)
+    for k, block in enumerate((own, got1()[...], got2()[...], got3()[...])):
+        full.ref[:, pl.ds(pl.multiple_of((mp ^ k) * LANES, LANES), LANES)] = block
 
 
 def fetch_maps(copies, far, near, order=(0, 1, 2)):
@@ -579,8 +582,7 @@
         ref.ref[i, :, :] = pack[mp ^ k, :, :]
 
 
-def weight_grads(copies, begin, sent, dv, dg, states, dml, sums, keep, send, pack):
-    begin()
+def weight_share(sent, dv, dg, states, dml, sums, pack):
     width = sent.dst.shape[1]
     parts = pack.shape[0]
     both = jnp.concatenate([dv()[...], dg()[...]], axis=1)
@@ -593,12 +595,15 @@
         cols = slice(j * LANES, (j + 1) * LANES)
         rows = jnp.concatenate([sums[:, cols], jnp.zeros((8, LANES), F32)], axis=0)
         pack[j, 3 * width : 3 * width + 16, :] = rows.astype(pack.dtype)
+
+
+def weight_grads(copies, begin, sent, dv, dg, states, dml, sums, keep, send, pack):
+    begin()
+    weight_share(sent, dv, dg, states, dml, sums, pack)
     share_out(keep, send, pack, copies)
 
 
-def input_grads(layer, copies, begin, slow, dlow, prods, weight, keep, send, pack, held, maps):
-    begin()
-    weight = Later(copies, [(weight.at[layer], maps)], maps)
+def input_share(base, copies, slow, dlow, prods, weight, pack, held):
     width = slow.dst.shape[1]
     held[...] = dot_tn(slow()[...], dlow()[...])
     half = width // 2
@@ -607,7 +612,7 @@
     for top in range(0, width, size):
         rows = slice(top, top + size)
         grad = held[rows, :]
-        put(pack, rows, grad)
+        put(pack, slice(base + top, base + top + size), grad)
         grad_re, grad_im = grad[:, :half], grad[:, half:]
         w = weight()[rows, :].astype(F32)
         w_re, w_im = w[:, :half], w[:, half:]
@@ -621,7 +626,22 @@
         rows += [y_re[:, cols]]
     tile = jnp.concatenate(rows + [jnp.zeros((10, LANES), F32)], axis=0).astype(pack.dtype)
     for j in range(pack.shape[0]):
-        pack[j, width : width + 16, :] = tile
+        pack[j, base + width : base + width + 16, :] = tile
+
+
+def input_grads(layer, copies, begin, slow, dlow, prods, weight, keep, send, pack, held, maps):
+    begin()
+    weight = Later(copies, [(weight.at[layer], maps)], maps)
+    input_share(0, copies, slow, dlow, prods, weight, pack, held)
+    share_out(keep, send, pack, copies)
+
+
+def both_grads(layer, copies, begin, sent, dv, dg, states, dml, sums, slow, dlow, prods, weight, keep, send,
+               pack, held, maps):
+    begin()
+    weight = Later(copies, [(weight.at[layer + 1], maps)], maps)
+    weight_share(sent, dv, dg, states, dml, sums, pack)
+    input_share(3 * sent.dst.shape[1] + 16, copies, slow, dlow, prods, weight, pack, held)
     share_out(keep, send, pack, copies)
 
 
@@ -652,9 +672,9 @@
         )
         states_low_out.ref[at, :] = states_low
         sent.ref[at, :] = sent_low
-        put(slope_out.ref, at, slope)
-        put(sig_out.ref, at, sig)
-        put(part_out.ref, at, gated * (1.0 - sig))
+        slope_out.ref[at, :] = slope.astype(BF16)
+        sig_out.ref[at, :] = sig.astype(BF16)
+        part_out.ref[at, :] = (gated * (1.0 - sig)).astype(BF16)
         new = x + gated
         put(new_h.ref, at, new)
         one = one + jnp.sum(new, axis=0, keepdims=True)
@@ -664,22 +684,18 @@
     add_chunk(new_mom, one, two)
 
 
-def turn(layer, copies, begin, start, gathered, mom, table, ends, norms, prm, drive, h, far_maps,
-         got1, got2, got3, cot,
-         ds, out, ends_out, h_far, states_low_out, full_cot, sent, dv, dg, dml, sums_out, r0, r1, r2, r3,
-         maps, states, new_h, cot_blocks):
+def turn(layer, copies, begin, start, gathered, mom, table, ends, norms, prm, drive, h, far_maps, cot,
+         ds, out, ends_out, h_far, states_low_out, sent, dv, dg, dml, sums_out, r0, r1, r2, r3,
+         maps, states, new_h):
     mp, _ = place()
     rows = states.shape[1]
     ready = fetch_maps(copies, far_maps, maps)
-    own_cot = Later(copies, [(own_rows(cot, rows), cot_blocks.at[mp])], cot_blocks)
+    begin()
     copies.flush(h.ref, h_far)
     reverse = layer % 2 == 1
     tab = table()[layer]
     init, reset = resume(start, rows, gathered(), mom(), tab, ends(), reverse, False)
     sweep(drive(), states, tab, init, reset, reverse, False)
-    for k, got in ((1, got1), (2, got2), (3, got3)):
-        cot_blocks[mp ^ k, :, :] = got()[...].astype(F32)
-    own_cot()
     norms, prm = norms(), prm()
     sums = [0.0, 0.0, 0.0]
     for i, at in enumerate(chunks(rows, 2)):
@@ -689,9 +705,8 @@
         states_low_out.ref[at, :] = states_low
         sent.ref[at, :] = sent_low
         put(new_h, at, x + gated)
-        g = cat(cot_blocks, at)
-        full_cot.ref[at, :] = g.astype(BF16)
-        for o in (states_low_out, sent, full_cot):
+        g = cot.part(i)[at, :].astype(F32)
+        for o in (states_low_out, sent):
             o.flush(i, 2)
         sums = back_chunk(i, at, g, sig, gated * (1.0 - sig), lambda: scaled, lambda: slope,
                           ready, (dv, dg, dml, ds), sums)
@@ -707,15 +722,15 @@
     reverse = layer % 2 == 0
     fwd, bwd = local_resets(start, rows)
     reset = bwd if reverse else fwd
-    ends, _ = sweep(ds, None, tab, zeros_state(2), reset, reverse, True)
+    ends = sweep(ds, None, tab, zeros_state(2), reset, reverse, True)
     emit_ends(out, ends_out, ends, tab, reset, rows // SUB, reverse, True)
 
 
 def back_first(layer, total_tokens, copies, begin, start, back, norms1, table, prm, u, norms,
                slow1, sig, part, slope, slow, far_maps, g_out, ds, out, ends_out, tile_out, dv, dg, dml, sums_out,
                maps):
-    begin()
-    maps = fetch_maps(copies, far_maps, maps, (1, 2, 0))
+    begin((slow1, 0), (sig, 0), (part, 0))
+    ready = fetch_maps(copies, far_maps, maps, (1, 2))
     rows = ds.ref.shape[1]
     tile = total_of(back())
     tile_out.ref[...] = tile
@@ -730,10 +745,15 @@
     sums = [0.0, 0.0, 0.0]
     for i, at in enumerate(chunks(rows, 2)):
         g = cat(u(), at) - m_one - slow1.part(i)[at, :].astype(F32) * m_two
+        if i == 0:
+            begin((slope, 0))
+            ready.update(fetch_maps(copies, far_maps, maps, (0,)))
+            begin((slow, 0), (slow1, 1), (sig, 1), (part, 1), (slope, 1), (slow, 1))
         put(g_out.ref, at, g)
-        sums = back_chunk(i, at, g, cat(sig.part(i), at), cat(part.part(i), at),
-                          lambda: slow.part(i)[at, :].astype(F32),
-                          lambda: cat(slope.part(i), at), maps, (dv, dg, dml, ds), sums)
+        g_out.flush(i, 2)
+        low = lambda x: x.part(i)[at, :].astype(F32)
+        sums = back_chunk(i, at, g, low(sig), low(part), lambda: low(slow), lambda: low(slope),
+                          ready, (dv, dg, dml, ds), sums)
     sums_rows(sums_out, sums)
     adjoint_start(layer, start, table()[layer], ds.ref, out, ends_out)
 
@@ -741,30 +761,33 @@
 def back_second(layer, copies, begin, start, gathered, mom, table, ends, norms, prm, ds, states_low, g, dml, h,
                 weight, *refs):
     if layer == 0:
-        back, prods, dlow, u0, u1, u2, u3, adj, states, maps, u_ref = refs
+        back, prods, dlow, u0, u1, u2, u3, adj, maps, u_ref = refs
     else:
-        back, u_out, prods, dlow, adj, states, maps = refs
+        back, u_out, prods, dlow, adj, maps = refs
         u_ref = u_out.ref
-    begin()
+        begin(g)
+    begin(states_low)
     weight = Later(copies, [(weight.at[layer], maps)], maps)
+    begin((dml, 0), (h, 0))
+    if layer == 0:
+        begin((g, 0), (g, 1))
+    begin((dml, 1), (h, 1))
     rows = adj.shape[1]
     reverse = layer % 2 == 0
     tab = table()[layer]
     init, reset = resume(start, rows, gathered(), mom(), tab, ends(), reverse, True)
-    for at in chunks(rows, 8):
-        put(states, at, states_low()[at, :].astype(F32))
-
-    def extra(at, a, sums):
-        new = []
-        for h_ in range(2):
-            re, im = a[h_], a[2 + h_]
-            sre, sim = states[h_, at, :], states[2 + h_, at, :]
-            new.append(re * sre + im * sim)
-            new.append(im * sre - re * sim)
-        return tuple(s + n for s, n in zip(sums, new, strict=True))
-
-    _, sums = sweep(ds(), adj, tab, init, reset, reverse, True, extra)
-    flat = [jnp.sum(s, axis=0, keepdims=True) for s in sums]
+    sweep(ds(), adj, tab, init, reset, reverse, True)
+    half = adj.shape[0] // 2 * LANES
+    prod_re = prod_im = jnp.zeros((SUB, half), F32)
+    for at in chunks(rows, 16):
+        a, s = cat(adj, at), states_low()[at, :].astype(F32)
+        a_re, a_im, s_re, s_im = a[:, :half], a[:, half:], s[:, :half], s[:, half:]
+        re, im = a_re * s_re + a_im * s_im, a_im * s_re - a_re * s_im
+        for top in range(0, re.shape[0], SUB):
+            prod_re = prod_re + re[top : top + SUB, :]
+            prod_im = prod_im + im[top : top + SUB, :]
+    flat = [jnp.sum(x, axis=0, keepdims=True) for x in (prod_re, prod_im)]
+    flat = [x[:, h_ * LANES : (h_ + 1) * LANES] for h_ in range(2) for x in flat]
     prods.ref[...] = jnp.concatenate(flat + [jnp.zeros((8 - len(flat), LANES), F32)], axis=0)
     prods.flush()
     gamma = lanes(tab[12:14, :])
@@ -780,7 +803,7 @@
         dlow.flush(i, 2)
         dscaled = dot_nt(low, weight()[...]) + dml.part(i)[at, :].astype(F32) * skip
         normed = (cat(h.part(i), at) - mean) * inverse
-        own = g()[at, :].astype(F32) if layer == 1 else cat(g(), at)
+        own = g()[at, :].astype(F32) if layer == 1 else cat(g.part(i), at)
         put(u_ref, at, own + factor * dscaled)
         one = one + jnp.sum(dscaled, axis=0, keepdims=True)
         two = two + jnp.sum(dscaled * normed, axis=0, keepdims=True)
@@ -843,43 +866,58 @@
         mine.ref[at, :] = (keep[0, at, :].astype(F32) + got[0, at, :].astype(F32)).astype(mine.ref.dtype)
 
 
-def four_sum(copies, begin, *refs):
+def four_sum(first, order, copies, begin, *refs):
     *ins, out = refs
     out = out.ref
-    top = 0
-    for mine, got in zip(ins[::2], ins[1::2], strict=True):
+    count, piece = out.shape[0], out.shape[1]
+    tops = {True: 0, False: 0}
+
+    def place_of(top, is_input):
+        size = first if is_input else piece - first
+        base = 0 if is_input else first
+        return top // size, base + top % size
+
+    for mine, got, spans in zip(ins[::2], ins[1::2], order, strict=True):
         mine, got = mine(), got()
-        rows = mine.shape[0]
-        for at in chunks(rows, rows // 16):
-            total = mine[at, :].astype(F32) + got[at, :].astype(F32)
-            out[top + at.start : top + at.stop, :] = total.astype(out.dtype)
-        top += rows
-    if top < out.shape[0]:
-        out[top:, :] = jnp.zeros((out.shape[0] - top, out.shape[1]), out.dtype)
-
-
-def piece_sum(copies, begin, pieces, out):
+        row = 0
+        for rows, is_input in spans:
+            for _ in range(rows // 16):
+                d, top = place_of(tops[is_input], is_input)
+                at = slice(row, row + 16)
+                total = mine[at, :].astype(F32) + got[at, :].astype(F32)
+                out[d, top : top + 16, :] = total.astype(out.dtype)
+                tops[is_input] += 16
+                row += 16
+    for is_input in (True, False):
+        size = first if is_input else piece - first
+        while tops[is_input] < count * size:
+            d, top = place_of(tops[is_input], is_input)
+            out[d, top : top + 16, :] = jnp.zeros((16, out.shape[2]), out.dtype)
+            tops[is_input] += 16
+
+
+def piece_sum(copies, begin, pieces, first, rest):
     pieces = pieces()
     count, rows = pieces.shape[0], pieces.shape[1]
+    split = first.ref.shape[1]
     for at in chunks(rows, rows // 16):
         total = pieces[0, at, :].astype(F32)
         for d in range(1, count):
             total = total + pieces[d, at, :].astype(F32)
-        low = total.astype(out.ref.dtype)
+        low = total.astype(first.ref.dtype)
+        out, top = (first.ref, 0) if at.start < split else (rest.ref, split)
         for d in range(count):
-            out.ref[d, at, :] = low
-
-
-def hand_out(features, copies, begin, decay, phase, full0,
-             in_own, o_grad, skip_grad, v_grad, g_grad, vb, gb, d_grad, p_grad, s_grad):
-    begin()
-    in_rows = features + 16
-    full0 = full0()
+            out[d, at.start - top : at.stop - top, :] = low
+
+
+def hand_out(features, copies, begin, decay, phase, full_in, full,
+             o_grad, skip_grad, v_grad, g_grad, vb, gb, d_grad, p_grad, s_grad):
+    begin()
+    in_rows, vgo_rows = features + 16, 3 * features + 16
+    full, full_in = full(), full_in()
+    decay, phase = decay(), phase()
     for layer in range(2):
-        top = layer * in_rows
-        in_own.ref[layer, :, :] = full0[top : top + features, :]
-    decay, phase = decay(), phase()
-    for layer, full, top in ((0, full0, 2 * in_rows), (1, full0, 2 * in_rows + 3 * features + 16)):
+        top = layer * vgo_rows
         for i, out in enumerate((v_grad, g_grad, o_grad)):
             out.ref[layer, :, :] = full[top + i * features : top + (i + 1) * features, :].astype(F32)
             copies.flush(out.ref.at[layer], out.dst.at[layer])
@@ -891,7 +929,7 @@
         gb.ref[row, :] = vecs[1:2, :]
         skip_grad.ref[row, :] = vecs[2:3, :]
         top = layer * in_rows + features
-        tile = full0[top : top + 16, :].astype(F32)
+        tile = full_in[top : top + 16, :].astype(F32)
         for h in range(2):
             cols = slice(h * LANES, (h + 1) * LANES)
             d_grad.ref[row, cols] = -jnp.exp(decay[row, cols]) * tile[3 * h : 3 * h + 1, :]
@@ -899,14 +937,15 @@
             s_grad.ref[row, cols] = tile[3 * h + 2 : 3 * h + 3, :]
 
 
-def input_kernel(copies, begin, p0, p1, p2, p3, out):
+def input_kernel(features, copies, begin, p0, p1, p2, p3, out):
     begin()
     mp, _ = place()
     for k, piece in enumerate((p0, p1, p2, p3)):
         cols = pl.ds(pl.multiple_of((mp ^ k) * LANES, LANES), LANES)
         piece = piece()
         for layer in range(out.ref.shape[0]):
-            out.ref[layer, :, cols] = piece[layer].astype(F32)
+            top = layer * (features + 16)
+            out.ref[layer, :, cols] = piece[top : top + features, :].astype(F32)
 
 
 def shape(dims, dtype=F32):
@@ -988,7 +1027,7 @@
     )
     table = Near(table)
     got_h = [Near(x) for x in swap(sends)]
-    mom0 = Near(every(after(mom_out, got_h[1].array)))
+    mom0 = Near(every(after(mom_out, *[g.array for g in got_h])))
     h0, prm = call(
         gather_block,
         [near_blocks, Near(shape((parts, 16, width)))],
@@ -1013,8 +1052,7 @@
     norms0 = Near(norms0)
     h1, mom_out, h0, states0, sent0, slope0, sig0, part0 = call(
         functools.partial(mix_first, 0),
-        [near_blocks, near_sums, Raw(blocks), wide_low, wide_low,
-         blocks, blocks, blocks],
+        [near_blocks, near_sums, Raw(blocks)] + [wide_low] * 5,
         [v_blocks, maps],
         start_offsets, got, mom0, table, Near(ends0), norms0, prm, Near(drive0), h0, Raw(full0),
         scalars=1,
@@ -1022,7 +1060,6 @@
     h1 = Near(h1)
     sends = call(pack_block, [low_block] * 3, [], after(cotangent, got.array))
     mom1 = Near(after(every(mom_out), *sends))
-    got_cot = [Near(x) for x in swap(sends)]
     w1 = after(packs[1], got.array)
     (full1,) = call(assemble, [all_maps], [], w1, *[Near(w) for w in spread(w1, mom1.array)])
     drive1, norms1, ends_all, ends1, slow1 = call(
@@ -1032,7 +1069,9 @@
         start_offsets, mom1, prm, table, h1, Raw(input_map),
         scalars=1,
     )
-    got = Near(after(every(ends_all), full1))
+    got_cot = [Near(x) for x in swap([after(s, norms1) for s in sends])]
+    (cot,) = call(gather_cotangent, [wide_low], [], *got_cot, after(cotangent, full1))
+    got = Near(after(every(ends_all), full1, cot))
     norms1 = Near(norms1)
     vgo_rows, in_rows = 3 * features + 16, features + 16
 
@@ -1043,14 +1082,16 @@
     vgo_half = Near(shape((2, vgo_rows, width), BF16))
     in_half = Near(shape((2, in_rows, width), BF16))
     vgo_pack = pltpu.VMEM((parts, vgo_rows, width), BF16)
+    both_half = Near(shape((2, vgo_rows + in_rows, width), BF16))
+    both_pack = pltpu.VMEM((parts, vgo_rows + in_rows, width), BF16)
     in_pack = pltpu.VMEM((parts, in_rows, width), BF16)
     in_room = [in_pack, pltpu.VMEM((features, features), F32), one_map]
-    ds1, ends_all, back_ends1, h1, states1, cot, sent1, dv, dg, dml1, sums, *res = call(
+    ds1, ends_all, back_ends1, h1, states1, sent1, dv, dg, dml1, sums, *res = call(
         functools.partial(turn, 1),
-        [near_blocks, near_every, near_ends, Raw(blocks)] + [wide_low] * 6 + [near_norms.array, shape(one_block)]
+        [near_blocks, near_every, near_ends, Raw(blocks)] + [wide_low] * 5 + [near_norms.array, shape(one_block)]
         + [low_block] * 3,
-        [maps, v_blocks, v_blocks, v_blocks],
-        start_offsets, got, mom0, table, Near(ends1), norms1, prm, Near(drive1), h1, Raw(full1), *got_cot, Raw(cotangent),
+        [maps, v_blocks, v_blocks],
+        start_offsets, got, mom0, table, Near(ends1), norms1, prm, Near(drive1), h1, Raw(full1), Halves(cot),
         scalars=1,
     )
     got = Near(every(ends_all))
@@ -1062,23 +1103,20 @@
     got = Near(after(got.array, keep1))
     back_out, u1, prods, dlow = call(
         functools.partial(back_second, 1),
-        [near_sums, near_blocks, Near(shape((8, LANES))), Near(wide_low)],
-        [v_blocks, v_blocks, one_map],
+        [near_sums, near_blocks, shape((8, LANES)), wide_low],
+        [v_blocks, one_map],
         start_offsets, got, mom0, table, Near(back_ends1), norms1, prm, Near(ds1), states1, cot, Halves(dml1),
         Halves(h1), Raw(input_map),
         scalars=1,
     )
     back1 = Near(every(back_out))
-    in_keep1, in_send1 = call(
-        functools.partial(input_grads, 1), [in_half, in_half], in_room, slow1, Near(dlow), Near(prods), Raw(input_map)
-    )
-    mine1, other1 = pair_share(keep1, send1)
-    in_send1 = after(in_send1, back1.array)
-    back1 = Near(after(back1.array, in_keep1, mine1))
+    late1 = (slow1, dlow, prods)
+    mine1, other1 = pair_share(after(keep1, back_out), send1)
+    back1 = Near(after(back1.array, mine1))
     far1 = hop(other1, 2)
     g0, ds0, ends_all, back_ends0, tile1, dv, dg, dml0, sums = call(
         functools.partial(back_first, 0, tokens),
-        [near_blocks, near_blocks, near_every, near_ends, Near(shape((2 * parts, LANES)))] + [wide_low] * 3
+        [blocks, near_blocks, near_every, near_ends, Near(shape((2 * parts, LANES)))] + [wide_low] * 3
         + [near_norms.array],
         [maps],
         start_offsets, back1, norms1, table, prm, Near(u1), norms0,
@@ -1087,25 +1125,25 @@
     )
     got = Near(every(after(ends_all, far1)))
     keep0, send0 = call(
-        weight_grads, [vgo_half, vgo_half], [vgo_pack], sent0, dv, dg, states0, dml0, sums
-    )
-    in_mine1, in_other1 = pair_share(in_keep1, in_send1)
-    in_far1 = hop(in_other1, 2)
+        functools.partial(both_grads, 0), [both_half, both_half], [both_pack] + in_room[1:],
+        sent0, dv, dg, states0, dml0, sums, *late1, Raw(input_map),
+    )
     send0 = after(send0, got.array)
-    got = Near(after(got.array, keep0, in_mine1))
+    got = Near(after(got.array, keep0))
     back_out, prods, dlow, *us = call(
         functools.partial(back_second, 0),
         [near_sums, Near(shape((8, LANES))), Near(wide_low), Near(shape(one_block))] + [near_low] * 3,
-        [v_blocks, v_blocks, one_map, v_blocks],
-        start_offsets, got, mom0, table, Near(back_ends0), norms0, prm, Near(ds0), states0, Near(g0), Halves(dml0),
+        [v_blocks, one_map, v_blocks],
+        start_offsets, got, mom0, table, Near(back_ends0), norms0, prm, Near(ds0), states0, Halves(g0), Halves(dml0),
         Halves(h0), Raw(input_map),
         scalars=1,
     )
+    mine0, other0 = pair_share(keep0, send0)
+    far0 = hop(other0, 2)
+    prods = after(prods, mine0)
     in_keep0, in_send0 = call(
         functools.partial(input_grads, 0), [in_half, in_half], in_room, slow0, Near(dlow), Near(prods), Raw(input_map)
     )
-    mine0, other0 = pair_share(keep0, send0)
-    far0 = hop(other0, 2)
     us = (us[0], *swap([after(u, in_send0) for u in us[1:]]))
     back0 = Near(every(after(back_out, in_send0, mine0)))
     in_mine0, in_other0 = pair_share(in_keep0, in_send0)
@@ -1118,30 +1156,37 @@
         norms0, back0, Near(tile1), *[Near(u) for u in us], Raw(stream),
     )
 
-    full_rows = 2 * (vgo_rows + in_rows)
     unit = 16 * count_dp
-    padded = -(-full_rows // unit) * unit
-    (own0,) = call(
-        four_sum, [Near(shape((padded, width), BF16))], [],
-        Near(in_mine0), Near(in_far0), Near(in_mine1), Near(in_far1), Near(mine0), Near(far0), Near(mine1), Near(far1),
-    )
-    split = (count_dp, padded // count_dp, width)
-    pieces = lax.all_to_all(after(own0, back0.array).reshape(split), "dp", 0, 0)
-    (copied,) = call(piece_sum, [Near(shape(split, BF16))], [], Near(pieces))
-    copied = after(copied, stream_grad)
-    result = [res[0], *swap([after(r, copied) for r in res[1:]])]
+    in_piece = -(-2 * in_rows // unit) * 16
+    piece = in_piece + -(-2 * vgo_rows // unit) * 16
+    order = (((in_rows, True),), ((vgo_rows, False), (in_rows, True)), ((vgo_rows, False),))
+    (own,) = call(
+        functools.partial(four_sum, in_piece, order), [Near(shape((count_dp, piece, width), BF16))], [],
+        Near(in_mine0), Near(in_far0), Near(mine0), Near(far0), Near(mine1), Near(far1),
+    )
+    pieces = lax.all_to_all(after(own, back0.array), "dp", 0, 0)
+    first, rest = call(
+        piece_sum,
+        [Near(shape((count_dp, n, width), BF16)) for n in (in_piece, piece - in_piece)],
+        [],
+        Near(pieces),
+    )
+    result = [res[0], *swap([after(r, own) for r in res[1:]])]
     (result,) = call(result_kernel, [shape((block, width))], [], res[0], *[Near(r) for r in result[1:]])
-    full0 = lax.all_to_all(copied, "dp", 0, 0).reshape(padded, width)
-    full0 = after(full0, result)
+    full_in = lax.all_to_all(after(first, stream_grad, result), "dp", 0, 0).reshape(-1, width)
+    rest = after(rest, full_in)
+    (input_grad,) = call(
+        functools.partial(input_kernel, features), [shape((layers, features, features))], [],
+        Near(full_in), *[Near(x) for x in spread(full_in)],
+    )
+    full = lax.all_to_all(rest, "dp", 0, 0).reshape(-1, width)
+    full = after(full, input_grad)
     mat, vec, state = shape((layers, features, width)), shape((layers, width)), shape(decay_log.shape)
-    in_own, o_grad, skip_grad, v_grad, g_grad, vb, gb, d_grad, p_grad, s_grad = call(
+    o_grad, skip_grad, v_grad, g_grad, vb, gb, d_grad, p_grad, s_grad = call(
         functools.partial(hand_out, features),
-        [Near(shape((layers, features, width), BF16)), mat, vec, mat, mat, vec, vec, state, state, state],
+        [mat, vec, mat, mat, vec, vec, state, state, state],
         [],
-        decay_log, phase_log, Near(full0),
-    )
-    (input_grad,) = call(
-        input_kernel, [shape((layers, features, features))], [], Near(in_own), *[Near(x) for x in spread(in_own)]
+        decay_log, phase_log, Near(full_in), Near(full),
     )
     return (
         result, stream_grad, gain_grad, shift_grad, input_grad, d_grad, p_grad, s_grad,

time: 244 us -> 224 us (0.918)
  waiting for transfers between devices: 112 us -> 77.6 us
  blocking collectives: 0 us -> 26.5 us
  Pallas kernels: 75.1 us -> 68 us
    all_to_all x0 -> x2, blocking collectives: none -> 26.5 us  [the longest x1 14 us: on_device(): lax.all_to_all(after(first, stream_grad, result), 'dp', 0, 0)]
    all_to_all x2, waiting for transfers between devices: 32.5 us -> 20.7 us  [the longest x1 11.4 us: on_device(): pieces = lax.all_to_all(after(own, back0.array), 'dp', 0, 0)]
    ppermute x29 -> x27, waiting for transfers between devices: 36.2 us -> 24.9 us  [hop(): return lax.ppermute(x, 'mp', [(i, i ^ k) for i in range(count)])]
    all_to_all x8 -> x7, waiting for transfers between devices: 43.2 us -> 32 us  [every(): return lax.all_to_all(x, AXES, 0, 0)]
    pallas_call x27 -> x26, Pallas kernels: 75.1 us -> 68 us  [call(): return made_call(max(used[0], 1))(*plain)]
    all_to_all x8 -> x7, starting transfers between devices: 25.3 us -> 22.9 us  [every(): return lax.all_to_all(x, AXES, 0, 0)]
    ppermute x29 -> x27, starting transfers between devices: 16.1 us -> 15.6 us  [hop(): return lax.ppermute(x, 'mp', [(i, i ^ k) for i in range(count)])]
  transfers between devices with their start and end apart: 39 -> 36, of which waited for: 23 -> 20; matrix products, arithmetic and copies ran while one was open for 0% -> 0% of each run, Pallas kernels for 24% -> 24%
where the time goes in v3:
time: 224 us; the launch traced here: 223 us
  waiting for transfers between devices  77.6 us (35%)
  Pallas kernels  68 us (30%)
  starting transfers between devices  46.7 us (21%)
  blocking collectives  26.5 us (12%)
  local copies, waits for them, and re-layouts  2.42 us (1%)
    pallas_call x26, Pallas kernels, call(): return made_call(max(used[0], 1))(*plain)  68 us
    all_to_all x7, waiting for transfers between devices, every(): return lax.all_to_all(x, AXES, 0, 0)  32 us
    ppermute x27, waiting for transfers between devices, hop(): return lax.ppermute(x, 'mp', [(i, i ^ k) for i in range(count)])  24.9 us
    all_to_all x7, starting transfers between devices, every(): return lax.all_to_all(x, AXES, 0, 0)  22.9 us
    ppermute x27, starting transfers between devices, hop(): return lax.ppermute(x, 'mp', [(i, i ^ k) for i in range(count)])  15.6 us
    all_to_all x1, blocking collectives, on_device(): lax.all_to_all(after(first, stream_grad, result), 'dp', 0, 0)  14 us
    all_to_all x1, blocking collectives, every(): return lax.all_to_all(x, AXES, 0, 0)  12.5 us
    all_to_all x1, waiting for transfers between devices, on_device(): pieces = lax.all_to_all(after(own, back0.array), 'dp', 0, 0)  11.4 us
  transfers between devices with their start and end apart: 36, of which 20 were waited for; matrix products, arithmetic and copies ran while one was open for 0% of the time, Pallas kernels for 24%

profile of v3, /device:TPU:0, one launch (start us, length us, event | category | flops | bytes accessed | tf_op | source)
XLA Modules:
  0.0 223.2 jit_solution(2043413668100138528)
XLA Ops:
  15.3 4.9 %all-to-all-start = ((f32[32,4,128]{2,1,0:T(4,128)}), f32[32,4,128]{2,1,0:T(4,128)S(1)}, u32[]{:S(2)}, u32[]{:S(2)}) async-start(f32[32,4,128]{2,1,0:T(4,128)} %get-tuple-element.142), calls=%async_computation | async-start | bytes 131072 | tf_op jit(solution)/shard_map/all_to_all | solution.py:956
  20.6 7.1 %all-to-all-done.refs_1_.refs_2_ = f32[32,4,128]{2,1,0:T(4,128)S(1)} async-done(((f32[32,4,128]{2,1,0:T(4,128)}), f32[32,4,128]{2,1,0:T(4,128)S(1)}, u32[]{:S(2)}, u32[]{:S(2)}) %all-to-all-start) | async-done | bytes 65568 | tf_op jit(solution)/shard_map/all_to_all | solution.py:956
  31.8 3.2 %all-to-all-start.1 = ((f32[32,4,128]{2,1,0:T(4,128)}), f32[32,4,128]{2,1,0:T(4,128)S(1)}, u32[]{:S(2)}, u32[]{:S(2)}) async-start(f32[32,4,128]{2,1,0:T(4,128)} %get-tuple-element.146), calls=%async_computation.1 | async-start | bytes 131072 | tf_op jit(solution)/shard_map/all_to_all | solution.py:956
  35.0 3.5 %shard_map.258.refs_9_.refs_12_ = bf16[3,512,512]{2,1,0:T(8,128)(2,1)} custom-call(bf16[1536,128]{1,0:T(8,128)(2,1)} %get-tuple-element.148.refs_0_, bf16[1536,128]{1,0:T(8,128)(2,1)S(1)} %collective-permute-done.3.refs_1_, bf16[1536,128]{1,0:T(8,128)(2,1)S(1)} %collective-permute-done.4.refs_2_, bf16[1536,128]{1,0:T(8,128)(2,1)} %collective-permute-done.5.refs_3_), custom_call_target="tpu_custom_call" | custom-call | tf_op jit(solution)/shard_map/pallas_call | solution.py:171
  38.5 3.9 %all-to-all-done.1.refs_1_ = f32[32,4,128]{2,1,0:T(4,128)S(1)} async-done(((f32[32,4,128]{2,1,0:T(4,128)}), f32[32,4,128]{2,1,0:T(4,128)S(1)}, u32[]{:S(2)}, u32[]{:S(2)}) %all-to-all-start.1) | async-done | bytes 65568 | tf_op jit(solution)/shard_map/all_to_all | solution.py:956
  42.8 5.4 %shard_map.259 = (f32[4,512,128]{2,1,0:T(8,128)S(1)}, f32[32,8,128]{2,1,0:T(8,128)}, f32[4,512,128]{2,1,0:T(8,128)}, bf16[512,512]{1,0:T(8,128)(2,1)}, bf16[512,...) custom-call(s32[1]{0:T(128)S(6)} %copy.29.refs_0_, ...), custom_call_target="tpu_custom_call" | custom-call | tf_op jit(solution)/shard_map/pallas_call | solution.py:171
  53.2 5.9 %all-to-all-done.2.refs_1_ = f32[32,8,128]{2,1,0:T(8,128)S(1)} async-done(((f32[32,8,128]{2,1,0:T(8,128)}), f32[32,8,128]{2,1,0:T(8,128)S(1)}, u32[]{:S(2)}, u32[]{:S(2)}) %all-to-all-start.2) | async-done | bytes 131104 | tf_op jit(solution)/shard_map/all_to_all | solution.py:956
  59.3 3.4 %shard_map.261 = (f32[4,512,128]{2,1,0:T(8,128)S(1)}, f32[8,512]{1,0:T(8,128)S(1)}, f32[32,4,128]{2,1,0:T(4,128)}, f32[4,8,128]{2,1,0:T(8,128)S(1)}, bf16[512,512]{1,0:T(8,128)(2,1)}) custom-call(s32[1]{0:T(128)S(6)} %copy.29.refs_0_, f32[32,8,128]{2,1,0:T(8,128)S(1)} %all-to-all-done.2.refs_1_, ...), custom_call_target="tpu_custom_call" | custom-call | tf_op jit(solution)/shard_map/pallas_call | solution.py:171
  67.3 3.5 %shard_map.262.refs_9_ = bf16[3,512,512]{2,1,0:T(8,128)(2,1)} custom-call(bf16[1536,128]{1,0:T(8,128)(2,1)} %get-tuple-element.163.refs_0_, bf16[1536,128]{1,0:T(8,128)(2,1)S(1)} %collective-permute-done.6.refs_1_, bf16[1536,128]{1,0:T(8,128)(2,1)} %collective-permute-done.7.refs_2_, bf16[1536,128]{1,0:T(8,128)(2,1)S(1)} %collective-permute-done.8.refs_3_), custom_call_target="tpu_custom_call" | custom-call | tf_op jit(solution)/shard_map/pallas_call | solution.py:171
  74.6 7.4 %shard_map.264 = (f32[4,512,128]{2,1,0:T(8,128)S(1)}, f32[32,4,128]{2,1,0:T(4,128)}, f32[4,8,128]{2,1,0:T(8,128)S(1)}, f32[4,512,128]{2,1,0:T(8,128)}, bf16[512,...) custom-call(s32[1]{0:T(128)S(6)} %copy.29.refs_0_, ...), custom_call_target="tpu_custom_call" | custom-call | tf_op jit(solution)/shard_map/pallas_call | solution.py:171
  82.0 4.0 %all-to-all-start.4 = ((f32[32,4,128]{2,1,0:T(4,128)}), f32[32,4,128]{2,1,0:T(4,128)S(1)}, u32[]{:S(2)}, u32[]{:S(2)}) async-start(f32[32,4,128]{2,1,0:T(4,128)} %get-tuple-element.176), calls=%async_computation.4 | async-start | bytes 131072 | tf_op jit(solution)/shard_map/all_to_all | solution.py:956
  88.8 4.6 %all-to-all-done.4.refs_1_ = f32[32,4,128]{2,1,0:T(4,128)S(1)} async-done(((f32[32,4,128]{2,1,0:T(4,128)}), f32[32,4,128]{2,1,0:T(4,128)S(1)}, u32[]{:S(2)}, u32[]{:S(2)}) %all-to-all-start.4) | async-done | bytes 65568 | tf_op jit(solution)/shard_map/all_to_all | solution.py:956
  97.4 12.5 %all_to_all.55.refs_1_ = f32[32,8,128]{2,1,0:T(8,128)S(1)} all-to-all(f32[32,8,128]{2,1,0:T(8,128)S(1)} %get-tuple-element.189), channel_id=1, replica_groups=mesh['dp'=8,'mp'=4] {'dp','mp'}, dimensions={0} | all-to-all | bytes 262144 | tf_op jit(solution)/shard_map/all_to_all | solution.py:956
  109.9 5.9 %shard_map.268 = (f32[4,512,128]{2,1,0:T(8,128)}, f32[4,512,128]{2,1,0:T(8,128)S(1)}, f32[32,4,128]{2,1,0:T(4,128)}, f32[4,8,128]{2,1,0:T(8,128)S(1)}, f32[8,128...) custom-call(s32[1]{0:T(128)S(6)} %copy.29.refs_0_, ...), custom_call_target="tpu_custom_call" | custom-call | tf_op jit(solution)/shard_map/pallas_call | solution.py:171
  119.2 3.6 %shard_map.269 = (bf16[2,2080,128]{2,1,0:T(8,128)(2,1)S(1)}, bf16[2,2080,128]{2,1,0:T(8,128)(2,1)S(1)}) custom-call(bf16[512,512]{1,0:T(8,128)(2,1)} %get-tuple-element.203.refs_0_, bf16[512,512]{1,0:T(8,128)(2,1)} %get-tuple-element.204.refs_1_, bf16[512,512]{1,0:T(8,128)(2,1)} %get-tuple-element.205.refs_2_, ...), custom_call_target="tpu_custom_call" | custom-call | tf_op jit(solution)/shard_map/pallas_call | solution.py:171
  131.0 4.2 %shard_map.270 = (f32[32,8,128]{2,1,0:T(8,128)}, f32[8,128]{1,0:T(8,128)S(1)}, bf16[512,512]{1,0:T(8,128)(2,1)S(1)}, f32[512,128]{1,0:T(8,128)S(1)}, bf16[512,12...) custom-call(s32[1]{0:T(128)S(6)} %copy.29.refs_0_, ...), custom_call_target="tpu_custom_call" | custom-call | tf_op jit(solution)/shard_map/pallas_call | solution.py:171
  137.9 3.1 %all-to-all-start.7 = ((f32[32,8,128]{2,1,0:T(8,128)}), f32[32,8,128]{2,1,0:T(8,128)S(1)}, u32[]{:S(2)}, u32[]{:S(2)}) async-start(f32[32,8,128]{2,1,0:T(8,128)} %get-tuple-element.234), calls=%async_computation.7 | async-start | bytes 262144 | tf_op jit(solution)/shard_map/all_to_all | solution.py:956
  142.9 6.3 %all-to-all-done.7.refs_1_ = f32[32,8,128]{2,1,0:T(8,128)S(1)} async-done(((f32[32,8,128]{2,1,0:T(8,128)}), f32[32,8,128]{2,1,0:T(8,128)S(1)}, u32[]{:S(2)}, u32[]{:S(2)}) %all-to-all-start.7) | async-done | bytes 131104 | tf_op jit(solution)/shard_map/all_to_all | solution.py:956
  150.5 4.6 %all-to-all-start.8 = ((bf16[8,544,128]{2,1,0:T(8,128)(2,1)}), bf16[8,544,128]{2,1,0:T(8,128)(2,1)S(1)}, u32[]{:S(2)}, u32[]{:S(2)}) async-start(bf16[8,544,128]{2,1,0:T(8,128)(2,1)} %shard_map.274), calls=%async_computation.8 | async-start | bytes 2228224 | tf_op jit(solution)/shard_map/all_to_all | solution.py:1167
  170.9 11.4 %all-to-all-done.8.refs_0_ = bf16[8,544,128]{2,1,0:T(8,128)(2,1)S(1)} async-done(((bf16[8,544,128]{2,1,0:T(8,128)(2,1)}), bf16[8,544,128]{2,1,0:T(8,128)(2,1)S(1)}, u32[]{:S(2)}, u32[]{:S(2)}) %all-to-all-start.8) | async-done | bytes 1114144 | tf_op jit(solution)/shard_map/all_to_all | solution.py:1167
  183.4 14.0 %all_to_all.56 = bf16[8,144,128]{2,1,0:T(8,128)(2,1)S(1)} all-to-all(bf16[8,144,128]{2,1,0:T(8,128)(2,1)S(1)} %get-tuple-element.249), channel_id=1, replica_groups=mesh['dp'=8,'mp'=4] {'dp'}, dimensions={0} | all-to-all | bytes 589824 | tf_op jit(solution)/shard_map/all_to_all | solution.py:1176
  197.3 3.5 %all-to-all-start.10 = ((bf16[8,400,128]{2,1,0:T(8,128)(2,1)}), bf16[8,400,128]{2,1,0:T(8,128)(2,1)S(1)}, u32[]{:S(2)}, u32[]{:S(2)}) async-start(bf16[8,400,128]{2,1,0:T(8,128)(2,1)} %get-tuple-element.251), calls=%async_computation.10 | async-start | bytes 1638400 | tf_op jit(solution)/shard_map/all_to_all | solution.py:1182
  201.3 7.2 %collective-permute-done.25.refs_2_ = bf16[1152,128]{1,0:T(8,128)(2,1)S(1)} collective-permute-done((bf16[1152,128]{1,0:T(8,128)(2,1)S(1)}, bf16[1152,128]{1,0:T(8,128)(2,1)S(1)}, u32[]{:S(2)}, u32[]{:S(2)}) %collective-permute-start.25) | collective-permute-done | bytes 294944 | tf_op jit(solution)/shard_map/ppermute | solution.py:961
  211.8 9.3 %all-to-all-done.10 = bf16[8,400,128]{2,1,0:T(8,128)(2,1)S(1)} async-done(((bf16[8,400,128]{2,1,0:T(8,128)(2,1)}), bf16[8,400,128]{2,1,0:T(8,128)(2,1)S(1)}, u32[]{:S(2)}, u32[]{:S(2)}) %all-to-all-start.10) | async-done | bytes 819232 | tf_op jit(solution)/shard_map/all_to_all | solution.py:1182
  (106 shorter events, 78.8 us)
Async XLA Ops:
  12.4 15.3 %collective-permute-start.4 = (bf16[1536,128]{1,0:T(8,128)(2,1)}, bf16[1536,128]{1,0:T(8,128)(2,1)S(1)}, u32[]{:S(2)}, u32[]{:S(2)}) collective-permute-start(bf16[1536,128]{1,0:T(8,128)(2,1)} %get-tuple-element.148.refs_0_), channel_id=1, source_target_pairs={{0,2},{1,3},{2,0},{3,1},{4,6},{5,7},{6,4},{7,5},{8,10},{9,11},{10,... | collective-permute-start | bytes 1179656 | tf_op jit(solution)/shard_map/ppermute | solution.py:961
  15.3 12.4 %all-to-all-start = ((f32[32,4,128]{2,1,0:T(4,128)}), f32[32,4,128]{2,1,0:T(4,128)S(1)}, u32[]{:S(2)}, u32[]{:S(2)}) async-start(f32[32,4,128]{2,1,0:T(4,128)} %get-tuple-element.142), calls=%async_computation | async-start | bytes 131072 | tf_op jit(solution)/shard_map/all_to_all | solution.py:956
  20.3 14.7 %collective-permute-start.3 = (bf16[1536,128]{1,0:T(8,128)(2,1)}, bf16[1536,128]{1,0:T(8,128)(2,1)S(1)}, u32[]{:S(2)}, u32[]{:S(2)}) collective-permute-start(bf16[1536,128]{1,0:T(8,128)(2,1)} %get-tuple-element.148.refs_0_), channel_id=1, source_target_pairs={{0,1},{1,0},{2,3},{3,2},{4,5},{5,4},{6,7},{7,6},{8,9},{9,8},{10,11... | collective-permute-start | bytes 1179656 | tf_op jit(solution)/shard_map/ppermute | solution.py:961
  31.8 10.6 %all-to-all-start.1 = ((f32[32,4,128]{2,1,0:T(4,128)}), f32[32,4,128]{2,1,0:T(4,128)S(1)}, u32[]{:S(2)}, u32[]{:S(2)}) async-start(f32[32,4,128]{2,1,0:T(4,128)} %get-tuple-element.146), calls=%async_computation.1 | async-start | bytes 131072 | tf_op jit(solution)/shard_map/all_to_all | solution.py:956
  42.4 16.7 %collective-permute-start.7 = (bf16[1536,128]{1,0:T(8,128)(2,1)}, bf16[1536,128]{1,0:T(8,128)(2,1)}, u32[]{:S(2)}, u32[]{:S(2)}) collective-permute-start(bf16[1536,128]{1,0:T(8,128)(2,1)} %get-tuple-element.163.refs_0_), channel_id=1, source_target_pairs={{0,2},{1,3},{2,0},{3,1},{4,6},{5,7},{6,4},{7,5},{8,10},{9,11},{10,... | collective-permute-start | bytes 1179656 | tf_op jit(solution)/shard_map/ppermute | solution.py:961
  48.3 10.8 %all-to-all-start.2 = ((f32[32,8,128]{2,1,0:T(8,128)}), f32[32,8,128]{2,1,0:T(8,128)S(1)}, u32[]{:S(2)}, u32[]{:S(2)}) async-start(f32[32,8,128]{2,1,0:T(8,128)} %get-tuple-element.154), calls=%async_computation.2 | async-start | bytes 262144 | tf_op jit(solution)/shard_map/all_to_all | solution.py:956
  50.8 16.4 %collective-permute-start.6 = (bf16[1536,128]{1,0:T(8,128)(2,1)}, bf16[1536,128]{1,0:T(8,128)(2,1)S(1)}, u32[]{:S(2)}, u32[]{:S(2)}) collective-permute-start(bf16[1536,128]{1,0:T(8,128)(2,1)} %get-tuple-element.163.refs_0_), channel_id=1, source_target_pairs={{0,1},{1,0},{2,3},{3,2},{4,5},{5,4},{6,7},{7,6},{8,9},{9,8},{10,11... | collective-permute-start | bytes 1179656 | tf_op jit(solution)/shard_map/ppermute | solution.py:961
  59.1 8.2 %collective-permute-start.8 = (bf16[1536,128]{1,0:T(8,128)(2,1)}, bf16[1536,128]{1,0:T(8,128)(2,1)S(1)}, u32[]{:S(2)}, u32[]{:S(2)}) collective-permute-start(bf16[1536,128]{1,0:T(8,128)(2,1)} %collective-permute-done.7.refs_2_), channel_id=1, source_target_pairs={{0,1},{1,0},{2,3},{3,2},{4,5},{5,4},{6,7},{7,6},{8,9},{9,8},{10,11... | collective-permute-start | bytes 1179656 | tf_op jit(solution)/shard_map/ppermute | solution.py:961
  62.7 8.0 %collective-permute-start.9 = (bf16[512,128]{1,0:T(8,128)(2,1)}, bf16[512,128]{1,0:T(8,128)(2,1)S(1)}, u32[]{:S(2)}, u32[]{:S(2)}) collective-permute-start(bf16[512,128]{1,0:T(8,128)(2,1)} %get-tuple-element.166), channel_id=1, source_target_pairs={{0,1},{1,0},{2,3},{3,2},{4,5},{5,4},{6,7},{7,6},{8,9},{9,8},{10,11... | collective-permute-start | bytes 393224 | tf_op jit(solution)/shard_map/ppermute | solution.py:961
  63.1 7.7 %collective-permute-start.10 = (bf16[512,128]{1,0:T(8,128)(2,1)}, bf16[512,128]{1,0:T(8,128)(2,1)S(1)}, u32[]{:S(2)}, u32[]{:S(2)}) collective-permute-start(bf16[512,128]{1,0:T(8,128)(2,1)} %get-tuple-element.167), channel_id=1, source_target_pairs={{0,2},{1,3},{2,0},{3,1},{4,6},{5,7},{6,4},{7,5},{8,10},{9,11},{10,... | collective-permute-start | bytes 393224 | tf_op jit(solution)/shard_map/ppermute | solution.py:961
  63.5 7.5 %collective-permute-start.11 = (bf16[512,128]{1,0:T(8,128)(2,1)}, bf16[512,128]{1,0:T(8,128)(2,1)S(1)}, u32[]{:S(2)}, u32[]{:S(2)}) collective-permute-start(bf16[512,128]{1,0:T(8,128)(2,1)} %get-tuple-element.168), channel_id=1, source_target_pairs={{0,3},{1,2},{2,1},{3,0},{4,7},{5,6},{6,5},{7,4},{8,11},{9,10},{10,... | collective-permute-start | bytes 393224 | tf_op jit(solution)/shard_map/ppermute | solution.py:961
  64.7 10.0 %all-to-all-start.3 = ((f32[32,4,128]{2,1,0:T(4,128)}), f32[32,4,128]{2,1,0:T(4,128)S(1)}, u32[]{:S(2)}, u32[]{:S(2)}) async-start(f32[32,4,128]{2,1,0:T(4,128)} %get-tuple-element.161), calls=%async_computation.3 | async-start | bytes 131072 | tf_op jit(solution)/shard_map/all_to_all | solution.py:956
  82.0 11.4 %all-to-all-start.4 = ((f32[32,4,128]{2,1,0:T(4,128)}), f32[32,4,128]{2,1,0:T(4,128)S(1)}, u32[]{:S(2)}, u32[]{:S(2)}) async-start(f32[32,4,128]{2,1,0:T(4,128)} %get-tuple-element.176), calls=%async_computation.4 | async-start | bytes 131072 | tf_op jit(solution)/shard_map/all_to_all | solution.py:956
  96.8 19.0 %collective-permute-start.13 = (bf16[1552,128]{1,0:T(8,128)(2,1)S(1)}, bf16[1552,128]{1,0:T(8,128)(2,1)S(1)}, u32[]{:S(2)}, u32[]{:S(2)}) collective-permute-start(bf16[1552,128]{1,0:T(8,128)(2,1)S(1)} %get-tuple-element.201), channel_id=1, source_target_pairs={{0,2},{1,3},{2,0},{3,1},{4,6},{5,7},{6,4},{7,5},{8,10},{9,11},{10,... | collective-permute-start | bytes 1191944 | tf_op jit(solution)/shard_map/ppermute | solution.py:961
  116.6 10.0 %all-to-all-start.6 = ((f32[32,4,128]{2,1,0:T(4,128)}), f32[32,4,128]{2,1,0:T(4,128)S(1)}, u32[]{:S(2)}, u32[]{:S(2)}) async-start(f32[32,4,128]{2,1,0:T(4,128)} %get-tuple-element.202), calls=%async_computation.6 | async-start | bytes 131072 | tf_op jit(solution)/shard_map/all_to_all | solution.py:956
  130.5 18.7 %collective-permute-start.17 = (bf16[2080,128]{1,0:T(8,128)(2,1)}, bf16[2080,128]{1,0:T(8,128)(2,1)S(1)}, u32[]{:S(2)}, u32[]{:S(2)}) collective-permute-start(bf16[2080,128]{1,0:T(8,128)(2,1)} %get-tuple-element.227), channel_id=1, source_target_pairs={{0,2},{1,3},{2,0},{3,1},{4,6},{5,7},{6,4},{7,5},{8,10},{9,11},{10,... | collective-permute-start | bytes 1597448 | tf_op jit(solution)/shard_map/ppermute | solution.py:961
  137.9 11.3 %all-to-all-start.7 = ((f32[32,8,128]{2,1,0:T(8,128)}), f32[32,8,128]{2,1,0:T(8,128)S(1)}, u32[]{:S(2)}, u32[]{:S(2)}) async-start(f32[32,8,128]{2,1,0:T(8,128)} %get-tuple-element.234), calls=%async_computation.7 | async-start | bytes 262144 | tf_op jit(solution)/shard_map/all_to_all | solution.py:956
  141.1 8.1 %collective-permute-start.16 = (bf16[528,128]{1,0:T(8,128)(2,1)S(1)}, bf16[528,128]{1,0:T(8,128)(2,1)S(1)}, u32[]{:S(2)}, u32[]{:S(2)}) collective-permute-start(bf16[528,128]{1,0:T(8,128)(2,1)S(1)} %get-tuple-element.226), channel_id=1, source_target_pairs={{0,2},{1,3},{2,0},{3,1},{4,6},{5,7},{6,4},{7,5},{8,10},{9,11},{10,... | collective-permute-start | bytes 405512 | tf_op jit(solution)/shard_map/ppermute | solution.py:961
  150.5 31.8 %all-to-all-start.8 = ((bf16[8,544,128]{2,1,0:T(8,128)(2,1)}), bf16[8,544,128]{2,1,0:T(8,128)(2,1)S(1)}, u32[]{:S(2)}, u32[]{:S(2)}) async-start(bf16[8,544,128]{2,1,0:T(8,128)(2,1)} %shard_map.274), calls=%async_computation.8 | async-start | bytes 2228224 | tf_op jit(solution)/shard_map/all_to_all | solution.py:1167
  157.1 8.5 %collective-permute-start.18 = (bf16[512,128]{1,0:T(8,128)(2,1)S(1)}, bf16[512,128]{1,0:T(8,128)(2,1)S(1)}, u32[]{:S(2)}, u32[]{:S(2)}) collective-permute-start(bf16[512,128]{1,0:T(8,128)(2,1)S(1)} %copy-done.14), channel_id=1, source_target_pairs={{0,1},{1,0},{2,3},{3,2},{4,5},{5,4},{6,7},{7,6},{8,9},{9,8},{10,11... | collective-permute-start | bytes 393224 | tf_op jit(solution)/shard_map/ppermute | solution.py:961
  157.4 9.8 %collective-permute-start.19 = (bf16[512,128]{1,0:T(8,128)(2,1)S(1)}, bf16[512,128]{1,0:T(8,128)(2,1)S(1)}, u32[]{:S(2)}, u32[]{:S(2)}) collective-permute-start(bf16[512,128]{1,0:T(8,128)(2,1)S(1)} %copy-done.13), channel_id=1, source_target_pairs={{0,2},{1,3},{2,0},{3,1},{4,6},{5,7},{6,4},{7,5},{8,10},{9,11},{10,... | collective-permute-start | bytes 393224 | tf_op jit(solution)/shard_map/ppermute | solution.py:961
  158.2 10.9 %collective-permute-start.20 = (bf16[512,128]{1,0:T(8,128)(2,1)S(1)}, bf16[512,128]{1,0:T(8,128)(2,1)S(1)}, u32[]{:S(2)}, u32[]{:S(2)}) collective-permute-start(bf16[512,128]{1,0:T(8,128)(2,1)S(1)} %copy-done.12), channel_id=1, source_target_pairs={{0,3},{1,2},{2,1},{3,0},{4,7},{5,6},{6,5},{7,4},{8,11},{9,10},{10,... | collective-permute-start | bytes 393224 | tf_op jit(solution)/shard_map/ppermute | solution.py:961
  197.3 23.7 %all-to-all-start.10 = ((bf16[8,400,128]{2,1,0:T(8,128)(2,1)}), bf16[8,400,128]{2,1,0:T(8,128)(2,1)S(1)}, u32[]{:S(2)}, u32[]{:S(2)}) async-start(bf16[8,400,128]{2,1,0:T(8,128)(2,1)} %get-tuple-element.251), calls=%async_computation.10 | async-start | bytes 1638400 | tf_op jit(solution)/shard_map/all_to_all | solution.py:1182
  200.9 7.7 %collective-permute-start.25 = (bf16[1152,128]{1,0:T(8,128)(2,1)S(1)}, bf16[1152,128]{1,0:T(8,128)(2,1)S(1)}, u32[]{:S(2)}, u32[]{:S(2)}) collective-permute-start(bf16[1152,128]{1,0:T(8,128)(2,1)S(1)} %bitcast.3), channel_id=1, source_target_pairs={{0,2},{1,3},{2,0},{3,1},{4,6},{5,7},{6,4},{7,5},{8,10},{9,11},{10,... | collective-permute-start | bytes 884744 | tf_op jit(solution)/shard_map/ppermute | solution.py:961
  (27 other events, 150.2 us)

commit v4 on v3

--- a/solution.py
+++ b/solution.py
@@ -389,8 +389,10 @@
             table[layer, 14 + h : 15 + h, :] = jnp.zeros((1, LANES), F32)
 
 
-def pack_maps(layers, copies, begin, c_own, v_own, g_own, *packs):
-    begin()
+def pack_maps(layers, copies, begin, c_own, v_own, g_own, weight, *packs):
+    begin()
+    *packs, near = packs
+    copies.flush(weight.at[0], near.ref)
     for layer in range(layers):
         for i, own in enumerate((c_own, v_own, g_own)):
             deep = own().shape[1]
@@ -398,10 +400,11 @@
         packs[layer].flush()
 
 
-def pack_block(copies, begin, x, *sends):
+def pack_block(copies, begin, x, weight, near, *sends):
     mp, _ = place()
     rows = sends[0].ref.shape[0]
     begin()
+    copies.flush(weight.at[1], near.ref)
     whole = x()
     for k, send in enumerate(sends):
         base = pl.multiple_of((mp ^ (k + 1)) * rows, SUB)
@@ -481,8 +484,7 @@
     return tile
 
 
-def drive_first(total_tokens, copies, begin, start, mom, table, h, prm, weight, drive, norms, out, ends, slow, maps):
-    weight = Later(copies, [(weight.at[0], maps)], maps)
+def drive_first(total_tokens, copies, begin, start, mom, table, h, prm, weight, drive, norms, out, ends, slow):
     mom = mom()
     groups = h.ref.shape[0]
     sums = [mom[j, 0:2, :] for j in range(groups)]
@@ -492,8 +494,7 @@
     drive_body(0, both[0:1, :], both[1:2, :], start, h(), prm(), table(), weight, drive, norms, out, ends, slow)
 
 
-def drive_next(layer, total_tokens, copies, begin, start, mom, prm, table, h, weight, drive, norms, out, ends, slow, maps):
-    weight = Later(copies, [(weight.at[layer], maps)], maps)
+def drive_next(layer, total_tokens, copies, begin, start, mom, prm, table, h, weight, drive, norms, out, ends, slow):
     tile = total_of(mom()) * (1.0 / total_tokens)
     half = tile.shape[0] // 2
     mean, second = lanes(tile[:half]), lanes(tile[half:])
@@ -603,7 +604,7 @@
     share_out(keep, send, pack, copies)
 
 
-def input_share(base, copies, slow, dlow, prods, weight, pack, held):
+def input_share(base, copies, slow, dlow, prods, weight, pack, held, sums=None):
     width = slow.dst.shape[1]
     held[...] = dot_tn(slow()[...], dlow()[...])
     half = width // 2
@@ -624,15 +625,17 @@
         cols = slice(h * LANES, (h + 1) * LANES)
         rows += [prods[2 * h : 2 * h + 1, :] - y_re[:, cols], prods[2 * h + 1 : 2 * h + 2, :] - y_im[:, cols]]
         rows += [y_re[:, cols]]
-    tile = jnp.concatenate(rows + [jnp.zeros((10, LANES), F32)], axis=0).astype(pack.dtype)
     for j in range(pack.shape[0]):
-        pack[j, base + width : base + width + 16, :] = tile
-
-
-def input_grads(layer, copies, begin, slow, dlow, prods, weight, keep, send, pack, held, maps):
+        cols = slice(j * LANES, (j + 1) * LANES)
+        more = [] if sums is None else [sums()[0:2, cols]]
+        tile = rows + more + [jnp.zeros((10 - 2 * len(more), LANES), F32)]
+        pack[j, base + width : base + width + 16, :] = jnp.concatenate(tile, axis=0).astype(pack.dtype)
+
+
+def input_grads(layer, copies, begin, slow, dlow, prods, sums, weight, keep, send, pack, held, maps):
     begin()
     weight = Later(copies, [(weight.at[layer], maps)], maps)
-    input_share(0, copies, slow, dlow, prods, weight, pack, held)
+    input_share(0, copies, slow, dlow, prods, weight, pack, held, sums)
     share_out(keep, send, pack, copies)
 
 
@@ -807,12 +810,14 @@
         put(u_ref, at, own + factor * dscaled)
         one = one + jnp.sum(dscaled, axis=0, keepdims=True)
         two = two + jnp.sum(dscaled * normed, axis=0, keepdims=True)
-    add_chunk(back, one, two)
     if layer == 0:
+        back.ref[...] = jnp.concatenate([one, two] + [jnp.zeros_like(one)] * 6, axis=0)
         mp, _ = place()
         for k, piece in enumerate((u0, u1, u2, u3)):
             piece.ref[...] = u_ref[mp ^ k, :, :].astype(piece.ref.dtype)
             piece.flush()
+    else:
+        add_chunk(back, one, two)
 
 
 def result_kernel(copies, begin, r0, r1, r2, r3, result):
@@ -826,21 +831,23 @@
     result.sent = True
 
 
-def last_kernel(total_tokens, copies, begin, norms, back, tile1, u0, u1, u2, u3, stream,
+def last_kernel(total_tokens, in_piece, copies, begin, norms, back, tile1, u0, u1, u2, u3, stream,
                 out, gain_out, shift_out, held):
     begin()
     mp, _ = place()
     rows = u0.dst.shape[0]
     streams = [Later(copies, [(own_rows(stream, rows, k), held.at[k])], held.at[k]) for k in range(4)]
-    tile, tile1, norms = total_of(back()), tile1(), norms()
-    half = tile.shape[0] // 2
+    tile1, norms = tile1(), norms()
+    width = norms.shape[1]
+    ((_, _, sums),) = unpieced(back(), 0, in_piece, width, 16)
+    sums = sums.astype(F32)
+    one, two = sums[6:7, :], sums[7:8, :]
+    half = tile1.shape[0] // 2
     zero = jnp.zeros((1, LANES), F32)
-    one, two, factor, inverse, mean, later_one, later_two = [zero] * 7
+    factor, inverse, mean, later_one, later_two = [zero] * 5
     for j in range(half):
         mine = jnp.where(mp == j, 1.0, 0.0)
         cols = slice(j * LANES, (j + 1) * LANES)
-        one = one + mine * tile[j : j + 1, :]
-        two = two + mine * tile[half + j : half + j + 1, :]
         later_one = later_one + mine * tile1[j : j + 1, :]
         later_two = later_two + mine * tile1[half + j : half + j + 1, :]
         factor = factor + mine * norms[0:1, cols]
@@ -866,70 +873,81 @@
         mine.ref[at, :] = (keep[0, at, :].astype(F32) + got[0, at, :].astype(F32)).astype(mine.ref.dtype)
 
 
-def four_sum(first, order, copies, begin, *refs):
+def four_sum(order, copies, begin, *refs):
     *ins, out = refs
     out = out.ref
-    count, piece = out.shape[0], out.shape[1]
-    tops = {True: 0, False: 0}
-
-    def place_of(top, is_input):
-        size = first if is_input else piece - first
-        base = 0 if is_input else first
-        return top // size, base + top % size
-
     for mine, got, spans in zip(ins[::2], ins[1::2], order, strict=True):
         mine, got = mine(), got()
         row = 0
-        for rows, is_input in spans:
-            for _ in range(rows // 16):
-                d, top = place_of(tops[is_input], is_input)
-                at = slice(row, row + 16)
-                total = mine[at, :].astype(F32) + got[at, :].astype(F32)
-                out[d, top : top + 16, :] = total.astype(out.dtype)
-                tops[is_input] += 16
-                row += 16
-    for is_input in (True, False):
-        size = first if is_input else piece - first
-        while tops[is_input] < count * size:
-            d, top = place_of(tops[is_input], is_input)
-            out[d, top : top + 16, :] = jnp.zeros((16, out.shape[2]), out.dtype)
-            tops[is_input] += 16
-
-
-def piece_sum(copies, begin, pieces, first, rest):
-    pieces = pieces()
-    count, rows = pieces.shape[0], pieces.shape[1]
-    split = first.ref.shape[1]
+        for rows, size, base in spans:
+            for i in range(0, out.shape[0] * size, 16):
+                d, top = i // size, base + i % size
+                if i < rows:
+                    at = slice(row + i, row + i + 16)
+                    total = (mine[at, :].astype(F32) + got[at, :].astype(F32)).astype(out.dtype)
+                else:
+                    total = jnp.zeros((16, out.shape[2]), out.dtype)
+                out[d, top : top + 16, :] = total
+            row += rows
+
+
+def piece_total(pieces, at):
+    total = pieces[0, at, :].astype(F32)
+    for d in range(1, pieces.shape[0]):
+        total = total + pieces[d, at, :].astype(F32)
+    return total.astype(BF16)
+
+
+def piece_sum(copies, begin, pieces, out):
+    for at in chunks(out.ref.shape[0], out.ref.shape[0] // 16):
+        out.ref[at, :] = piece_total(pieces(), at)
+
+
+def piece_sums(sizes, copies, begin, pieces, other, first, rest):
+    in_piece, vgo_piece = sizes
+    rows = pieces().shape[1]
     for at in chunks(rows, rows // 16):
-        total = pieces[0, at, :].astype(F32)
-        for d in range(1, count):
-            total = total + pieces[d, at, :].astype(F32)
-        low = total.astype(first.ref.dtype)
-        out, top = (first.ref, 0) if at.start < split else (rest.ref, split)
-        for d in range(count):
-            out[d, at.start - top : at.stop - top, :] = low
-
-
-def hand_out(features, copies, begin, decay, phase, full_in, full,
+        low = piece_total(pieces(), at)
+        inputs = at.start < 2 * in_piece
+        out, top = (first.ref, at.start) if inputs else (rest.ref, at.start - 2 * in_piece)
+        for d in range(out.shape[0]):
+            out[d, top : top + 16, :] = low
+    for at in chunks(vgo_piece, vgo_piece // 16):
+        low = other()[at, :]
+        for d in range(rest.ref.shape[0]):
+            rest.ref[d, vgo_piece + at.start : vgo_piece + at.stop, :] = low
+
+
+def unpieced(pieces, offset, size, first, rows):
+    at = first
+    while at < first + rows:
+        piece, inside = at // size, at % size
+        count = min(size - inside, first + rows - at)
+        yield at - first, count, pieces[piece, offset + inside : offset + inside + count, :]
+        at += count
+
+
+def hand_out(features, sizes, copies, begin, decay, phase, full_in, full,
              o_grad, skip_grad, v_grad, g_grad, vb, gb, d_grad, p_grad, s_grad):
     begin()
-    in_rows, vgo_rows = features + 16, 3 * features + 16
     full, full_in = full(), full_in()
     decay, phase = decay(), phase()
+    in_piece, vgo_piece = sizes
     for layer in range(2):
-        top = layer * vgo_rows
+        base = layer * vgo_piece
         for i, out in enumerate((v_grad, g_grad, o_grad)):
-            out.ref[layer, :, :] = full[top + i * features : top + (i + 1) * features, :].astype(F32)
+            for at, count, rows in unpieced(full, base, vgo_piece, i * features, features):
+                out.ref[layer, at : at + count, :] = rows.astype(F32)
             copies.flush(out.ref.at[layer], out.dst.at[layer])
             out.sent = True
-        top += 3 * features
         row = slice(layer, layer + 1)
-        vecs = full[top : top + 16, :].astype(F32)
+        ((_, _, vecs),) = unpieced(full, base, vgo_piece, 3 * features, 16)
+        vecs = vecs.astype(F32)
         vb.ref[row, :] = vecs[0:1, :]
         gb.ref[row, :] = vecs[1:2, :]
         skip_grad.ref[row, :] = vecs[2:3, :]
-        top = layer * in_rows + features
-        tile = full_in[top : top + 16, :].astype(F32)
+        ((_, _, tile),) = unpieced(full_in, layer * in_piece, in_piece, features, 16)
+        tile = tile.astype(F32)
         for h in range(2):
             cols = slice(h * LANES, (h + 1) * LANES)
             d_grad.ref[row, cols] = -jnp.exp(decay[row, cols]) * tile[3 * h : 3 * h + 1, :]
@@ -937,15 +955,14 @@
             s_grad.ref[row, cols] = tile[3 * h + 2 : 3 * h + 3, :]
 
 
-def input_kernel(features, copies, begin, p0, p1, p2, p3, out):
+def input_kernel(features, size, copies, begin, p0, p1, p2, p3, out):
     begin()
     mp, _ = place()
-    for k, piece in enumerate((p0, p1, p2, p3)):
+    for k, pieces in enumerate((p0, p1, p2, p3)):
         cols = pl.ds(pl.multiple_of((mp ^ k) * LANES, LANES), LANES)
-        piece = piece()
         for layer in range(out.ref.shape[0]):
-            top = layer * (features + 16)
-            out.ref[layer, :, cols] = piece[top : top + features, :].astype(F32)
+            for at, count, rows in unpieced(pieces(), layer * size, size, 0, features):
+                out.ref[layer, at : at + count, cols] = rows.astype(F32)
 
 
 def shape(dims, dtype=F32):
@@ -1017,6 +1034,7 @@
     one_map = pltpu.VMEM((features, features), BF16)
     maps = pltpu.VMEM((3, features, features), BF16)
     all_maps = shape((3, features, features), BF16)
+    near_map = Near(shape((features, features), BF16))
 
     mom_out, table, *sends = call(
         functools.partial(first_kernel, rows),
@@ -1027,16 +1045,17 @@
     )
     table = Near(table)
     got_h = [Near(x) for x in swap(sends)]
-    mom0 = Near(every(after(mom_out, *[g.array for g in got_h])))
+    mom0 = every(after(mom_out, *[g.array for g in got_h]))
     h0, prm = call(
         gather_block,
         [near_blocks, Near(shape((parts, 16, width)))],
         [pltpu.VMEM(one_block, F32)],
         *got_h, *plist, Raw(stream),
     )
-    h0, prm = Near(h0), Near(prm)
-    packs = call(
-        functools.partial(pack_maps, layers), [packed_w] * layers, [], output_map, value_weight, gate_weight
+    h0, prm, mom0 = Near(h0), Near(prm), Near(after(mom0, h0))
+    *packs, near_in = call(
+        functools.partial(pack_maps, layers), [packed_w] * layers + [near_map], [],
+        output_map, value_weight, gate_weight, Raw(input_map),
     )
     w0 = after(packs[0], got_h[1].array, got_h[2].array)
     (full0,) = call(assemble, [all_maps], [], w0, *[Near(w) for w in spread(w0, mom0.array)])
@@ -1044,8 +1063,8 @@
     drive0, norms0, ends_all, ends0, slow0 = call(
         functools.partial(drive_first, tokens),
         [near_blocks, near_norms, near_every, near_ends, wide_low],
-        [one_map],
-        start_offsets, mom0, table, h0, prm, Raw(input_map),
+        [],
+        start_offsets, mom0, table, h0, prm, Near(near_in),
         scalars=1,
     )
     got = Near(after(every(ends_all), full0))
@@ -1058,15 +1077,17 @@
         scalars=1,
     )
     h1 = Near(h1)
-    sends = call(pack_block, [low_block] * 3, [], after(cotangent, got.array))
+    near_in, *sends = call(
+        pack_block, [near_map] + [low_block] * 3, [], after(cotangent, got.array), Raw(input_map)
+    )
     mom1 = Near(after(every(mom_out), *sends))
     w1 = after(packs[1], got.array)
     (full1,) = call(assemble, [all_maps], [], w1, *[Near(w) for w in spread(w1, mom1.array)])
     drive1, norms1, ends_all, ends1, slow1 = call(
         functools.partial(drive_next, 1, tokens),
         [near_blocks, near_norms, near_every, near_ends, wide_low],
-        [one_map],
-        start_offsets, mom1, prm, table, h1, Raw(input_map),
+        [],
+        start_offsets, mom1, prm, table, h1, Near(near_in),
         scalars=1,
     )
     got_cot = [Near(x) for x in swap([after(s, norms1) for s in sends])]
@@ -1123,16 +1144,27 @@
         Halves(slow1), Halves(sig0), Halves(part0), Halves(slope0), Halves(slow0), Raw(full0),
         scalars=1,
     )
+    unit = 16 * count_dp
+    in_piece, vgo_piece = (-(-n // unit) * 16 for n in (in_rows, vgo_rows))
+
+    def joined(order, *operands):
+        piece = max(base + size for spans in order for _, size, base in spans)
+        out = Near(shape((count_dp, piece, width), BF16))
+        return call(functools.partial(four_sum, order), [out], [], *map(Near, operands))[0]
+
+    own1 = joined((((vgo_rows, vgo_piece, 0),),), mine1, far1)
     got = Near(every(after(ends_all, far1)))
     keep0, send0 = call(
         functools.partial(both_grads, 0), [both_half, both_half], [both_pack] + in_room[1:],
         sent0, dv, dg, states0, dml0, sums, *late1, Raw(input_map),
     )
+    pieces = lax.all_to_all(after(own1, got.array), "dp", 0, 0)
+    (summed1,) = call(piece_sum, [Near(shape((vgo_piece, width), BF16))], [], Near(pieces))
     send0 = after(send0, got.array)
     got = Near(after(got.array, keep0))
     back_out, prods, dlow, *us = call(
         functools.partial(back_second, 0),
-        [near_sums, Near(shape((8, LANES))), Near(wide_low), Near(shape(one_block))] + [near_low] * 3,
+        [near_norms, Near(shape((8, LANES))), Near(wide_low), Near(shape(one_block))] + [near_low] * 3,
         [v_blocks, one_map, v_blocks],
         start_offsets, got, mom0, table, Near(back_ends0), norms0, prm, Near(ds0), states0, Halves(g0), Halves(dml0),
         Halves(h0), Raw(input_map),
@@ -1142,48 +1174,43 @@
     far0 = hop(other0, 2)
     prods = after(prods, mine0)
     in_keep0, in_send0 = call(
-        functools.partial(input_grads, 0), [in_half, in_half], in_room, slow0, Near(dlow), Near(prods), Raw(input_map)
+        functools.partial(input_grads, 0), [in_half, in_half], in_room, slow0, Near(dlow), Near(prods), Near(back_out), Raw(input_map)
     )
     us = (us[0], *swap([after(u, in_send0) for u in us[1:]]))
-    back0 = Near(every(after(back_out, in_send0, mine0)))
     in_mine0, in_other0 = pair_share(in_keep0, in_send0)
     in_far0 = hop(in_other0, 2)
-    back0 = Near(after(back0.array, in_mine0))
+
+    order = (
+        ((in_rows, in_piece, 0),),
+        ((vgo_rows, vgo_piece, 2 * in_piece), (in_rows, in_piece, in_piece)),
+    )
+    own0 = joined(order, in_mine0, in_far0, mine0, far0)
+    pieces = lax.all_to_all(after(own0, summed1), "dp", 0, 0)
+    first, rest = call(
+        functools.partial(piece_sums, (in_piece, vgo_piece)),
+        [Near(shape((count_dp, 2 * n, width), BF16)) for n in (in_piece, vgo_piece)],
+        [],
+        Near(pieces), Near(summed1),
+    )
+    result = [res[0], *swap([after(r, own0) for r in res[1:]])]
+    (result,) = call(result_kernel, [shape((block, width))], [], res[0], *[Near(r) for r in result[1:]])
+    full_in = lax.all_to_all(after(first, result, *us[1:]), "dp", 0, 0)
     stream_grad, gain_grad, shift_grad = call(
-        functools.partial(last_kernel, tokens),
+        functools.partial(last_kernel, tokens, in_piece),
         [shape((block, width)), shape((layers, width)), shape((layers, width))],
         [pltpu.VMEM((4,) + one_block, F32)],
-        norms0, back0, Near(tile1), *[Near(u) for u in us], Raw(stream),
-    )
-
-    unit = 16 * count_dp
-    in_piece = -(-2 * in_rows // unit) * 16
-    piece = in_piece + -(-2 * vgo_rows // unit) * 16
-    order = (((in_rows, True),), ((vgo_rows, False), (in_rows, True)), ((vgo_rows, False),))
-    (own,) = call(
-        functools.partial(four_sum, in_piece, order), [Near(shape((count_dp, piece, width), BF16))], [],
-        Near(in_mine0), Near(in_far0), Near(mine0), Near(far0), Near(mine1), Near(far1),
-    )
-    pieces = lax.all_to_all(after(own, back0.array), "dp", 0, 0)
-    first, rest = call(
-        piece_sum,
-        [Near(shape((count_dp, n, width), BF16)) for n in (in_piece, piece - in_piece)],
-        [],
-        Near(pieces),
-    )
-    result = [res[0], *swap([after(r, own) for r in res[1:]])]
-    (result,) = call(result_kernel, [shape((block, width))], [], res[0], *[Near(r) for r in result[1:]])
-    full_in = lax.all_to_all(after(first, stream_grad, result), "dp", 0, 0).reshape(-1, width)
+        norms0, Near(full_in), Near(tile1), *[Near(u) for u in us], Raw(stream),
+    )
     rest = after(rest, full_in)
     (input_grad,) = call(
-        functools.partial(input_kernel, features), [shape((layers, features, features))], [],
+        functools.partial(input_kernel, features, in_piece), [shape((layers, features, features))], [],
         Near(full_in), *[Near(x) for x in spread(full_in)],
     )
-    full = lax.all_to_all(rest, "dp", 0, 0).reshape(-1, width)
-    full = after(full, input_grad)
+    full = lax.all_to_all(rest, "dp", 0, 0)
+    full = after(full, input_grad, stream_grad)
     mat, vec, state = shape((layers, features, width)), shape((layers, width)), shape(decay_log.shape)
     o_grad, skip_grad, v_grad, g_grad, vb, gb, d_grad, p_grad, s_grad = call(
-        functools.partial(hand_out, features),
+        functools.partial(hand_out, features, (in_piece, vgo_piece)),
         [mat, vec, mat, mat, vec, vec, state, state, state],
         [],
         decay_log, phase_log, Near(full_in), Near(full),

time: 224 us -> 216 us (0.964)
  waiting for transfers between devices: 77.6 us -> 70.6 us
    all_to_all x7 -> x6, waiting for transfers between devices: 32 us -> 25.5 us  [every(): return lax.all_to_all(x, AXES, 0, 0)]
    all_to_all x2 -> x3, starting transfers between devices: 8.13 us -> 12.7 us  [the longest x1 5.65 us: on_device(): pieces = lax.all_to_all(after(own0, summed1), 'dp', 0, 0)]
    all_to_all x7 -> x6, starting transfers between devices: 22.9 us -> 20 us  [every(): return lax.all_to_all(x, AXES, 0, 0)]
    pallas_call x26 -> x28, Pallas kernels: 68 us -> 66.1 us  [call(): return made_call(max(used[0], 1))(*plain)]
    all_to_all x2 -> x3, waiting for transfers between devices: 20.7 us -> 20.5 us  [the longest x1 8.83 us: on_device(): full = lax.all_to_all(rest, 'dp', 0, 0)]
  transfers between devices with their start and end apart: 36 -> 36, of which waited for: 20 -> 18; matrix products, arithmetic and copies ran while one was open for 0% -> 0% of each run, Pallas kernels for 24% -> 25%
where the time goes in v4:
time: 216 us; the launch traced here: 215 us
  waiting for transfers between devices  70.6 us (33%)
  Pallas kernels  66.1 us (31%)
  starting transfers between devices  48.1 us (22%)
  blocking collectives  27 us (12%)
    pallas_call x28, Pallas kernels, call(): return made_call(max(used[0], 1))(*plain)  66.1 us
    all_to_all x6, waiting for transfers between devices, every(): return lax.all_to_all(x, AXES, 0, 0)  25.5 us
    ppermute x27, waiting for transfers between devices, hop(): return lax.ppermute(x, 'mp', [(i, i ^ k) for i in range(count)])  24.6 us
    all_to_all x6, starting transfers between devices, every(): return lax.all_to_all(x, AXES, 0, 0)  20 us
    ppermute x27, starting transfers between devices, hop(): return lax.ppermute(x, 'mp', [(i, i ^ k) for i in range(count)])  15.4 us
    all_to_all x1, blocking collectives, on_device(): full_in = lax.all_to_all(after(first, result, *us[1:]), 'dp', 0, 0)  14.5 us
    all_to_all x1, blocking collectives, every(): return lax.all_to_all(x, AXES, 0, 0)  12.5 us
    all_to_all x1, waiting for transfers between devices, on_device(): full = lax.all_to_all(rest, 'dp', 0, 0)  8.83 us
  transfers between devices with their start and end apart: 36, of which 18 were waited for; matrix products, arithmetic and copies ran while one was open for 0% of the time, Pallas kernels for 25%

profile of v4, /device:TPU:0, one launch (start us, length us, event | category | flops | bytes accessed | tf_op | source)
XLA Modules:
  0.0 214.8 jit_solution(16758835789238856367)
XLA Ops:
  15.3 4.9 %all-to-all-start = ((f32[32,4,128]{2,1,0:T(4,128)}), f32[32,4,128]{2,1,0:T(4,128)S(1)}, u32[]{:S(2)}, u32[]{:S(2)}) async-start(f32[32,4,128]{2,1,0:T(4,128)} %get-tuple-element.144), calls=%async_computation | async-start | bytes 131072 | tf_op jit(solution)/shard_map/all_to_all | solution.py:973
  21.6 6.1 %all-to-all-done.refs_1_.refs_2_ = f32[32,4,128]{2,1,0:T(4,128)S(1)} async-done(((f32[32,4,128]{2,1,0:T(4,128)}), f32[32,4,128]{2,1,0:T(4,128)S(1)}, u32[]{:S(2)}, u32[]{:S(2)}) %all-to-all-start) | async-done | bytes 65568 | tf_op jit(solution)/shard_map/all_to_all | solution.py:973
  29.6 3.2 %all-to-all-start.1 = ((f32[32,4,128]{2,1,0:T(4,128)}), f32[32,4,128]{2,1,0:T(4,128)S(1)}, u32[]{:S(2)}, u32[]{:S(2)}) async-start(f32[32,4,128]{2,1,0:T(4,128)} %get-tuple-element.150), calls=%async_computation.1 | async-start | bytes 131072 | tf_op jit(solution)/shard_map/all_to_all | solution.py:973
  32.9 3.6 %shard_map.258.refs_9_.refs_12_ = bf16[3,512,512]{2,1,0:T(8,128)(2,1)} custom-call(bf16[1536,128]{1,0:T(8,128)(2,1)} %get-tuple-element.152.refs_0_, bf16[1536,128]{1,0:T(8,128)(2,1)} %collective-permute-done.3.refs_1_, bf16[1536,128]{1,0:T(8,128)(2,1)S(1)} %collective-permute-done.4.refs_2_, bf16[1536,128]{1,0:T(8,128)(2,1)} %collective-permute-done.5.refs_3_), custom_call_target="tpu_custom_call" | custom-call | tf_op jit(solution)/shard_map/pallas_call | solution.py:171
  36.5 3.8 %all-to-all-done.1.refs_1_ = f32[32,4,128]{2,1,0:T(4,128)S(1)} async-done(((f32[32,4,128]{2,1,0:T(4,128)}), f32[32,4,128]{2,1,0:T(4,128)S(1)}, u32[]{:S(2)}, u32[]{:S(2)}) %all-to-all-start.1) | async-done | bytes 65568 | tf_op jit(solution)/shard_map/all_to_all | solution.py:973
  40.7 5.4 %shard_map.259 = (f32[4,512,128]{2,1,0:T(8,128)S(1)}, f32[32,8,128]{2,1,0:T(8,128)}, f32[4,512,128]{2,1,0:T(8,128)}, bf16[512,512]{1,0:T(8,128)(2,1)}, bf16[512,...) custom-call(s32[1]{0:T(128)S(6)} %copy.29.refs_0_, ...), custom_call_target="tpu_custom_call" | custom-call | tf_op jit(solution)/shard_map/pallas_call | solution.py:171
  51.0 5.9 %all-to-all-done.2.refs_1_ = f32[32,8,128]{2,1,0:T(8,128)S(1)} async-done(((f32[32,8,128]{2,1,0:T(8,128)}), f32[32,8,128]{2,1,0:T(8,128)S(1)}, u32[]{:S(2)}, u32[]{:S(2)}) %all-to-all-start.2) | async-done | bytes 131104 | tf_op jit(solution)/shard_map/all_to_all | solution.py:973
  64.0 3.7 %shard_map.262.refs_9_ = bf16[3,512,512]{2,1,0:T(8,128)(2,1)} custom-call(bf16[1536,128]{1,0:T(8,128)(2,1)} %get-tuple-element.168.refs_0_, bf16[1536,128]{1,0:T(8,128)(2,1)S(1)} %collective-permute-done.6.refs_1_, bf16[1536,128]{1,0:T(8,128)(2,1)} %collective-permute-done.7.refs_2_, bf16[1536,128]{1,0:T(8,128)(2,1)} %collective-permute-done.8.refs_3_), custom_call_target="tpu_custom_call" | custom-call | tf_op jit(solution)/shard_map/pallas_call | solution.py:171
  71.4 7.4 %shard_map.264 = (f32[4,512,128]{2,1,0:T(8,128)S(1)}, f32[32,4,128]{2,1,0:T(4,128)}, f32[4,8,128]{2,1,0:T(8,128)S(1)}, f32[4,512,128]{2,1,0:T(8,128)}, bf16[512,...) custom-call(s32[1]{0:T(128)S(6)} %copy.29.refs_0_, ...), custom_call_target="tpu_custom_call" | custom-call | tf_op jit(solution)/shard_map/pallas_call | solution.py:171
  78.8 4.1 %all-to-all-start.4 = ((f32[32,4,128]{2,1,0:T(4,128)}), f32[32,4,128]{2,1,0:T(4,128)S(1)}, u32[]{:S(2)}, u32[]{:S(2)}) async-start(f32[32,4,128]{2,1,0:T(4,128)} %get-tuple-element.181), calls=%async_computation.4 | async-start | bytes 131072 | tf_op jit(solution)/shard_map/all_to_all | solution.py:973
  85.7 4.6 %all-to-all-done.4.refs_1_ = f32[32,4,128]{2,1,0:T(4,128)S(1)} async-done(((f32[32,4,128]{2,1,0:T(4,128)}), f32[32,4,128]{2,1,0:T(4,128)S(1)}, u32[]{:S(2)}, u32[]{:S(2)}) %all-to-all-start.4) | async-done | bytes 65568 | tf_op jit(solution)/shard_map/all_to_all | solution.py:973
  94.3 12.5 %all_to_all.55.refs_1_ = f32[32,8,128]{2,1,0:T(8,128)S(1)} all-to-all(f32[32,8,128]{2,1,0:T(8,128)S(1)} %get-tuple-element.194), channel_id=1, replica_groups=mesh['dp'=8,'mp'=4] {'dp','mp'}, dimensions={0} | all-to-all | bytes 262144 | tf_op jit(solution)/shard_map/all_to_all | solution.py:973
  106.8 5.9 %shard_map.268 = (f32[4,512,128]{2,1,0:T(8,128)}, f32[4,512,128]{2,1,0:T(8,128)S(1)}, f32[32,4,128]{2,1,0:T(4,128)}, f32[4,8,128]{2,1,0:T(8,128)S(1)}, f32[8,128...) custom-call(s32[1]{0:T(128)S(6)} %copy.29.refs_0_, ...), custom_call_target="tpu_custom_call" | custom-call | tf_op jit(solution)/shard_map/pallas_call | solution.py:171
  116.3 3.6 %shard_map.269 = (bf16[2,2080,128]{2,1,0:T(8,128)(2,1)S(1)}, bf16[2,2080,128]{2,1,0:T(8,128)(2,1)S(1)}) custom-call(bf16[512,512]{1,0:T(8,128)(2,1)} %get-tuple-element.208.refs_0_, bf16[512,512]{1,0:T(8,128)(2,1)} %get-tuple-element.209.refs_1_, bf16[512,512]{1,0:T(8,128)(2,1)} %get-tuple-element.210.refs_2_, ...), custom_call_target="tpu_custom_call" | custom-call | tf_op jit(solution)/shard_map/pallas_call | solution.py:171
  120.0 3.7 %all-to-all-done.6.refs_1_ = f32[32,4,128]{2,1,0:T(4,128)S(1)} async-done(((f32[32,4,128]{2,1,0:T(4,128)}), f32[32,4,128]{2,1,0:T(4,128)S(1)}, u32[]{:S(2)}, u32[]{:S(2)}) %all-to-all-start.6) | async-done | bytes 65568 | tf_op jit(solution)/shard_map/all_to_all | solution.py:973
  124.7 3.5 %all-to-all-start.7 = ((bf16[8,208,128]{2,1,0:T(8,128)(2,1)}), bf16[8,208,128]{2,1,0:T(8,128)(2,1)S(1)}, u32[]{:S(2)}, u32[]{:S(2)}) async-start(bf16[8,208,128]{2,1,0:T(8,128)(2,1)} %shard_map.276), calls=%async_computation.7 | async-start | bytes 851968 | tf_op jit(solution)/shard_map/all_to_all | solution.py:1161
  130.4 3.5 %shard_map.270 = (f32[8,512]{1,0:T(8,128)S(1)}, f32[8,128]{1,0:T(8,128)S(1)}, bf16[512,512]{1,0:T(8,128)(2,1)S(1)}, f32[512,128]{1,0:T(8,128)S(1)}, bf16[512,128...) custom-call(s32[1]{0:T(128)S(6)} %copy.29.refs_0_, ...), custom_call_target="tpu_custom_call" | custom-call | tf_op jit(solution)/shard_map/pallas_call | solution.py:171
  141.4 5.4 %collective-permute-done.16.refs_1_ = bf16[528,128]{1,0:T(8,128)(2,1)S(1)} collective-permute-done((bf16[528,128]{1,0:T(8,128)(2,1)S(1)}, bf16[528,128]{1,0:T(8,128)(2,1)S(1)}, u32[]{:S(2)}, u32[]{:S(2)}) %collective-permute-start.16) | collective-permute-done | bytes 135200 | tf_op jit(solution)/shard_map/ppermute | solution.py:978
  147.9 5.7 %all-to-all-start.8 = ((bf16[8,368,128]{2,1,0:T(8,128)(2,1)}), bf16[8,368,128]{2,1,0:T(8,128)(2,1)S(1)}, u32[]{:S(2)}, u32[]{:S(2)}) async-start(bf16[8,368,128]{2,1,0:T(8,128)(2,1)} %shard_map.274), calls=%async_computation.8 | async-start | bytes 1507328 | tf_op jit(solution)/shard_map/all_to_all | solution.py:1188
  163.7 8.7 %all-to-all-done.8.refs_0_ = bf16[8,368,128]{2,1,0:T(8,128)(2,1)S(1)} async-done(((bf16[8,368,128]{2,1,0:T(8,128)(2,1)}), bf16[8,368,128]{2,1,0:T(8,128)(2,1)S(1)}, u32[]{:S(2)}, u32[]{:S(2)}) %all-to-all-start.8) | async-done | bytes 753696 | tf_op jit(solution)/shard_map/all_to_all | solution.py:1188
  173.5 14.5 %all_to_all.56.refs_1_.refs_0_.refs_2_ = bf16[8,160,128]{2,1,0:T(8,128)(2,1)S(1)} all-to-all(bf16[8,160,128]{2,1,0:T(8,128)(2,1)S(1)} %get-tuple-element.248), channel_id=1, replica_groups=mesh['dp'=8,'mp'=4] {'dp'}, dimensions={0} | all-to-all | bytes 655360 | tf_op jit(solution)/shard_map/all_to_all | solution.py:1197
  188.0 3.5 %all-to-all-start.10 = ((bf16[8,416,128]{2,1,0:T(8,128)(2,1)}), bf16[8,416,128]{2,1,0:T(8,128)(2,1)S(1)}, u32[]{:S(2)}, u32[]{:S(2)}) async-start(bf16[8,416,128]{2,1,0:T(8,128)(2,1)} %get-tuple-element.255), calls=%async_computation.10 | async-start | bytes 1703936 | tf_op jit(solution)/shard_map/all_to_all | solution.py:1209
  191.9 8.1 %collective-permute-done.25.refs_2_ = bf16[8,160,128]{2,1,0:T(8,128)(2,1)S(1)} collective-permute-done((bf16[8,160,128]{2,1,0:T(8,128)(2,1)S(1)}, bf16[8,160,128]{2,1,0:T(8,128)(2,1)S(1)}, u32[]{:S(2)}, u32[]{:S(2)}) %collective-permute-start.25) | collective-permute-done | bytes 327712 | tf_op jit(solution)/shard_map/ppermute | solution.py:978
  203.8 8.8 %all-to-all-done.10.refs_3_ = bf16[8,416,128]{2,1,0:T(8,128)(2,1)S(1)} async-done(((bf16[8,416,128]{2,1,0:T(8,128)(2,1)}), bf16[8,416,128]{2,1,0:T(8,128)(2,1)S(1)}, u32[]{:S(2)}, u32[]{:S(2)}) %all-to-all-start.10) | async-done | bytes 852000 | tf_op jit(solution)/shard_map/all_to_all | solution.py:1209
  (94 shorter events, 72.6 us)
Async XLA Ops:
  12.4 15.3 %collective-permute-start.4 = (bf16[1536,128]{1,0:T(8,128)(2,1)}, bf16[1536,128]{1,0:T(8,128)(2,1)S(1)}, u32[]{:S(2)}, u32[]{:S(2)}) collective-permute-start(bf16[1536,128]{1,0:T(8,128)(2,1)} %get-tuple-element.152.refs_0_), channel_id=1, source_target_pairs={{0,2},{1,3},{2,0},{3,1},{4,6},{5,7},{6,4},{7,5},{8,10},{9,11},{10,... | collective-permute-start | bytes 1179656 | tf_op jit(solution)/shard_map/ppermute | solution.py:978
  15.3 12.4 %all-to-all-start = ((f32[32,4,128]{2,1,0:T(4,128)}), f32[32,4,128]{2,1,0:T(4,128)S(1)}, u32[]{:S(2)}, u32[]{:S(2)}) async-start(f32[32,4,128]{2,1,0:T(4,128)} %get-tuple-element.144), calls=%async_computation | async-start | bytes 131072 | tf_op jit(solution)/shard_map/all_to_all | solution.py:973
  20.3 12.6 %collective-permute-start.3 = (bf16[1536,128]{1,0:T(8,128)(2,1)}, bf16[1536,128]{1,0:T(8,128)(2,1)}, u32[]{:S(2)}, u32[]{:S(2)}) collective-permute-start(bf16[1536,128]{1,0:T(8,128)(2,1)} %get-tuple-element.152.refs_0_), channel_id=1, source_target_pairs={{0,1},{1,0},{2,3},{3,2},{4,5},{5,4},{6,7},{7,6},{8,9},{9,8},{10,11... | collective-permute-start | bytes 1179656 | tf_op jit(solution)/shard_map/ppermute | solution.py:978
  29.6 10.6 %all-to-all-start.1 = ((f32[32,4,128]{2,1,0:T(4,128)}), f32[32,4,128]{2,1,0:T(4,128)S(1)}, u32[]{:S(2)}, u32[]{:S(2)}) async-start(f32[32,4,128]{2,1,0:T(4,128)} %get-tuple-element.150), calls=%async_computation.1 | async-start | bytes 131072 | tf_op jit(solution)/shard_map/all_to_all | solution.py:973
  40.3 16.7 %collective-permute-start.7 = (bf16[1536,128]{1,0:T(8,128)(2,1)}, bf16[1536,128]{1,0:T(8,128)(2,1)}, u32[]{:S(2)}, u32[]{:S(2)}) collective-permute-start(bf16[1536,128]{1,0:T(8,128)(2,1)} %get-tuple-element.168.refs_0_), channel_id=1, source_target_pairs={{0,2},{1,3},{2,0},{3,1},{4,6},{5,7},{6,4},{7,5},{8,10},{9,11},{10,... | collective-permute-start | bytes 1179656 | tf_op jit(solution)/shard_map/ppermute | solution.py:978
  46.1 10.8 %all-to-all-start.2 = ((f32[32,8,128]{2,1,0:T(8,128)}), f32[32,8,128]{2,1,0:T(8,128)S(1)}, u32[]{:S(2)}, u32[]{:S(2)}) async-start(f32[32,8,128]{2,1,0:T(8,128)} %get-tuple-element.158), calls=%async_computation.2 | async-start | bytes 262144 | tf_op jit(solution)/shard_map/all_to_all | solution.py:973
  48.7 15.3 %collective-permute-start.6 = (bf16[1536,128]{1,0:T(8,128)(2,1)}, bf16[1536,128]{1,0:T(8,128)(2,1)S(1)}, u32[]{:S(2)}, u32[]{:S(2)}) collective-permute-start(bf16[1536,128]{1,0:T(8,128)(2,1)} %get-tuple-element.168.refs_0_), channel_id=1, source_target_pairs={{0,1},{1,0},{2,3},{3,2},{4,5},{5,4},{6,7},{7,6},{8,9},{9,8},{10,11... | collective-permute-start | bytes 1179656 | tf_op jit(solution)/shard_map/ppermute | solution.py:978
  59.5 8.2 %collective-permute-start.9 = (bf16[512,128]{1,0:T(8,128)(2,1)}, bf16[512,128]{1,0:T(8,128)(2,1)S(1)}, u32[]{:S(2)}, u32[]{:S(2)}) collective-permute-start(bf16[512,128]{1,0:T(8,128)(2,1)} %get-tuple-element.171), channel_id=1, source_target_pairs={{0,1},{1,0},{2,3},{3,2},{4,5},{5,4},{6,7},{7,6},{8,9},{9,8},{10,11... | collective-permute-start | bytes 393224 | tf_op jit(solution)/shard_map/ppermute | solution.py:978
  59.8 7.8 %collective-permute-start.10 = (bf16[512,128]{1,0:T(8,128)(2,1)}, bf16[512,128]{1,0:T(8,128)(2,1)S(1)}, u32[]{:S(2)}, u32[]{:S(2)}) collective-permute-start(bf16[512,128]{1,0:T(8,128)(2,1)} %get-tuple-element.172), channel_id=1, source_target_pairs={{0,2},{1,3},{2,0},{3,1},{4,6},{5,7},{6,4},{7,5},{8,10},{9,11},{10,... | collective-permute-start | bytes 393224 | tf_op jit(solution)/shard_map/ppermute | solution.py:978
  60.3 7.5 %collective-permute-start.11 = (bf16[512,128]{1,0:T(8,128)(2,1)S(1)}, bf16[512,128]{1,0:T(8,128)(2,1)S(1)}, u32[]{:S(2)}, u32[]{:S(2)}) collective-permute-start(bf16[512,128]{1,0:T(8,128)(2,1)S(1)} %copy-done.7), channel_id=1, source_target_pairs={{0,3},{1,2},{2,1},{3,0},{4,7},{5,6},{6,5},{7,4},{8,11},{9,10},{10,... | collective-permute-start | bytes 393224 | tf_op jit(solution)/shard_map/ppermute | solution.py:978
  61.4 10.0 %all-to-all-start.3 = ((f32[32,4,128]{2,1,0:T(4,128)}), f32[32,4,128]{2,1,0:T(4,128)S(1)}, u32[]{:S(2)}, u32[]{:S(2)}) async-start(f32[32,4,128]{2,1,0:T(4,128)} %get-tuple-element.166), calls=%async_computation.3 | async-start | bytes 131072 | tf_op jit(solution)/shard_map/all_to_all | solution.py:973
  78.8 11.5 %all-to-all-start.4 = ((f32[32,4,128]{2,1,0:T(4,128)}), f32[32,4,128]{2,1,0:T(4,128)S(1)}, u32[]{:S(2)}, u32[]{:S(2)}) async-start(f32[32,4,128]{2,1,0:T(4,128)} %get-tuple-element.181), calls=%async_computation.4 | async-start | bytes 131072 | tf_op jit(solution)/shard_map/all_to_all | solution.py:973
  93.7 20.1 %collective-permute-start.13 = (bf16[1552,128]{1,0:T(8,128)(2,1)S(1)}, bf16[1552,128]{1,0:T(8,128)(2,1)S(1)}, u32[]{:S(2)}, u32[]{:S(2)}) collective-permute-start(bf16[1552,128]{1,0:T(8,128)(2,1)S(1)} %get-tuple-element.206), channel_id=1, source_target_pairs={{0,2},{1,3},{2,0},{3,1},{4,6},{5,7},{6,4},{7,5},{8,10},{9,11},{10,... | collective-permute-start | bytes 1191944 | tf_op jit(solution)/shard_map/ppermute | solution.py:978
  113.8 10.0 %all-to-all-start.6 = ((f32[32,4,128]{2,1,0:T(4,128)}), f32[32,4,128]{2,1,0:T(4,128)S(1)}, u32[]{:S(2)}, u32[]{:S(2)}) async-start(f32[32,4,128]{2,1,0:T(4,128)} %get-tuple-element.207), calls=%async_computation.6 | async-start | bytes 131072 | tf_op jit(solution)/shard_map/all_to_all | solution.py:973
  124.7 16.6 %all-to-all-start.7 = ((bf16[8,208,128]{2,1,0:T(8,128)(2,1)}), bf16[8,208,128]{2,1,0:T(8,128)(2,1)S(1)}, u32[]{:S(2)}, u32[]{:S(2)}) async-start(bf16[8,208,128]{2,1,0:T(8,128)(2,1)} %shard_map.276), calls=%async_computation.7 | async-start | bytes 851968 | tf_op jit(solution)/shard_map/all_to_all | solution.py:1161
  129.2 17.6 %collective-permute-start.17 = (bf16[2080,128]{1,0:T(8,128)(2,1)}, bf16[2080,128]{1,0:T(8,128)(2,1)S(1)}, u32[]{:S(2)}, u32[]{:S(2)}) collective-permute-start(bf16[2080,128]{1,0:T(8,128)(2,1)} %get-tuple-element.233), channel_id=1, source_target_pairs={{0,2},{1,3},{2,0},{3,1},{4,6},{5,7},{6,4},{7,5},{8,10},{9,11},{10,... | collective-permute-start | bytes 1597448 | tf_op jit(solution)/shard_map/ppermute | solution.py:978
  137.5 9.3 %collective-permute-start.16 = (bf16[528,128]{1,0:T(8,128)(2,1)S(1)}, bf16[528,128]{1,0:T(8,128)(2,1)S(1)}, u32[]{:S(2)}, u32[]{:S(2)}) collective-permute-start(bf16[528,128]{1,0:T(8,128)(2,1)S(1)} %get-tuple-element.232), channel_id=1, source_target_pairs={{0,2},{1,3},{2,0},{3,1},{4,6},{5,7},{6,4},{7,5},{8,10},{9,11},{10,... | collective-permute-start | bytes 405512 | tf_op jit(solution)/shard_map/ppermute | solution.py:978
  147.9 24.6 %all-to-all-start.8 = ((bf16[8,368,128]{2,1,0:T(8,128)(2,1)}), bf16[8,368,128]{2,1,0:T(8,128)(2,1)S(1)}, u32[]{:S(2)}, u32[]{:S(2)}) async-start(bf16[8,368,128]{2,1,0:T(8,128)(2,1)} %shard_map.274), calls=%async_computation.8 | async-start | bytes 1507328 | tf_op jit(solution)/shard_map/all_to_all | solution.py:1188
  155.5 18.0 %collective-permute-start.21 = (bf16[512,128]{1,0:T(8,128)(2,1)S(1)}, bf16[512,128]{1,0:T(8,128)(2,1)S(1)}, u32[]{:S(2)}, u32[]{:S(2)}) collective-permute-start(bf16[512,128]{1,0:T(8,128)(2,1)S(1)} %get-tuple-element.243), channel_id=1, source_target_pairs={{0,1},{1,0},{2,3},{3,2},{4,5},{5,4},{6,7},{7,6},{8,9},{9,8},{10,11... | collective-permute-start | bytes 393224 | tf_op jit(solution)/shard_map/ppermute | solution.py:978
  155.8 17.7 %collective-permute-start.22 = (bf16[512,128]{1,0:T(8,128)(2,1)S(1)}, bf16[512,128]{1,0:T(8,128)(2,1)S(1)}, u32[]{:S(2)}, u32[]{:S(2)}) collective-permute-start(bf16[512,128]{1,0:T(8,128)(2,1)S(1)} %get-tuple-element.245), channel_id=1, source_target_pairs={{0,2},{1,3},{2,0},{3,1},{4,6},{5,7},{6,4},{7,5},{8,10},{9,11},{10,... | collective-permute-start | bytes 393224 | tf_op jit(solution)/shard_map/ppermute | solution.py:978
  156.7 16.9 %collective-permute-start.23 = (bf16[512,128]{1,0:T(8,128)(2,1)S(1)}, bf16[512,128]{1,0:T(8,128)(2,1)S(1)}, u32[]{:S(2)}, u32[]{:S(2)}) collective-permute-start(bf16[512,128]{1,0:T(8,128)(2,1)S(1)} %get-tuple-element.247), channel_id=1, source_target_pairs={{0,3},{1,2},{2,1},{3,0},{4,7},{5,6},{6,5},{7,4},{8,11},{9,10},{10,... | collective-permute-start | bytes 393224 | tf_op jit(solution)/shard_map/ppermute | solution.py:978
  188.0 24.6 %all-to-all-start.10 = ((bf16[8,416,128]{2,1,0:T(8,128)(2,1)}), bf16[8,416,128]{2,1,0:T(8,128)(2,1)S(1)}, u32[]{:S(2)}, u32[]{:S(2)}) async-start(bf16[8,416,128]{2,1,0:T(8,128)(2,1)} %get-tuple-element.255), calls=%async_computation.10 | async-start | bytes 1703936 | tf_op jit(solution)/shard_map/all_to_all | solution.py:1209
  191.6 8.5 %collective-permute-start.25 = (bf16[8,160,128]{2,1,0:T(8,128)(2,1)S(1)}, bf16[8,160,128]{2,1,0:T(8,128)(2,1)S(1)}, u32[]{:S(2)}, u32[]{:S(2)}) collective-permute-start(bf16[8,160,128]{2,1,0:T(8,128)(2,1)S(1)} %all_to_all.56.refs_1_.refs_0_.refs_2_), channel_id=1, source_target_pairs={{0,2},{1,3},{2,0},{3,1},{4,6},{5,7},{6,4},{7,5},{8,10},{9,11},{10,... | collective-permute-start | bytes 983048 | tf_op jit(solution)/shard_map/ppermute | solution.py:978
  191.9 10.2 %collective-permute-start.24 = (bf16[8,160,128]{2,1,0:T(8,128)(2,1)S(1)}, bf16[8,160,128]{2,1,0:T(8,128)(2,1)S(1)}, u32[]{:S(2)}, u32[]{:S(2)}) collective-permute-start(bf16[8,160,128]{2,1,0:T(8,128)(2,1)S(1)} %all_to_all.56.refs_1_.refs_0_.refs_2_), channel_id=1, source_target_pairs={{0,1},{1,0},{2,3},{3,2},{4,5},{5,4},{6,7},{7,6},{8,9},{9,8},{10,11... | collective-permute-start | bytes 983048 | tf_op jit(solution)/shard_map/ppermute | solution.py:978
  (20 other events, 97.4 us)

commit v5 on v4

--- a/solution.py
+++ b/solution.py
@@ -879,9 +879,9 @@
     for mine, got, spans in zip(ins[::2], ins[1::2], order, strict=True):
         mine, got = mine(), got()
         row = 0
-        for rows, size, base in spans:
-            for i in range(0, out.shape[0] * size, 16):
-                d, top = i // size, base + i % size
+        for rows, size, base, first, last in spans:
+            for i in range(0, out.shape[0] * size - first if last else rows, 16):
+                d, top = (first + i) // size, base + (first + i) % size
                 if i < rows:
                     at = slice(row + i, row + i + 16)
                     total = (mine[at, :].astype(F32) + got[at, :].astype(F32)).astype(out.dtype)
@@ -908,8 +908,8 @@
     rows = pieces().shape[1]
     for at in chunks(rows, rows // 16):
         low = piece_total(pieces(), at)
-        inputs = at.start < 2 * in_piece
-        out, top = (first.ref, at.start) if inputs else (rest.ref, at.start - 2 * in_piece)
+        inputs = at.start < in_piece
+        out, top = (first.ref, at.start) if inputs else (rest.ref, at.start - in_piece)
         for d in range(out.shape[0]):
             out[d, top : top + 16, :] = low
     for at in chunks(vgo_piece, vgo_piece // 16):
@@ -931,8 +931,8 @@
              o_grad, skip_grad, v_grad, g_grad, vb, gb, d_grad, p_grad, s_grad):
     begin()
     full, full_in = full(), full_in()
-    decay, phase = decay(), phase()
     in_piece, vgo_piece = sizes
+    in_rows = features + 16
     for layer in range(2):
         base = layer * vgo_piece
         for i, out in enumerate((v_grad, g_grad, o_grad)):
@@ -940,13 +940,16 @@
                 out.ref[layer, at : at + count, :] = rows.astype(F32)
             copies.flush(out.ref.at[layer], out.dst.at[layer])
             out.sent = True
+    decay, phase = decay(), phase()
+    for layer in range(2):
+        base = layer * vgo_piece
         row = slice(layer, layer + 1)
         ((_, _, vecs),) = unpieced(full, base, vgo_piece, 3 * features, 16)
         vecs = vecs.astype(F32)
         vb.ref[row, :] = vecs[0:1, :]
         gb.ref[row, :] = vecs[1:2, :]
         skip_grad.ref[row, :] = vecs[2:3, :]
-        ((_, _, tile),) = unpieced(full_in, layer * in_piece, in_piece, features, 16)
+        ((_, _, tile),) = unpieced(full_in, 0, in_piece, layer * in_rows + features, 16)
         tile = tile.astype(F32)
         for h in range(2):
             cols = slice(h * LANES, (h + 1) * LANES)
@@ -961,7 +964,7 @@
     for k, pieces in enumerate((p0, p1, p2, p3)):
         cols = pl.ds(pl.multiple_of((mp ^ k) * LANES, LANES), LANES)
         for layer in range(out.ref.shape[0]):
-            for at, count, rows in unpieced(pieces(), layer * size, size, 0, features):
+            for at, count, rows in unpieced(pieces(), 0, size, layer * (features + 16), features):
                 out.ref[layer, at : at + count, cols] = rows.astype(F32)
 
 
@@ -1145,14 +1148,14 @@
         scalars=1,
     )
     unit = 16 * count_dp
-    in_piece, vgo_piece = (-(-n // unit) * 16 for n in (in_rows, vgo_rows))
+    in_piece, vgo_piece = (-(-n // unit) * 16 for n in (2 * in_rows, vgo_rows))
 
     def joined(order, *operands):
-        piece = max(base + size for spans in order for _, size, base in spans)
+        piece = max(base + size for spans in order for _, size, base, _, _ in spans)
         out = Near(shape((count_dp, piece, width), BF16))
         return call(functools.partial(four_sum, order), [out], [], *map(Near, operands))[0]
 
-    own1 = joined((((vgo_rows, vgo_piece, 0),),), mine1, far1)
+    own1 = joined((((vgo_rows, vgo_piece, 0, 0, True),),), mine1, far1)
     got = Near(every(after(ends_all, far1)))
     keep0, send0 = call(
         functools.partial(both_grads, 0), [both_half, both_half], [both_pack] + in_room[1:],
@@ -1181,14 +1184,14 @@
     in_far0 = hop(in_other0, 2)
 
     order = (
-        ((in_rows, in_piece, 0),),
-        ((vgo_rows, vgo_piece, 2 * in_piece), (in_rows, in_piece, in_piece)),
+        ((in_rows, in_piece, 0, 0, False),),
+        ((vgo_rows, vgo_piece, in_piece, 0, True), (in_rows, in_piece, 0, in_rows, True)),
     )
     own0 = joined(order, in_mine0, in_far0, mine0, far0)
     pieces = lax.all_to_all(after(own0, summed1), "dp", 0, 0)
     first, rest = call(
         functools.partial(piece_sums, (in_piece, vgo_piece)),
-        [Near(shape((count_dp, 2 * n, width), BF16)) for n in (in_piece, vgo_piece)],
+        [Near(shape((count_dp, n, width), BF16)) for n in (in_piece, 2 * vgo_piece)],
         [],
         Near(pieces), Near(summed1),
     )

time: 216 us -> 214 us (level)
  no operation moved by 1% of the time
where the time goes in v5:
time: 214 us; the launch traced here: 213 us
  waiting for transfers between devices  69.9 us (33%)
  Pallas kernels  65.5 us (31%)
  starting transfers between devices  48 us (22%)
  blocking collectives  26.5 us (12%)
    pallas_call x28, Pallas kernels, call(): return made_call(max(used[0], 1))(*plain)  65.5 us
    all_to_all x6, waiting for transfers between devices, every(): return lax.all_to_all(x, AXES, 0, 0)  25.5 us
    ppermute x27, waiting for transfers between devices, hop(): return lax.ppermute(x, 'mp', [(i, i ^ k) for i in range(count)])  24 us
    all_to_all x6, starting transfers between devices, every(): return lax.all_to_all(x, AXES, 0, 0)  20 us
    ppermute x27, starting transfers between devices, hop(): return lax.ppermute(x, 'mp', [(i, i ^ k) for i in range(count)])  15.3 us
    all_to_all x1, blocking collectives, on_device(): full_in = lax.all_to_all(after(first, result, *us[1:]), 'dp', 0, 0)  13.9 us
    all_to_all x1, blocking collectives, every(): return lax.all_to_all(x, AXES, 0, 0)  12.5 us
    all_to_all x1, waiting for transfers between devices, on_device(): full = lax.all_to_all(rest, 'dp', 0, 0)  9.53 us
  transfers between devices with their start and end apart: 36, of which 18 were waited for; matrix products, arithmetic and copies ran while one was open for 0% of the time, Pallas kernels for 25%

profile of v5, /device:TPU:0, one launch (start us, length us, event | category | flops | bytes accessed | tf_op | source)
XLA Modules:
  0.0 212.8 jit_solution(10710164291865373024)
XLA Ops:
  15.3 4.9 %all-to-all-start = ((f32[32,4,128]{2,1,0:T(4,128)}), f32[32,4,128]{2,1,0:T(4,128)S(1)}, u32[]{:S(2)}, u32[]{:S(2)}) async-start(f32[32,4,128]{2,1,0:T(4,128)} %get-tuple-element.144), calls=%async_computation | async-start | bytes 131072 | tf_op jit(solution)/shard_map/all_to_all | solution.py:976
  21.6 6.1 %all-to-all-done.refs_1_.refs_2_ = f32[32,4,128]{2,1,0:T(4,128)S(1)} async-done(((f32[32,4,128]{2,1,0:T(4,128)}), f32[32,4,128]{2,1,0:T(4,128)S(1)}, u32[]{:S(2)}, u32[]{:S(2)}) %all-to-all-start) | async-done | bytes 65568 | tf_op jit(solution)/shard_map/all_to_all | solution.py:976
  29.6 3.2 %all-to-all-start.1 = ((f32[32,4,128]{2,1,0:T(4,128)}), f32[32,4,128]{2,1,0:T(4,128)S(1)}, u32[]{:S(2)}, u32[]{:S(2)}) async-start(f32[32,4,128]{2,1,0:T(4,128)} %get-tuple-element.150), calls=%async_computation.1 | async-start | bytes 131072 | tf_op jit(solution)/shard_map/all_to_all | solution.py:976
  32.9 3.6 %shard_map.258.refs_9_.refs_12_ = bf16[3,512,512]{2,1,0:T(8,128)(2,1)} custom-call(bf16[1536,128]{1,0:T(8,128)(2,1)} %get-tuple-element.152.refs_0_, bf16[1536,128]{1,0:T(8,128)(2,1)} %collective-permute-done.3.refs_1_, bf16[1536,128]{1,0:T(8,128)(2,1)S(1)} %collective-permute-done.4.refs_2_, bf16[1536,128]{1,0:T(8,128)(2,1)} %collective-permute-done.5.refs_3_), custom_call_target="tpu_custom_call" | custom-call | tf_op jit(solution)/shard_map/pallas_call | solution.py:171
  36.5 3.8 %all-to-all-done.1.refs_1_ = f32[32,4,128]{2,1,0:T(4,128)S(1)} async-done(((f32[32,4,128]{2,1,0:T(4,128)}), f32[32,4,128]{2,1,0:T(4,128)S(1)}, u32[]{:S(2)}, u32[]{:S(2)}) %all-to-all-start.1) | async-done | bytes 65568 | tf_op jit(solution)/shard_map/all_to_all | solution.py:976
  40.7 5.4 %shard_map.259 = (f32[4,512,128]{2,1,0:T(8,128)S(1)}, f32[32,8,128]{2,1,0:T(8,128)}, f32[4,512,128]{2,1,0:T(8,128)}, bf16[512,512]{1,0:T(8,128)(2,1)}, bf16[512,...) custom-call(s32[1]{0:T(128)S(6)} %copy.29.refs_0_, ...), custom_call_target="tpu_custom_call" | custom-call | tf_op jit(solution)/shard_map/pallas_call | solution.py:171
  51.0 5.9 %all-to-all-done.2.refs_1_ = f32[32,8,128]{2,1,0:T(8,128)S(1)} async-done(((f32[32,8,128]{2,1,0:T(8,128)}), f32[32,8,128]{2,1,0:T(8,128)S(1)}, u32[]{:S(2)}, u32[]{:S(2)}) %all-to-all-start.2) | async-done | bytes 131104 | tf_op jit(solution)/shard_map/all_to_all | solution.py:976
  64.0 3.7 %shard_map.262.refs_9_ = bf16[3,512,512]{2,1,0:T(8,128)(2,1)} custom-call(bf16[1536,128]{1,0:T(8,128)(2,1)} %get-tuple-element.168.refs_0_, bf16[1536,128]{1,0:T(8,128)(2,1)S(1)} %collective-permute-done.6.refs_1_, bf16[1536,128]{1,0:T(8,128)(2,1)} %collective-permute-done.7.refs_2_, bf16[1536,128]{1,0:T(8,128)(2,1)} %collective-permute-done.8.refs_3_), custom_call_target="tpu_custom_call" | custom-call | tf_op jit(solution)/shard_map/pallas_call | solution.py:171
  71.4 7.4 %shard_map.264 = (f32[4,512,128]{2,1,0:T(8,128)S(1)}, f32[32,4,128]{2,1,0:T(4,128)}, f32[4,8,128]{2,1,0:T(8,128)S(1)}, f32[4,512,128]{2,1,0:T(8,128)}, bf16[512,...) custom-call(s32[1]{0:T(128)S(6)} %copy.29.refs_0_, ...), custom_call_target="tpu_custom_call" | custom-call | tf_op jit(solution)/shard_map/pallas_call | solution.py:171
  78.8 4.1 %all-to-all-start.4 = ((f32[32,4,128]{2,1,0:T(4,128)}), f32[32,4,128]{2,1,0:T(4,128)S(1)}, u32[]{:S(2)}, u32[]{:S(2)}) async-start(f32[32,4,128]{2,1,0:T(4,128)} %get-tuple-element.181), calls=%async_computation.4 | async-start | bytes 131072 | tf_op jit(solution)/shard_map/all_to_all | solution.py:976
  85.7 4.6 %all-to-all-done.4.refs_1_ = f32[32,4,128]{2,1,0:T(4,128)S(1)} async-done(((f32[32,4,128]{2,1,0:T(4,128)}), f32[32,4,128]{2,1,0:T(4,128)S(1)}, u32[]{:S(2)}, u32[]{:S(2)}) %all-to-all-start.4) | async-done | bytes 65568 | tf_op jit(solution)/shard_map/all_to_all | solution.py:976
  94.3 12.5 %all_to_all.55.refs_1_ = f32[32,8,128]{2,1,0:T(8,128)S(1)} all-to-all(f32[32,8,128]{2,1,0:T(8,128)S(1)} %get-tuple-element.194), channel_id=1, replica_groups=mesh['dp'=8,'mp'=4] {'dp','mp'}, dimensions={0} | all-to-all | bytes 262144 | tf_op jit(solution)/shard_map/all_to_all | solution.py:976
  106.8 5.9 %shard_map.268 = (f32[4,512,128]{2,1,0:T(8,128)}, f32[4,512,128]{2,1,0:T(8,128)S(1)}, f32[32,4,128]{2,1,0:T(4,128)}, f32[4,8,128]{2,1,0:T(8,128)S(1)}, f32[8,128...) custom-call(s32[1]{0:T(128)S(6)} %copy.29.refs_0_, ...), custom_call_target="tpu_custom_call" | custom-call | tf_op jit(solution)/shard_map/pallas_call | solution.py:171
  116.3 3.6 %shard_map.269 = (bf16[2,2080,128]{2,1,0:T(8,128)(2,1)S(1)}, bf16[2,2080,128]{2,1,0:T(8,128)(2,1)S(1)}) custom-call(bf16[512,512]{1,0:T(8,128)(2,1)} %get-tuple-element.208.refs_0_, bf16[512,512]{1,0:T(8,128)(2,1)} %get-tuple-element.209.refs_1_, bf16[512,512]{1,0:T(8,128)(2,1)} %get-tuple-element.210.refs_2_, ...), custom_call_target="tpu_custom_call" | custom-call | tf_op jit(solution)/shard_map/pallas_call | solution.py:171
  120.0 3.7 %all-to-all-done.6.refs_1_ = f32[32,4,128]{2,1,0:T(4,128)S(1)} async-done(((f32[32,4,128]{2,1,0:T(4,128)}), f32[32,4,128]{2,1,0:T(4,128)S(1)}, u32[]{:S(2)}, u32[]{:S(2)}) %all-to-all-start.6) | async-done | bytes 65568 | tf_op jit(solution)/shard_map/all_to_all | solution.py:976
  124.7 3.5 %all-to-all-start.7 = ((bf16[8,208,128]{2,1,0:T(8,128)(2,1)}), bf16[8,208,128]{2,1,0:T(8,128)(2,1)S(1)}, u32[]{:S(2)}, u32[]{:S(2)}) async-start(bf16[8,208,128]{2,1,0:T(8,128)(2,1)} %shard_map.276), calls=%async_computation.7 | async-start | bytes 851968 | tf_op jit(solution)/shard_map/all_to_all | solution.py:1164
  130.4 3.5 %shard_map.270 = (f32[8,512]{1,0:T(8,128)S(1)}, f32[8,128]{1,0:T(8,128)S(1)}, bf16[512,512]{1,0:T(8,128)(2,1)S(1)}, f32[512,128]{1,0:T(8,128)S(1)}, bf16[512,128...) custom-call(s32[1]{0:T(128)S(6)} %copy.29.refs_0_, ...), custom_call_target="tpu_custom_call" | custom-call | tf_op jit(solution)/shard_map/pallas_call | solution.py:171
  141.4 5.4 %collective-permute-done.16.refs_1_ = bf16[528,128]{1,0:T(8,128)(2,1)S(1)} collective-permute-done((bf16[528,128]{1,0:T(8,128)(2,1)S(1)}, bf16[528,128]{1,0:T(8,128)(2,1)S(1)}, u32[]{:S(2)}, u32[]{:S(2)}) %collective-permute-start.16) | collective-permute-done | bytes 135200 | tf_op jit(solution)/shard_map/ppermute | solution.py:981
  147.8 5.7 %all-to-all-start.8 = ((bf16[8,352,128]{2,1,0:T(8,128)(2,1)}), bf16[8,352,128]{2,1,0:T(8,128)(2,1)S(1)}, u32[]{:S(2)}, u32[]{:S(2)}) async-start(bf16[8,352,128]{2,1,0:T(8,128)(2,1)} %shard_map.274), calls=%async_computation.8 | async-start | bytes 1441792 | tf_op jit(solution)/shard_map/all_to_all | solution.py:1191
  163.7 8.0 %all-to-all-done.8.refs_0_ = bf16[8,352,128]{2,1,0:T(8,128)(2,1)S(1)} async-done(((bf16[8,352,128]{2,1,0:T(8,128)(2,1)}), bf16[8,352,128]{2,1,0:T(8,128)(2,1)S(1)}, u32[]{:S(2)}, u32[]{:S(2)}) %all-to-all-start.8) | async-done | bytes 720928 | tf_op jit(solution)/shard_map/all_to_all | solution.py:1191
  172.8 13.9 %all_to_all.56.refs_1_.refs_0_.refs_2_ = bf16[8,144,128]{2,1,0:T(8,128)(2,1)S(1)} all-to-all(bf16[8,144,128]{2,1,0:T(8,128)(2,1)S(1)} %get-tuple-element.248), channel_id=1, replica_groups=mesh['dp'=8,'mp'=4] {'dp'}, dimensions={0} | all-to-all | bytes 589824 | tf_op jit(solution)/shard_map/all_to_all | solution.py:1200
  186.7 3.5 %all-to-all-start.10 = ((bf16[8,416,128]{2,1,0:T(8,128)(2,1)}), bf16[8,416,128]{2,1,0:T(8,128)(2,1)S(1)}, u32[]{:S(2)}, u32[]{:S(2)}) async-start(bf16[8,416,128]{2,1,0:T(8,128)(2,1)} %get-tuple-element.255), calls=%async_computation.10 | async-start | bytes 1703936 | tf_op jit(solution)/shard_map/all_to_all | solution.py:1212
  190.5 7.4 %collective-permute-done.25.refs_2_ = bf16[8,144,128]{2,1,0:T(8,128)(2,1)S(1)} collective-permute-done((bf16[8,144,128]{2,1,0:T(8,128)(2,1)S(1)}, bf16[8,144,128]{2,1,0:T(8,128)(2,1)S(1)}, u32[]{:S(2)}, u32[]{:S(2)}) %collective-permute-start.25) | collective-permute-done | bytes 294944 | tf_op jit(solution)/shard_map/ppermute | solution.py:981
  201.7 9.5 %all-to-all-done.10.refs_3_ = bf16[8,416,128]{2,1,0:T(8,128)(2,1)S(1)} async-done(((bf16[8,416,128]{2,1,0:T(8,128)(2,1)}), bf16[8,416,128]{2,1,0:T(8,128)(2,1)S(1)}, u32[]{:S(2)}, u32[]{:S(2)}) %all-to-all-start.10) | async-done | bytes 852000 | tf_op jit(solution)/shard_map/all_to_all | solution.py:1212
  (94 shorter events, 71.9 us)
Async XLA Ops:
  12.4 15.3 %collective-permute-start.4 = (bf16[1536,128]{1,0:T(8,128)(2,1)}, bf16[1536,128]{1,0:T(8,128)(2,1)S(1)}, u32[]{:S(2)}, u32[]{:S(2)}) collective-permute-start(bf16[1536,128]{1,0:T(8,128)(2,1)} %get-tuple-element.152.refs_0_), channel_id=1, source_target_pairs={{0,2},{1,3},{2,0},{3,1},{4,6},{5,7},{6,4},{7,5},{8,10},{9,11},{10,... | collective-permute-start | bytes 1179656 | tf_op jit(solution)/shard_map/ppermute | solution.py:981
  15.3 12.4 %all-to-all-start = ((f32[32,4,128]{2,1,0:T(4,128)}), f32[32,4,128]{2,1,0:T(4,128)S(1)}, u32[]{:S(2)}, u32[]{:S(2)}) async-start(f32[32,4,128]{2,1,0:T(4,128)} %get-tuple-element.144), calls=%async_computation | async-start | bytes 131072 | tf_op jit(solution)/shard_map/all_to_all | solution.py:976
  20.3 12.6 %collective-permute-start.3 = (bf16[1536,128]{1,0:T(8,128)(2,1)}, bf16[1536,128]{1,0:T(8,128)(2,1)}, u32[]{:S(2)}, u32[]{:S(2)}) collective-permute-start(bf16[1536,128]{1,0:T(8,128)(2,1)} %get-tuple-element.152.refs_0_), channel_id=1, source_target_pairs={{0,1},{1,0},{2,3},{3,2},{4,5},{5,4},{6,7},{7,6},{8,9},{9,8},{10,11... | collective-permute-start | bytes 1179656 | tf_op jit(solution)/shard_map/ppermute | solution.py:981
  29.6 10.6 %all-to-all-start.1 = ((f32[32,4,128]{2,1,0:T(4,128)}), f32[32,4,128]{2,1,0:T(4,128)S(1)}, u32[]{:S(2)}, u32[]{:S(2)}) async-start(f32[32,4,128]{2,1,0:T(4,128)} %get-tuple-element.150), calls=%async_computation.1 | async-start | bytes 131072 | tf_op jit(solution)/shard_map/all_to_all | solution.py:976
  40.3 16.7 %collective-permute-start.7 = (bf16[1536,128]{1,0:T(8,128)(2,1)}, bf16[1536,128]{1,0:T(8,128)(2,1)}, u32[]{:S(2)}, u32[]{:S(2)}) collective-permute-start(bf16[1536,128]{1,0:T(8,128)(2,1)} %get-tuple-element.168.refs_0_), channel_id=1, source_target_pairs={{0,2},{1,3},{2,0},{3,1},{4,6},{5,7},{6,4},{7,5},{8,10},{9,11},{10,... | collective-permute-start | bytes 1179656 | tf_op jit(solution)/shard_map/ppermute | solution.py:981
  46.1 10.8 %all-to-all-start.2 = ((f32[32,8,128]{2,1,0:T(8,128)}), f32[32,8,128]{2,1,0:T(8,128)S(1)}, u32[]{:S(2)}, u32[]{:S(2)}) async-start(f32[32,8,128]{2,1,0:T(8,128)} %get-tuple-element.158), calls=%async_computation.2 | async-start | bytes 262144 | tf_op jit(solution)/shard_map/all_to_all | solution.py:976
  48.7 15.3 %collective-permute-start.6 = (bf16[1536,128]{1,0:T(8,128)(2,1)}, bf16[1536,128]{1,0:T(8,128)(2,1)S(1)}, u32[]{:S(2)}, u32[]{:S(2)}) collective-permute-start(bf16[1536,128]{1,0:T(8,128)(2,1)} %get-tuple-element.168.refs_0_), channel_id=1, source_target_pairs={{0,1},{1,0},{2,3},{3,2},{4,5},{5,4},{6,7},{7,6},{8,9},{9,8},{10,11... | collective-permute-start | bytes 1179656 | tf_op jit(solution)/shard_map/ppermute | solution.py:981
  59.5 8.2 %collective-permute-start.9 = (bf16[512,128]{1,0:T(8,128)(2,1)}, bf16[512,128]{1,0:T(8,128)(2,1)S(1)}, u32[]{:S(2)}, u32[]{:S(2)}) collective-permute-start(bf16[512,128]{1,0:T(8,128)(2,1)} %get-tuple-element.171), channel_id=1, source_target_pairs={{0,1},{1,0},{2,3},{3,2},{4,5},{5,4},{6,7},{7,6},{8,9},{9,8},{10,11... | collective-permute-start | bytes 393224 | tf_op jit(solution)/shard_map/ppermute | solution.py:981
  59.8 7.8 %collective-permute-start.10 = (bf16[512,128]{1,0:T(8,128)(2,1)}, bf16[512,128]{1,0:T(8,128)(2,1)S(1)}, u32[]{:S(2)}, u32[]{:S(2)}) collective-permute-start(bf16[512,128]{1,0:T(8,128)(2,1)} %get-tuple-element.172), channel_id=1, source_target_pairs={{0,2},{1,3},{2,0},{3,1},{4,6},{5,7},{6,4},{7,5},{8,10},{9,11},{10,... | collective-permute-start | bytes 393224 | tf_op jit(solution)/shard_map/ppermute | solution.py:981
  60.3 7.5 %collective-permute-start.11 = (bf16[512,128]{1,0:T(8,128)(2,1)S(1)}, bf16[512,128]{1,0:T(8,128)(2,1)S(1)}, u32[]{:S(2)}, u32[]{:S(2)}) collective-permute-start(bf16[512,128]{1,0:T(8,128)(2,1)S(1)} %copy-done.7), channel_id=1, source_target_pairs={{0,3},{1,2},{2,1},{3,0},{4,7},{5,6},{6,5},{7,4},{8,11},{9,10},{10,... | collective-permute-start | bytes 393224 | tf_op jit(solution)/shard_map/ppermute | solution.py:981
  61.4 10.0 %all-to-all-start.3 = ((f32[32,4,128]{2,1,0:T(4,128)}), f32[32,4,128]{2,1,0:T(4,128)S(1)}, u32[]{:S(2)}, u32[]{:S(2)}) async-start(f32[32,4,128]{2,1,0:T(4,128)} %get-tuple-element.166), calls=%async_computation.3 | async-start | bytes 131072 | tf_op jit(solution)/shard_map/all_to_all | solution.py:976
  78.8 11.5 %all-to-all-start.4 = ((f32[32,4,128]{2,1,0:T(4,128)}), f32[32,4,128]{2,1,0:T(4,128)S(1)}, u32[]{:S(2)}, u32[]{:S(2)}) async-start(f32[32,4,128]{2,1,0:T(4,128)} %get-tuple-element.181), calls=%async_computation.4 | async-start | bytes 131072 | tf_op jit(solution)/shard_map/all_to_all | solution.py:976
  93.7 20.1 %collective-permute-start.13 = (bf16[1552,128]{1,0:T(8,128)(2,1)S(1)}, bf16[1552,128]{1,0:T(8,128)(2,1)S(1)}, u32[]{:S(2)}, u32[]{:S(2)}) collective-permute-start(bf16[1552,128]{1,0:T(8,128)(2,1)S(1)} %get-tuple-element.206), channel_id=1, source_target_pairs={{0,2},{1,3},{2,0},{3,1},{4,6},{5,7},{6,4},{7,5},{8,10},{9,11},{10,... | collective-permute-start | bytes 1191944 | tf_op jit(solution)/shard_map/ppermute | solution.py:981
  113.8 10.0 %all-to-all-start.6 = ((f32[32,4,128]{2,1,0:T(4,128)}), f32[32,4,128]{2,1,0:T(4,128)S(1)}, u32[]{:S(2)}, u32[]{:S(2)}) async-start(f32[32,4,128]{2,1,0:T(4,128)} %get-tuple-element.207), calls=%async_computation.6 | async-start | bytes 131072 | tf_op jit(solution)/shard_map/all_to_all | solution.py:976
  124.7 16.6 %all-to-all-start.7 = ((bf16[8,208,128]{2,1,0:T(8,128)(2,1)}), bf16[8,208,128]{2,1,0:T(8,128)(2,1)S(1)}, u32[]{:S(2)}, u32[]{:S(2)}) async-start(bf16[8,208,128]{2,1,0:T(8,128)(2,1)} %shard_map.276), calls=%async_computation.7 | async-start | bytes 851968 | tf_op jit(solution)/shard_map/all_to_all | solution.py:1164
  129.2 17.6 %collective-permute-start.17 = (bf16[2080,128]{1,0:T(8,128)(2,1)}, bf16[2080,128]{1,0:T(8,128)(2,1)S(1)}, u32[]{:S(2)}, u32[]{:S(2)}) collective-permute-start(bf16[2080,128]{1,0:T(8,128)(2,1)} %get-tuple-element.233), channel_id=1, source_target_pairs={{0,2},{1,3},{2,0},{3,1},{4,6},{5,7},{6,4},{7,5},{8,10},{9,11},{10,... | collective-permute-start | bytes 1597448 | tf_op jit(solution)/shard_map/ppermute | solution.py:981
  137.5 9.3 %collective-permute-start.16 = (bf16[528,128]{1,0:T(8,128)(2,1)S(1)}, bf16[528,128]{1,0:T(8,128)(2,1)S(1)}, u32[]{:S(2)}, u32[]{:S(2)}) collective-permute-start(bf16[528,128]{1,0:T(8,128)(2,1)S(1)} %get-tuple-element.232), channel_id=1, source_target_pairs={{0,2},{1,3},{2,0},{3,1},{4,6},{5,7},{6,4},{7,5},{8,10},{9,11},{10,... | collective-permute-start | bytes 405512 | tf_op jit(solution)/shard_map/ppermute | solution.py:981
  147.8 23.8 %all-to-all-start.8 = ((bf16[8,352,128]{2,1,0:T(8,128)(2,1)}), bf16[8,352,128]{2,1,0:T(8,128)(2,1)S(1)}, u32[]{:S(2)}, u32[]{:S(2)}) async-start(bf16[8,352,128]{2,1,0:T(8,128)(2,1)} %shard_map.274), calls=%async_computation.8 | async-start | bytes 1441792 | tf_op jit(solution)/shard_map/all_to_all | solution.py:1191
  155.5 17.3 %collective-permute-start.21 = (bf16[512,128]{1,0:T(8,128)(2,1)S(1)}, bf16[512,128]{1,0:T(8,128)(2,1)S(1)}, u32[]{:S(2)}, u32[]{:S(2)}) collective-permute-start(bf16[512,128]{1,0:T(8,128)(2,1)S(1)} %get-tuple-element.243), channel_id=1, source_target_pairs={{0,1},{1,0},{2,3},{3,2},{4,5},{5,4},{6,7},{7,6},{8,9},{9,8},{10,11... | collective-permute-start | bytes 393224 | tf_op jit(solution)/shard_map/ppermute | solution.py:981
  155.8 16.9 %collective-permute-start.22 = (bf16[512,128]{1,0:T(8,128)(2,1)S(1)}, bf16[512,128]{1,0:T(8,128)(2,1)S(1)}, u32[]{:S(2)}, u32[]{:S(2)}) collective-permute-start(bf16[512,128]{1,0:T(8,128)(2,1)S(1)} %get-tuple-element.245), channel_id=1, source_target_pairs={{0,2},{1,3},{2,0},{3,1},{4,6},{5,7},{6,4},{7,5},{8,10},{9,11},{10,... | collective-permute-start | bytes 393224 | tf_op jit(solution)/shard_map/ppermute | solution.py:981
  156.6 16.1 %collective-permute-start.23 = (bf16[512,128]{1,0:T(8,128)(2,1)S(1)}, bf16[512,128]{1,0:T(8,128)(2,1)S(1)}, u32[]{:S(2)}, u32[]{:S(2)}) collective-permute-start(bf16[512,128]{1,0:T(8,128)(2,1)S(1)} %get-tuple-element.247), channel_id=1, source_target_pairs={{0,3},{1,2},{2,1},{3,0},{4,7},{5,6},{6,5},{7,4},{8,11},{9,10},{10,... | collective-permute-start | bytes 393224 | tf_op jit(solution)/shard_map/ppermute | solution.py:981
  186.7 24.5 %all-to-all-start.10 = ((bf16[8,416,128]{2,1,0:T(8,128)(2,1)}), bf16[8,416,128]{2,1,0:T(8,128)(2,1)S(1)}, u32[]{:S(2)}, u32[]{:S(2)}) async-start(bf16[8,416,128]{2,1,0:T(8,128)(2,1)} %get-tuple-element.255), calls=%async_computation.10 | async-start | bytes 1703936 | tf_op jit(solution)/shard_map/all_to_all | solution.py:1212
  190.3 7.7 %collective-permute-start.25 = (bf16[8,144,128]{2,1,0:T(8,128)(2,1)S(1)}, bf16[8,144,128]{2,1,0:T(8,128)(2,1)S(1)}, u32[]{:S(2)}, u32[]{:S(2)}) collective-permute-start(bf16[8,144,128]{2,1,0:T(8,128)(2,1)S(1)} %all_to_all.56.refs_1_.refs_0_.refs_2_), channel_id=1, source_target_pairs={{0,2},{1,3},{2,0},{3,1},{4,6},{5,7},{6,4},{7,5},{8,10},{9,11},{10,... | collective-permute-start | bytes 884744 | tf_op jit(solution)/shard_map/ppermute | solution.py:981
  190.5 9.5 %collective-permute-start.24 = (bf16[8,144,128]{2,1,0:T(8,128)(2,1)S(1)}, bf16[8,144,128]{2,1,0:T(8,128)(2,1)S(1)}, u32[]{:S(2)}, u32[]{:S(2)}) collective-permute-start(bf16[8,144,128]{2,1,0:T(8,128)(2,1)S(1)} %all_to_all.56.refs_1_.refs_0_.refs_2_), channel_id=1, source_target_pairs={{0,1},{1,0},{2,3},{3,2},{4,5},{5,4},{6,7},{7,6},{8,9},{9,8},{10,11... | collective-permute-start | bytes 884744 | tf_op jit(solution)/shard_map/ppermute | solution.py:981
  (20 other events, 97.4 us)

commit v6 on v5

--- a/solution.py
+++ b/solution.py
@@ -801,10 +801,10 @@
     factor, bias, inverse, mean = (norms[i : i + 1, :] for i in range(4))
     one = two = 0.0
     for i, at in enumerate(chunks(rows, 2)):
-        low = (cat(adj, at) * gamma).astype(BF16)
-        dlow.ref[at, :] = low
+        dlow.ref[at, :] = (cat(adj, at) * gamma).astype(BF16)
         dlow.flush(i, 2)
-        dscaled = dot_nt(low, weight()[...]) + dml.part(i)[at, :].astype(F32) * skip
+    for i, at in enumerate(chunks(rows, 2)):
+        dscaled = dot_nt(dlow.ref[at, :], weight()[...]) + dml.part(i)[at, :].astype(F32) * skip
         normed = (cat(h.part(i), at) - mean) * inverse
         own = g()[at, :].astype(F32) if layer == 1 else cat(g.part(i), at)
         put(u_ref, at, own + factor * dscaled)
@@ -1048,7 +1048,7 @@
     )
     table = Near(table)
     got_h = [Near(x) for x in swap(sends)]
-    mom0 = every(after(mom_out, *[g.array for g in got_h]))
+    mom0 = every(after(mom_out, got_h[0].array, got_h[1].array))
     h0, prm = call(
         gather_block,
         [near_blocks, Near(shape((parts, 16, width)))],

time: 214 us -> 214 us (level)
  no operation moved by 1% of the time
where the time goes in v6:
time: 214 us; the launch traced here: 213 us
  waiting for transfers between devices  69.9 us (33%)
  Pallas kernels  65.5 us (31%)
  starting transfers between devices  48 us (22%)
  blocking collectives  26.5 us (12%)
    pallas_call x28, Pallas kernels, call(): return made_call(max(used[0], 1))(*plain)  65.5 us
    all_to_all x6, waiting for transfers between devices, every(): return lax.all_to_all(x, AXES, 0, 0)  25.5 us
    ppermute x27, waiting for transfers between devices, hop(): return lax.ppermute(x, 'mp', [(i, i ^ k) for i in range(count)])  23.9 us
    all_to_all x6, starting transfers between devices, every(): return lax.all_to_all(x, AXES, 0, 0)  20 us
    ppermute x27, starting transfers between devices, hop(): return lax.ppermute(x, 'mp', [(i, i ^ k) for i in range(count)])  15.3 us
    all_to_all x1, blocking collectives, on_device(): full_in = lax.all_to_all(after(first, result, *us[1:]), 'dp', 0, 0)  13.9 us
    all_to_all x1, blocking collectives, every(): return lax.all_to_all(x, AXES, 0, 0)  12.5 us
    all_to_all x1, waiting for transfers between devices, on_device(): full = lax.all_to_all(rest, 'dp', 0, 0)  9.53 us
  transfers between devices with their start and end apart: 36, of which 18 were waited for; matrix products, arithmetic and copies ran while one was open for 0% of the time, Pallas kernels for 25%

profile of v6, /device:TPU:0, one launch (start us, length us, event | category | flops | bytes accessed | tf_op | source)
XLA Modules:
  0.0 212.7 jit_solution(3696133481717582063)
XLA Ops:
  15.3 4.9 %all-to-all-start = ((f32[32,4,128]{2,1,0:T(4,128)}), f32[32,4,128]{2,1,0:T(4,128)S(1)}, u32[]{:S(2)}, u32[]{:S(2)}) async-start(f32[32,4,128]{2,1,0:T(4,128)} %get-tuple-element.143), calls=%async_computation | async-start | bytes 131072 | tf_op jit(solution)/shard_map/all_to_all | solution.py:976
  21.6 6.1 %all-to-all-done.refs_1_.refs_2_ = f32[32,4,128]{2,1,0:T(4,128)S(1)} async-done(((f32[32,4,128]{2,1,0:T(4,128)}), f32[32,4,128]{2,1,0:T(4,128)S(1)}, u32[]{:S(2)}, u32[]{:S(2)}) %all-to-all-start) | async-done | bytes 65568 | tf_op jit(solution)/shard_map/all_to_all | solution.py:976
  29.6 3.2 %all-to-all-start.1 = ((f32[32,4,128]{2,1,0:T(4,128)}), f32[32,4,128]{2,1,0:T(4,128)S(1)}, u32[]{:S(2)}, u32[]{:S(2)}) async-start(f32[32,4,128]{2,1,0:T(4,128)} %get-tuple-element.150), calls=%async_computation.1 | async-start | bytes 131072 | tf_op jit(solution)/shard_map/all_to_all | solution.py:976
  32.9 3.6 %shard_map.258.refs_9_.refs_12_ = bf16[3,512,512]{2,1,0:T(8,128)(2,1)} custom-call(bf16[1536,128]{1,0:T(8,128)(2,1)} %get-tuple-element.152.refs_0_, bf16[1536,128]{1,0:T(8,128)(2,1)} %collective-permute-done.3.refs_1_, bf16[1536,128]{1,0:T(8,128)(2,1)S(1)} %collective-permute-done.4.refs_2_, bf16[1536,128]{1,0:T(8,128)(2,1)} %collective-permute-done.5.refs_3_), custom_call_target="tpu_custom_call" | custom-call | tf_op jit(solution)/shard_map/pallas_call | solution.py:171
  36.5 3.8 %all-to-all-done.1.refs_1_ = f32[32,4,128]{2,1,0:T(4,128)S(1)} async-done(((f32[32,4,128]{2,1,0:T(4,128)}), f32[32,4,128]{2,1,0:T(4,128)S(1)}, u32[]{:S(2)}, u32[]{:S(2)}) %all-to-all-start.1) | async-done | bytes 65568 | tf_op jit(solution)/shard_map/all_to_all | solution.py:976
  40.7 5.4 %shard_map.259 = (f32[4,512,128]{2,1,0:T(8,128)S(1)}, f32[32,8,128]{2,1,0:T(8,128)}, f32[4,512,128]{2,1,0:T(8,128)}, bf16[512,512]{1,0:T(8,128)(2,1)}, bf16[512,...) custom-call(s32[1]{0:T(128)S(6)} %copy.29.refs_0_, ...), custom_call_target="tpu_custom_call" | custom-call | tf_op jit(solution)/shard_map/pallas_call | solution.py:171
  51.0 5.9 %all-to-all-done.2.refs_1_ = f32[32,8,128]{2,1,0:T(8,128)S(1)} async-done(((f32[32,8,128]{2,1,0:T(8,128)}), f32[32,8,128]{2,1,0:T(8,128)S(1)}, u32[]{:S(2)}, u32[]{:S(2)}) %all-to-all-start.2) | async-done | bytes 131104 | tf_op jit(solution)/shard_map/all_to_all | solution.py:976
  64.0 3.7 %shard_map.262.refs_9_ = bf16[3,512,512]{2,1,0:T(8,128)(2,1)} custom-call(bf16[1536,128]{1,0:T(8,128)(2,1)} %get-tuple-element.168.refs_0_, bf16[1536,128]{1,0:T(8,128)(2,1)S(1)} %collective-permute-done.6.refs_1_, bf16[1536,128]{1,0:T(8,128)(2,1)} %collective-permute-done.7.refs_2_, bf16[1536,128]{1,0:T(8,128)(2,1)} %collective-permute-done.8.refs_3_), custom_call_target="tpu_custom_call" | custom-call | tf_op jit(solution)/shard_map/pallas_call | solution.py:171
  71.4 7.4 %shard_map.264 = (f32[4,512,128]{2,1,0:T(8,128)S(1)}, f32[32,4,128]{2,1,0:T(4,128)}, f32[4,8,128]{2,1,0:T(8,128)S(1)}, f32[4,512,128]{2,1,0:T(8,128)}, bf16[512,...) custom-call(s32[1]{0:T(128)S(6)} %copy.29.refs_0_, ...), custom_call_target="tpu_custom_call" | custom-call | tf_op jit(solution)/shard_map/pallas_call | solution.py:171
  78.8 4.1 %all-to-all-start.4 = ((f32[32,4,128]{2,1,0:T(4,128)}), f32[32,4,128]{2,1,0:T(4,128)S(1)}, u32[]{:S(2)}, u32[]{:S(2)}) async-start(f32[32,4,128]{2,1,0:T(4,128)} %get-tuple-element.181), calls=%async_computation.4 | async-start | bytes 131072 | tf_op jit(solution)/shard_map/all_to_all | solution.py:976
  85.7 4.6 %all-to-all-done.4.refs_1_ = f32[32,4,128]{2,1,0:T(4,128)S(1)} async-done(((f32[32,4,128]{2,1,0:T(4,128)}), f32[32,4,128]{2,1,0:T(4,128)S(1)}, u32[]{:S(2)}, u32[]{:S(2)}) %all-to-all-start.4) | async-done | bytes 65568 | tf_op jit(solution)/shard_map/all_to_all | solution.py:976
  94.2 12.5 %all_to_all.55.refs_1_ = f32[32,8,128]{2,1,0:T(8,128)S(1)} all-to-all(f32[32,8,128]{2,1,0:T(8,128)S(1)} %get-tuple-element.194), channel_id=1, replica_groups=mesh['dp'=8,'mp'=4] {'dp','mp'}, dimensions={0} | all-to-all | bytes 262144 | tf_op jit(solution)/shard_map/all_to_all | solution.py:976
  106.8 5.9 %shard_map.268 = (f32[4,512,128]{2,1,0:T(8,128)}, f32[4,512,128]{2,1,0:T(8,128)S(1)}, f32[32,4,128]{2,1,0:T(4,128)}, f32[4,8,128]{2,1,0:T(8,128)S(1)}, f32[8,128...) custom-call(s32[1]{0:T(128)S(6)} %copy.29.refs_0_, ...), custom_call_target="tpu_custom_call" | custom-call | tf_op jit(solution)/shard_map/pallas_call | solution.py:171
  116.3 3.6 %shard_map.269 = (bf16[2,2080,128]{2,1,0:T(8,128)(2,1)S(1)}, bf16[2,2080,128]{2,1,0:T(8,128)(2,1)S(1)}) custom-call(bf16[512,512]{1,0:T(8,128)(2,1)} %get-tuple-element.208.refs_0_, bf16[512,512]{1,0:T(8,128)(2,1)} %get-tuple-element.209.refs_1_, bf16[512,512]{1,0:T(8,128)(2,1)} %get-tuple-element.210.refs_2_, ...), custom_call_target="tpu_custom_call" | custom-call | tf_op jit(solution)/shard_map/pallas_call | solution.py:171
  120.0 3.7 %all-to-all-done.6.refs_1_ = f32[32,4,128]{2,1,0:T(4,128)S(1)} async-done(((f32[32,4,128]{2,1,0:T(4,128)}), f32[32,4,128]{2,1,0:T(4,128)S(1)}, u32[]{:S(2)}, u32[]{:S(2)}) %all-to-all-start.6) | async-done | bytes 65568 | tf_op jit(solution)/shard_map/all_to_all | solution.py:976
  124.7 3.5 %all-to-all-start.7 = ((bf16[8,208,128]{2,1,0:T(8,128)(2,1)}), bf16[8,208,128]{2,1,0:T(8,128)(2,1)S(1)}, u32[]{:S(2)}, u32[]{:S(2)}) async-start(bf16[8,208,128]{2,1,0:T(8,128)(2,1)} %shard_map.276), calls=%async_computation.7 | async-start | bytes 851968 | tf_op jit(solution)/shard_map/all_to_all | solution.py:1164
  130.4 3.6 %shard_map.270 = (f32[8,512]{1,0:T(8,128)S(1)}, f32[8,128]{1,0:T(8,128)S(1)}, bf16[512,512]{1,0:T(8,128)(2,1)S(1)}, f32[512,128]{1,0:T(8,128)S(1)}, bf16[512,128...) custom-call(s32[1]{0:T(128)S(6)} %copy.29.refs_0_, ...), custom_call_target="tpu_custom_call" | custom-call | tf_op jit(solution)/shard_map/pallas_call | solution.py:171
  141.4 5.4 %collective-permute-done.16.refs_1_ = bf16[528,128]{1,0:T(8,128)(2,1)S(1)} collective-permute-done((bf16[528,128]{1,0:T(8,128)(2,1)S(1)}, bf16[528,128]{1,0:T(8,128)(2,1)S(1)}, u32[]{:S(2)}, u32[]{:S(2)}) %collective-permute-start.16) | collective-permute-done | bytes 135200 | tf_op jit(solution)/shard_map/ppermute | solution.py:981
  147.8 5.7 %all-to-all-start.8 = ((bf16[8,352,128]{2,1,0:T(8,128)(2,1)}), bf16[8,352,128]{2,1,0:T(8,128)(2,1)S(1)}, u32[]{:S(2)}, u32[]{:S(2)}) async-start(bf16[8,352,128]{2,1,0:T(8,128)(2,1)} %shard_map.274), calls=%async_computation.8 | async-start | bytes 1441792 | tf_op jit(solution)/shard_map/all_to_all | solution.py:1191
  163.6 8.0 %all-to-all-done.8.refs_0_ = bf16[8,352,128]{2,1,0:T(8,128)(2,1)S(1)} async-done(((bf16[8,352,128]{2,1,0:T(8,128)(2,1)}), bf16[8,352,128]{2,1,0:T(8,128)(2,1)S(1)}, u32[]{:S(2)}, u32[]{:S(2)}) %all-to-all-start.8) | async-done | bytes 720928 | tf_op jit(solution)/shard_map/all_to_all | solution.py:1191
  172.7 13.9 %all_to_all.56.refs_1_.refs_0_.refs_2_ = bf16[8,144,128]{2,1,0:T(8,128)(2,1)S(1)} all-to-all(bf16[8,144,128]{2,1,0:T(8,128)(2,1)S(1)} %get-tuple-element.248), channel_id=1, replica_groups=mesh['dp'=8,'mp'=4] {'dp'}, dimensions={0} | all-to-all | bytes 589824 | tf_op jit(solution)/shard_map/all_to_all | solution.py:1200
  186.7 3.5 %all-to-all-start.10 = ((bf16[8,416,128]{2,1,0:T(8,128)(2,1)}), bf16[8,416,128]{2,1,0:T(8,128)(2,1)S(1)}, u32[]{:S(2)}, u32[]{:S(2)}) async-start(bf16[8,416,128]{2,1,0:T(8,128)(2,1)} %get-tuple-element.255), calls=%async_computation.10 | async-start | bytes 1703936 | tf_op jit(solution)/shard_map/all_to_all | solution.py:1212
  190.5 7.4 %collective-permute-done.25.refs_2_ = bf16[8,144,128]{2,1,0:T(8,128)(2,1)S(1)} collective-permute-done((bf16[8,144,128]{2,1,0:T(8,128)(2,1)S(1)}, bf16[8,144,128]{2,1,0:T(8,128)(2,1)S(1)}, u32[]{:S(2)}, u32[]{:S(2)}) %collective-permute-start.25) | collective-permute-done | bytes 294944 | tf_op jit(solution)/shard_map/ppermute | solution.py:981
  201.6 9.5 %all-to-all-done.10.refs_3_ = bf16[8,416,128]{2,1,0:T(8,128)(2,1)S(1)} async-done(((bf16[8,416,128]{2,1,0:T(8,128)(2,1)}), bf16[8,416,128]{2,1,0:T(8,128)(2,1)S(1)}, u32[]{:S(2)}, u32[]{:S(2)}) %all-to-all-start.10) | async-done | bytes 852000 | tf_op jit(solution)/shard_map/all_to_all | solution.py:1212
  (94 shorter events, 71.8 us)
Async XLA Ops:
  12.4 15.3 %collective-permute-start.4 = (bf16[1536,128]{1,0:T(8,128)(2,1)}, bf16[1536,128]{1,0:T(8,128)(2,1)S(1)}, u32[]{:S(2)}, u32[]{:S(2)}) collective-permute-start(bf16[1536,128]{1,0:T(8,128)(2,1)} %get-tuple-element.152.refs_0_), channel_id=1, source_target_pairs={{0,2},{1,3},{2,0},{3,1},{4,6},{5,7},{6,4},{7,5},{8,10},{9,11},{10,... | collective-permute-start | bytes 1179656 | tf_op jit(solution)/shard_map/ppermute | solution.py:981
  15.3 12.4 %all-to-all-start = ((f32[32,4,128]{2,1,0:T(4,128)}), f32[32,4,128]{2,1,0:T(4,128)S(1)}, u32[]{:S(2)}, u32[]{:S(2)}) async-start(f32[32,4,128]{2,1,0:T(4,128)} %get-tuple-element.143), calls=%async_computation | async-start | bytes 131072 | tf_op jit(solution)/shard_map/all_to_all | solution.py:976
  20.3 12.6 %collective-permute-start.3 = (bf16[1536,128]{1,0:T(8,128)(2,1)}, bf16[1536,128]{1,0:T(8,128)(2,1)}, u32[]{:S(2)}, u32[]{:S(2)}) collective-permute-start(bf16[1536,128]{1,0:T(8,128)(2,1)} %get-tuple-element.152.refs_0_), channel_id=1, source_target_pairs={{0,1},{1,0},{2,3},{3,2},{4,5},{5,4},{6,7},{7,6},{8,9},{9,8},{10,11... | collective-permute-start | bytes 1179656 | tf_op jit(solution)/shard_map/ppermute | solution.py:981
  29.6 10.6 %all-to-all-start.1 = ((f32[32,4,128]{2,1,0:T(4,128)}), f32[32,4,128]{2,1,0:T(4,128)S(1)}, u32[]{:S(2)}, u32[]{:S(2)}) async-start(f32[32,4,128]{2,1,0:T(4,128)} %get-tuple-element.150), calls=%async_computation.1 | async-start | bytes 131072 | tf_op jit(solution)/shard_map/all_to_all | solution.py:976
  40.3 16.7 %collective-permute-start.7 = (bf16[1536,128]{1,0:T(8,128)(2,1)}, bf16[1536,128]{1,0:T(8,128)(2,1)}, u32[]{:S(2)}, u32[]{:S(2)}) collective-permute-start(bf16[1536,128]{1,0:T(8,128)(2,1)} %get-tuple-element.168.refs_0_), channel_id=1, source_target_pairs={{0,2},{1,3},{2,0},{3,1},{4,6},{5,7},{6,4},{7,5},{8,10},{9,11},{10,... | collective-permute-start | bytes 1179656 | tf_op jit(solution)/shard_map/ppermute | solution.py:981
  46.1 10.8 %all-to-all-start.2 = ((f32[32,8,128]{2,1,0:T(8,128)}), f32[32,8,128]{2,1,0:T(8,128)S(1)}, u32[]{:S(2)}, u32[]{:S(2)}) async-start(f32[32,8,128]{2,1,0:T(8,128)} %get-tuple-element.158), calls=%async_computation.2 | async-start | bytes 262144 | tf_op jit(solution)/shard_map/all_to_all | solution.py:976
  48.7 15.3 %collective-permute-start.6 = (bf16[1536,128]{1,0:T(8,128)(2,1)}, bf16[1536,128]{1,0:T(8,128)(2,1)S(1)}, u32[]{:S(2)}, u32[]{:S(2)}) collective-permute-start(bf16[1536,128]{1,0:T(8,128)(2,1)} %get-tuple-element.168.refs_0_), channel_id=1, source_target_pairs={{0,1},{1,0},{2,3},{3,2},{4,5},{5,4},{6,7},{7,6},{8,9},{9,8},{10,11... | collective-permute-start | bytes 1179656 | tf_op jit(solution)/shard_map/ppermute | solution.py:981
  59.5 8.2 %collective-permute-start.9 = (bf16[512,128]{1,0:T(8,128)(2,1)}, bf16[512,128]{1,0:T(8,128)(2,1)S(1)}, u32[]{:S(2)}, u32[]{:S(2)}) collective-permute-start(bf16[512,128]{1,0:T(8,128)(2,1)} %get-tuple-element.171), channel_id=1, source_target_pairs={{0,1},{1,0},{2,3},{3,2},{4,5},{5,4},{6,7},{7,6},{8,9},{9,8},{10,11... | collective-permute-start | bytes 393224 | tf_op jit(solution)/shard_map/ppermute | solution.py:981
  59.8 7.8 %collective-permute-start.10 = (bf16[512,128]{1,0:T(8,128)(2,1)}, bf16[512,128]{1,0:T(8,128)(2,1)S(1)}, u32[]{:S(2)}, u32[]{:S(2)}) collective-permute-start(bf16[512,128]{1,0:T(8,128)(2,1)} %get-tuple-element.172), channel_id=1, source_target_pairs={{0,2},{1,3},{2,0},{3,1},{4,6},{5,7},{6,4},{7,5},{8,10},{9,11},{10,... | collective-permute-start | bytes 393224 | tf_op jit(solution)/shard_map/ppermute | solution.py:981
  60.3 7.5 %collective-permute-start.11 = (bf16[512,128]{1,0:T(8,128)(2,1)S(1)}, bf16[512,128]{1,0:T(8,128)(2,1)S(1)}, u32[]{:S(2)}, u32[]{:S(2)}) collective-permute-start(bf16[512,128]{1,0:T(8,128)(2,1)S(1)} %copy-done.7), channel_id=1, source_target_pairs={{0,3},{1,2},{2,1},{3,0},{4,7},{5,6},{6,5},{7,4},{8,11},{9,10},{10,... | collective-permute-start | bytes 393224 | tf_op jit(solution)/shard_map/ppermute | solution.py:981
  61.4 10.0 %all-to-all-start.3 = ((f32[32,4,128]{2,1,0:T(4,128)}), f32[32,4,128]{2,1,0:T(4,128)S(1)}, u32[]{:S(2)}, u32[]{:S(2)}) async-start(f32[32,4,128]{2,1,0:T(4,128)} %get-tuple-element.166), calls=%async_computation.3 | async-start | bytes 131072 | tf_op jit(solution)/shard_map/all_to_all | solution.py:976
  78.8 11.5 %all-to-all-start.4 = ((f32[32,4,128]{2,1,0:T(4,128)}), f32[32,4,128]{2,1,0:T(4,128)S(1)}, u32[]{:S(2)}, u32[]{:S(2)}) async-start(f32[32,4,128]{2,1,0:T(4,128)} %get-tuple-element.181), calls=%async_computation.4 | async-start | bytes 131072 | tf_op jit(solution)/shard_map/all_to_all | solution.py:976
  93.6 20.1 %collective-permute-start.13 = (bf16[1552,128]{1,0:T(8,128)(2,1)S(1)}, bf16[1552,128]{1,0:T(8,128)(2,1)S(1)}, u32[]{:S(2)}, u32[]{:S(2)}) collective-permute-start(bf16[1552,128]{1,0:T(8,128)(2,1)S(1)} %get-tuple-element.206), channel_id=1, source_target_pairs={{0,2},{1,3},{2,0},{3,1},{4,6},{5,7},{6,4},{7,5},{8,10},{9,11},{10,... | collective-permute-start | bytes 1191944 | tf_op jit(solution)/shard_map/ppermute | solution.py:981
  113.7 10.0 %all-to-all-start.6 = ((f32[32,4,128]{2,1,0:T(4,128)}), f32[32,4,128]{2,1,0:T(4,128)S(1)}, u32[]{:S(2)}, u32[]{:S(2)}) async-start(f32[32,4,128]{2,1,0:T(4,128)} %get-tuple-element.207), calls=%async_computation.6 | async-start | bytes 131072 | tf_op jit(solution)/shard_map/all_to_all | solution.py:976
  124.7 16.6 %all-to-all-start.7 = ((bf16[8,208,128]{2,1,0:T(8,128)(2,1)}), bf16[8,208,128]{2,1,0:T(8,128)(2,1)S(1)}, u32[]{:S(2)}, u32[]{:S(2)}) async-start(bf16[8,208,128]{2,1,0:T(8,128)(2,1)} %shard_map.276), calls=%async_computation.7 | async-start | bytes 851968 | tf_op jit(solution)/shard_map/all_to_all | solution.py:1164
  129.2 17.6 %collective-permute-start.17 = (bf16[2080,128]{1,0:T(8,128)(2,1)}, bf16[2080,128]{1,0:T(8,128)(2,1)S(1)}, u32[]{:S(2)}, u32[]{:S(2)}) collective-permute-start(bf16[2080,128]{1,0:T(8,128)(2,1)} %get-tuple-element.233), channel_id=1, source_target_pairs={{0,2},{1,3},{2,0},{3,1},{4,6},{5,7},{6,4},{7,5},{8,10},{9,11},{10,... | collective-permute-start | bytes 1597448 | tf_op jit(solution)/shard_map/ppermute | solution.py:981
  137.4 9.3 %collective-permute-start.16 = (bf16[528,128]{1,0:T(8,128)(2,1)S(1)}, bf16[528,128]{1,0:T(8,128)(2,1)S(1)}, u32[]{:S(2)}, u32[]{:S(2)}) collective-permute-start(bf16[528,128]{1,0:T(8,128)(2,1)S(1)} %get-tuple-element.232), channel_id=1, source_target_pairs={{0,2},{1,3},{2,0},{3,1},{4,6},{5,7},{6,4},{7,5},{8,10},{9,11},{10,... | collective-permute-start | bytes 405512 | tf_op jit(solution)/shard_map/ppermute | solution.py:981
  147.8 23.8 %all-to-all-start.8 = ((bf16[8,352,128]{2,1,0:T(8,128)(2,1)}), bf16[8,352,128]{2,1,0:T(8,128)(2,1)S(1)}, u32[]{:S(2)}, u32[]{:S(2)}) async-start(bf16[8,352,128]{2,1,0:T(8,128)(2,1)} %shard_map.274), calls=%async_computation.8 | async-start | bytes 1441792 | tf_op jit(solution)/shard_map/all_to_all | solution.py:1191
  155.4 17.3 %collective-permute-start.21 = (bf16[512,128]{1,0:T(8,128)(2,1)S(1)}, bf16[512,128]{1,0:T(8,128)(2,1)S(1)}, u32[]{:S(2)}, u32[]{:S(2)}) collective-permute-start(bf16[512,128]{1,0:T(8,128)(2,1)S(1)} %get-tuple-element.243), channel_id=1, source_target_pairs={{0,1},{1,0},{2,3},{3,2},{4,5},{5,4},{6,7},{7,6},{8,9},{9,8},{10,11... | collective-permute-start | bytes 393224 | tf_op jit(solution)/shard_map/ppermute | solution.py:981
  155.8 16.9 %collective-permute-start.22 = (bf16[512,128]{1,0:T(8,128)(2,1)S(1)}, bf16[512,128]{1,0:T(8,128)(2,1)S(1)}, u32[]{:S(2)}, u32[]{:S(2)}) collective-permute-start(bf16[512,128]{1,0:T(8,128)(2,1)S(1)} %get-tuple-element.245), channel_id=1, source_target_pairs={{0,2},{1,3},{2,0},{3,1},{4,6},{5,7},{6,4},{7,5},{8,10},{9,11},{10,... | collective-permute-start | bytes 393224 | tf_op jit(solution)/shard_map/ppermute | solution.py:981
  156.6 16.1 %collective-permute-start.23 = (bf16[512,128]{1,0:T(8,128)(2,1)S(1)}, bf16[512,128]{1,0:T(8,128)(2,1)S(1)}, u32[]{:S(2)}, u32[]{:S(2)}) collective-permute-start(bf16[512,128]{1,0:T(8,128)(2,1)S(1)} %get-tuple-element.247), channel_id=1, source_target_pairs={{0,3},{1,2},{2,1},{3,0},{4,7},{5,6},{6,5},{7,4},{8,11},{9,10},{10,... | collective-permute-start | bytes 393224 | tf_op jit(solution)/shard_map/ppermute | solution.py:981
  186.7 24.5 %all-to-all-start.10 = ((bf16[8,416,128]{2,1,0:T(8,128)(2,1)}), bf16[8,416,128]{2,1,0:T(8,128)(2,1)S(1)}, u32[]{:S(2)}, u32[]{:S(2)}) async-start(bf16[8,416,128]{2,1,0:T(8,128)(2,1)} %get-tuple-element.255), calls=%async_computation.10 | async-start | bytes 1703936 | tf_op jit(solution)/shard_map/all_to_all | solution.py:1212
  190.2 7.7 %collective-permute-start.25 = (bf16[8,144,128]{2,1,0:T(8,128)(2,1)S(1)}, bf16[8,144,128]{2,1,0:T(8,128)(2,1)S(1)}, u32[]{:S(2)}, u32[]{:S(2)}) collective-permute-start(bf16[8,144,128]{2,1,0:T(8,128)(2,1)S(1)} %all_to_all.56.refs_1_.refs_0_.refs_2_), channel_id=1, source_target_pairs={{0,2},{1,3},{2,0},{3,1},{4,6},{5,7},{6,4},{7,5},{8,10},{9,11},{10,... | collective-permute-start | bytes 884744 | tf_op jit(solution)/shard_map/ppermute | solution.py:981
  190.5 9.5 %collective-permute-start.24 = (bf16[8,144,128]{2,1,0:T(8,128)(2,1)S(1)}, bf16[8,144,128]{2,1,0:T(8,128)(2,1)S(1)}, u32[]{:S(2)}, u32[]{:S(2)}) collective-permute-start(bf16[8,144,128]{2,1,0:T(8,128)(2,1)S(1)} %all_to_all.56.refs_1_.refs_0_.refs_2_), channel_id=1, source_target_pairs={{0,1},{1,0},{2,3},{3,2},{4,5},{5,4},{6,7},{7,6},{8,9},{9,8},{10,11... | collective-permute-start | bytes 884744 | tf_op jit(solution)/shard_map/ppermute | solution.py:981
  (20 other events, 97.3 us)
